TPU v7x, 512 devices: a whole 4x8x8 slice. The times are simulated.
512 devices in a mesh: layer: 4 (over x), row: 4 (over y_lo), col: 32 (over z, y_hi, core).
Axes of the slice: x: 4, y: 8 (y_hi: 2, y_lo: 4; y = y_hi * 4 + y_lo), z: 8, core: 2. Of those that a mesh axis runs over, the one named last changes fastest.
Arguments:
- lower_coupling: bfloat16 [4, 4, 2560, 1024], P('layer', None, 'col', 'row'), may hold values from -0.1875 to 0.1875
- upper_inverse: bfloat16 [4, 1024, 1024], P('layer', 'row'), may hold values from -1 to 2, as said below
- upper_coupling: bfloat16 [4, 1024, 10240], P('layer', None, ('row', 'col')), may hold values from -6 to 6
- lower_inverse: bfloat16 [4, 1024, 1024], P('layer'), may hold values from -1 to 1, as said below
- row_pattern: int32 [4, 10240], P('layer'), may hold values 0 or 1
- ancestor_block: bfloat16 [10240, 10240], P(('layer', 'col'), 'row'), may hold values from -6 to 6
Outputs:
- ancestor: bfloat16 [10240, 10240], P(('layer', 'col'), 'row')
Inputs may be any that keep to these rules, and one draw needn't show every extreme that they name: `upper_inverse`: zero below the diagonal; diagonal entries between 0.5 and 2. `lower_inverse`: zero above the diagonal; diagonal entries 1.
All inputs are finite; a program needn't handle non-finite values. No bound on the sum of `row_pattern` on one device may be relied on, other than what follows from the above.
Results may differ from a plain program's by a relative error of at most 0.02.
Values may be sent and summed in bfloat16 or wider, within the bound.
No kernel may reach another device: no remote copies, remote signals or barrier semaphores. Data moves between devices by JAX's collectives and lax.ppermute only.
A program may use at most 64 MiB of HBM per device.

v0:
```python
import jax
import jax.numpy as jnp
from jax import lax
from jax.sharding import PartitionSpec as P


def shards(
    lower_coupling, upper_inverse, upper_coupling, lower_inverse, row_pattern, ancestor_block
):
    groups = lower_coupling.shape[1]
    slab_rows = lower_coupling.shape[2]
    col_count = lax.axis_size("col")
    col_index = lax.axis_index("col")
    row_index = lax.axis_index("row")
    pattern = row_pattern[0]
    block_span = pattern.shape[0] // groups
    row_mask = lax.dynamic_slice_in_dim(
        pattern.reshape(groups, block_span), col_index * slab_rows, slab_rows, 1
    )
    row_mask = row_mask.reshape(groups * slab_rows, 1).astype(jnp.float32)
    col_mask = lax.dynamic_slice_in_dim(
        pattern, (row_index * col_count + col_index) * slab_rows, slab_rows, 0
    )
    col_mask = col_mask.reshape(1, slab_rows).astype(jnp.float32)
    coupling = lower_coupling[0].reshape(groups * slab_rows, lower_coupling.shape[3])
    partial_value = jnp.dot(coupling, upper_inverse[0], preferred_element_type=jnp.float32)
    lower_full = lax.psum(partial_value.astype(jnp.bfloat16), "row").astype(jnp.float32)
    lower_panel = (lower_full * row_mask).astype(jnp.bfloat16)
    upper_full = jnp.dot(lower_inverse[0], upper_coupling[0], preferred_element_type=jnp.float32)
    upper_panel = (upper_full * col_mask).astype(jnp.bfloat16)
    contribution = jnp.dot(
        lower_panel,
        lax.all_gather(upper_panel, "col", axis=1, tiled=True),
        preferred_element_type=jnp.float32,
    )
    summed = lax.psum_scatter(
        contribution.reshape(groups, slab_rows, block_span).astype(jnp.bfloat16),
        "layer",
        scatter_dimension=0,
        tiled=True,
    ).astype(jnp.float32)[0]
    return (ancestor_block.astype(jnp.float32) - summed).astype(jnp.bfloat16)


def solution(mesh):
    placed = (
        P("layer", None, "col", "row"),
        P("layer", "row", None),
        P("layer", None, ("row", "col")),
        P("layer", None, None),
        P("layer", None),
        P(("layer", "col"), "row"),
    )
    return jax.shard_map(
        shards, mesh=mesh, in_specs=placed, out_specs=P(("layer", "col"), "row"), check_vma=False
    )
```

profile of v0, /device:TPU:1, one launch (start us, length us, event | category | flops | bytes accessed | tf_op | source)
XLA Modules:
  0.0 174.5 jit_solution(5305869252796697274)
XLA Ops:
  7.4 0.0 copy-start
  7.4 0.0 copy-start.2
  7.4 0.0 all-reduce.2.cloned.1.call-start
  7.4 0.0 copy-start.3
  7.4 2.5 %convolution_convert_fusion.1 = bf16[320,1024]{1,0:T(8,128)(2,1)} fusion(bf16[320,256]{1,0:T(8,128)(2,1)} %bitcast.23, bf16[1,256,1024]{2,1,0:T(8,128)(2,1)} %param.7), kind=kOutput, calls=%fused_computation.3 | convolution fusion | flops 168099840 | bytes 1343488 | tf_op jit(solution)/shard_map/dot_general | solution.py:26
  9.9 0.0 all-reduce.2.cloned.1.call-update
  9.9 0.0 all-gather.2.cloned.1.call-start
  10.0 0.8 convert_bitcast_fusion
  10.7 0.0 copy-done
  10.7 0.0 copy-done.2
  10.7 1.4 fusion.5
  12.2 0.0 all-gather.2.cloned.1.call-update
  12.2 0.0 reduce-scatter.2.cloned.1.call-start
  12.2 0.5 broadcast.3
  12.8 0.0 copy-done.3
  12.8 0.7 reduce.3
  13.5 0.1 dynamic-slice_convert_fusion
  13.5 0.1 convert_element_type.45
  13.6 0.0 copy-start.1
  13.6 64.9 %all-reduce.2.cloned.1.call-done = bf16[320,1024]{1,0:T(8,128)(2,1)} async-done(((bf16[320,1024]{1,0:T(8,128)(2,1)}), bf16[320,1024]{1,0:T(8,128)(2,1)}) %all-reduce.2.cloned.1.call-update) | async-done | bytes 655376 | tf_op jit(solution)/shard_map/psum | solution.py:27
  78.5 48.0 %all-gather.2.cloned.1.call-done = bf16[1024,2560]{0,1:T(8,128)(2,1)} async-done(((bf16[1024,80]{0,1:T(8,128)(2,1)}), bf16[1024,2560]{0,1:T(8,128)(2,1)}) %all-gather.2.cloned.1.call-update) | async-done | bytes 5242896 | tf_op jit(solution)/shard_map/all_gather | solution.py:33
  126.5 5.9 %convolution_convert_fusion = bf16[320,2560]{1,0:T(8,128)(2,1)} fusion(bf16[1024,2560]{0,1:T(8,128)(2,1)} %all-gather.2.cloned.1.call-done, bf16[320,1024]{1,0:T(8,128)(2,1)} %all-reduce.2.cloned.1.call-done, f32[320]{0:T(512)S(1)} %convert_element_type.45), kind=kOutput, calls=%fused_computation | convolution fusion | flops 1679523840 | bytes 7537920 | tf_op jit(solution)/shard_map/dot_general | solution.py:31
  132.4 0.0 reduce-scatter.2.cloned.1.call-update
  132.4 32.8 %reduce-scatter.2.cloned.1.call-done = bf16[1,80,2560]{2,1,0:T(8,128)(2,1)} async-done(((bf16[4,80,2560]{2,1,0:T(8,128)(2,1)}), bf16[1,80,2560]{2,1,0:T(8,128)(2,1)}) %reduce-scatter.2.cloned.1.call-update) | async-done | bytes 409616 | tf_op jit(solution)/shard_map/reduce_scatter | solution.py:36
  165.2 0.0 copy-done.1
  165.2 1.9 %fusion.8 = bf16[80,2560]{1,0:T(8,128)(2,1)} fusion(bf16[80,2560]{1,0:T(8,128)(2,1)S(1)} %copy-done.1, bf16[1,80,2560]{2,1,0:T(8,128)(2,1)} %reduce-scatter.2.cloned.1.call-done), kind=kLoop, calls=%fused_computation.8 | loop fusion | flops 819200 | bytes 1228800 | tf_op jit(solution)/shard_map/convert_element_type | solution.py:42
  (1 shorter events, 0.0 us)
Async XLA Ops:
  7.4 3.4 %copy-start = (bf16[1,1024,1024]{2,1,0:T(8,128)(2,1)S(1)}, bf16[1,1024,1024]{2,1,0:T(8,128)(2,1)}, u32[]{:S(2)}) copy-start(bf16[1,1024,1024]{2,1,0:T(8,128)(2,1)} %param.9) | copy-start | bytes 6291460
  7.4 3.4 %copy-start.2 = (bf16[1,1024,80]{1,2,0:T(8,128)(2,1)S(1)}, bf16[1,1024,80]{1,2,0:T(8,128)(2,1)}, u32[]{:S(2)}) copy-start(bf16[1,1024,80]{1,2,0:T(8,128)(2,1)} %param.8) | copy-start | bytes 491524
  7.4 71.1 %all-reduce.2.cloned.1.call-start = ((), (), s32[]{:S(2)}) async-start(), calls=%async_computation.1 | async-start | bytes 1310720 | tf_op jit(solution)/shard_map/psum | solution.py:27
  7.4 5.4 %copy-start.3 = (s32[1,10240]{1,0:T(1,128)S(1)}, s32[1,10240]{1,0:T(1,128)}, u32[]{:S(2)}) copy-start(s32[1,10240]{1,0:T(1,128)} %param.10) | copy-start | bytes 122884
  9.9 116.6 %all-gather.2.cloned.1.call-start = ((), (), s32[]{:S(2)}) async-start(), calls=%async_computation.2 | async-start | bytes 5406720 | tf_op jit(solution)/shard_map/all_gather | solution.py:33
  12.2 153.0 %reduce-scatter.2.cloned.1.call-start = ((), (), s32[]{:S(2)}) async-start(), calls=%async_computation.3 | async-start | bytes 2048000 | tf_op jit(solution)/shard_map/reduce_scatter | solution.py:36
  13.6 151.6 %copy-start.1 = (bf16[80,2560]{1,0:T(8,128)(2,1)S(1)}, bf16[80,2560]{1,0:T(8,128)(2,1)}, u32[]{:S(2)}) copy-start(bf16[80,2560]{1,0:T(8,128)(2,1)} %param.11) | copy-start | bytes 1228804
Sparse Core Ops, SparseCore 0:
  11.1 67.3 all-reduce.1
  132.5 32.5 reduce-scatter.1
Sparse Core Ops, SparseCore 1:
  13.7 112.7 all-gather.1
where the time goes:
time: 175 us
  waiting for transfers between devices  146 us (83%)
  between operations  14.9 us (9%)
  matrix products  9.82 us (6%)
  other arithmetic  3.38 us (2%)
    psum x1, waiting for transfers between devices, shards(): lax.psum(partial_value.astype(jnp.bfloat16), 'row').astype(jnp.float32)  64.9 us
    all_gather x1, waiting for transfers between devices, shards(): lax.all_gather(upper_panel, 'col', axis=1, tiled=True)  48 us
    reduce_scatter x1, waiting for transfers between devices, shards(): lax.psum_scatter(contribution.reshape(groups, slab_rows, block_span).asty...  32.8 us
    dot_general x1, matrix products, shards(): jnp.dot(lower_panel, lax.all_gather(upper_panel, 'col', axis=1, tiled=Tru...  5.89 us
  transfers between devices with their start and end apart: 3, of which 3 were waited for; matrix products, arithmetic and copies ran while one was open for 2% of the time, Pallas kernels for 0%

commit v1 on v0

v1 whole, which is shorter than its diff:
```python
import jax
import jax.numpy as jnp
from jax import lax
from jax.sharding import Mesh
from jax.sharding import PartitionSpec as P

AXES = ("layer", "row", "deep", "half", "core")
RING = ("row", "half")


def ring_pairs(step):
    def place(y):
        return (y % 4) * 2 + (y // 4) % 2

    return [(place(y), place((y + step) % 8)) for y in range(8)]


def dot(a, b, contract):
    return lax.dot_general(a, b, (contract, ((), ())), preferred_element_type=jnp.float32)


def shards(
    lower_coupling, upper_inverse, upper_coupling, lower_inverse, row_pattern, ancestor_block
):
    groups, slab_rows = lower_coupling.shape[1:3]
    row_index = lax.axis_index("row")
    deep_index = lax.axis_index("deep")
    half_index = lax.axis_index("half")
    core_index = lax.axis_index("core")
    col_index = deep_index * 4 + half_index * 2 + core_index
    pattern = row_pattern[0].reshape(groups, -1)
    row_mask = lax.dynamic_slice_in_dim(pattern, col_index * slab_rows, slab_rows, 1)
    row_mask = row_mask.reshape(groups * slab_rows, 1).astype(jnp.float32)

    def col_mask(half):
        start = (row_index * 32 + deep_index * 4 + half * 2 + core_index) * slab_rows
        taken = lax.dynamic_slice_in_dim(row_pattern[0], start, slab_rows, 0)
        return taken.reshape(slab_rows, 1).astype(jnp.float32)

    coupling_t = upper_coupling[0].T
    other_coupling_t = lax.ppermute(coupling_t, "half", [(0, 1), (1, 0)])

    def upper_panel(taken, half):
        solved = dot(taken, lower_inverse[0], ((1,), (1,))) * col_mask(half)
        return lax.all_gather(solved.astype(jnp.bfloat16), ("deep", "core"), axis=0, tiled=True)

    upper_own = upper_panel(coupling_t, half_index)
    upper_other = upper_panel(other_coupling_t, 1 - half_index)

    coupling = lower_coupling[0].reshape(groups * slab_rows, -1)
    couplings = [coupling]
    for step in (1, 2, 3):
        pairs = [((r + step) % 4, r) for r in range(4)]
        couplings.append(lax.ppermute(coupling, "row", pairs))
    depth = upper_inverse.shape[1] // 2
    part = lax.dynamic_slice_in_dim(upper_inverse[0], core_index * depth, depth, 0)
    parts = [lax.ppermute(part, RING, ring_pairs(-step)) for step in (1, 2, -1)]
    parts = jnp.concatenate(parts, axis=0)
    other_parts = lax.ppermute(parts, "core", [(0, 1), (1, 0)])
    first = jnp.where(core_index == 0, parts, other_parts)
    second = jnp.where(core_index == 0, other_parts, parts)
    inverses = [upper_inverse[0]]
    for k in range(3):
        inverses.append(first[k * depth : (k + 1) * depth])
        inverses.append(second[k * depth : (k + 1) * depth])
    lower_panel = dot(
        jnp.concatenate(couplings, axis=1), jnp.concatenate(inverses, axis=0), ((1,), (0,))
    )
    lower_panel = (lower_panel * row_mask).astype(jnp.bfloat16)

    def total(panel):
        contribution = dot(lower_panel, panel, ((1,), (1,))).astype(jnp.bfloat16)
        contribution = contribution.reshape(groups, slab_rows, -1)
        arrived = lax.all_to_all(contribution, "layer", 0, 0, tiled=True)
        return jnp.sum(arrived.astype(jnp.float32), axis=0)

    total_own = total(upper_own)
    total_other = total(upper_other)
    low = jnp.where(half_index == 0, total_own, total_other)
    high = jnp.where(half_index == 0, total_other, total_own)
    width = 2 * slab_rows
    strips = []
    for k in range(8):
        strips.append(low[:, k * width : (k + 1) * width])
        strips.append(high[:, k * width : (k + 1) * width])
    summed = jnp.concatenate(strips, axis=1)
    return (ancestor_block.astype(jnp.float32) - summed).astype(jnp.bfloat16)


def solution(mesh):
    fine = Mesh(mesh.devices.reshape(4, 4, 8, 2, 2), AXES)
    col = ("deep", "half", "core")
    placed = (
        P("layer", None, col, "row"),
        P("layer", "row", None),
        P("layer", None, ("row",) + col),
        P("layer", None, None),
        P("layer", None),
        P(("layer",) + col, "row"),
    )
    return jax.shard_map(
        shards, mesh=fine, in_specs=placed, out_specs=P(("layer",) + col, "row"), check_vma=False
    )
```

time: 175 us -> 138 us (0.79)
  waiting for transfers between devices: 146 us -> 58.2 us
  starting transfers between devices: 0.09 us -> 41.6 us
  matrix products: 9.82 us -> 13.6 us
  local copies, waits for them, and re-layouts: 0.64 us -> 4.39 us
  other arithmetic: 3.38 us -> 5.25 us
    psum x1 -> x0, waiting for transfers between devices: 64.9 us -> none  [shards(): lax.psum(partial_value.astype(jnp.bfloat16), 'row').astype(jnp.float32)]
    ppermute x0 -> x8, starting transfers between devices: none -> 33.9 us  [the longest x3 11.5 us: shards(): parts = [lax.ppermute(part, RING, ring_pairs(-step)) for step in (1, 2, -1)]]
    reduce_scatter x1 -> x0, waiting for transfers between devices: 32.8 us -> none  [shards(): lax.psum_scatter(contribution.reshape(groups, slab_rows, block_span).asty...]
    all_gather x1 -> x2, waiting for transfers between devices: 48 us -> 20.7 us  [upper_panel(): lax.all_gather(solved.astype(jnp.bfloat16), ('deep', 'core'), axis=0, til...]
    ppermute x0 -> x8, waiting for transfers between devices: none -> 25.1 us  [the longest x3 10.3 us: shards(): parts = [lax.ppermute(part, RING, ring_pairs(-step)) for step in (1, 2, -1)]]
    all_to_all x0 -> x2, waiting for transfers between devices: none -> 12.3 us  [total(): arrived = lax.all_to_all(contribution, 'layer', 0, 0, tiled=True)]
    all_to_all x0 -> x2, starting transfers between devices: none -> 7.68 us  [total(): arrived = lax.all_to_all(contribution, 'layer', 0, 0, tiled=True)]
    dot_general x3 -> x5, matrix products: 9.82 us -> 13.6 us  [dot(): lax.dot_general(a, b, (contract, ((), ())), preferred_element_type=jnp.fl...]
  transfers between devices with their start and end apart: 3 -> 12, of which waited for: 3 -> 6; matrix products, arithmetic and copies ran while one was open for 2% -> 10% of each run, Pallas kernels for 0% -> 0%
where the time goes in v1:
time: 138 us; the launch traced here: 137 us
  waiting for transfers between devices  58.2 us (42%)
  starting transfers between devices  41.6 us (30%)
  between operations  13.7 us (10%)
  matrix products  13.6 us (10%)
  other arithmetic  5.25 us (4%)
  local copies, waits for them, and re-layouts  4.39 us (3%)
    all_gather x2, waiting for transfers between devices, upper_panel(): lax.all_gather(solved.astype(jnp.bfloat16), ('deep', 'core'), axis=0, til...  20.7 us
    dot_general x5, matrix products, dot(): lax.dot_general(a, b, (contract, ((), ())), preferred_element_type=jnp.fl...  13.6 us
    all_to_all x2, waiting for transfers between devices, total(): arrived = lax.all_to_all(contribution, 'layer', 0, 0, tiled=True)  12.3 us
    ppermute x3, starting transfers between devices, shards(): parts = [lax.ppermute(part, RING, ring_pairs(-step)) for step in (1, 2, -1)]  11.5 us
    ppermute x3, waiting for transfers between devices, shards(): parts = [lax.ppermute(part, RING, ring_pairs(-step)) for step in (1, 2, -1)]  10.3 us
    ppermute x3, starting transfers between devices, shards(): couplings.append(lax.ppermute(coupling, 'row', pairs))  9.78 us
    ppermute x3, waiting for transfers between devices, shards(): couplings.append(lax.ppermute(coupling, 'row', pairs))  8.45 us
    ppermute x1, starting transfers between devices, shards(): other_coupling_t = lax.ppermute(coupling_t, 'half', [(0, 1), (1, 0)])  8.28 us
  transfers between devices with their start and end apart: 12, of which 6 were waited for; matrix products, arithmetic and copies ran while one was open for 10% of the time, Pallas kernels for 0%

profile of v1, /device:TPU:1, one launch (start us, length us, event | category | flops | bytes accessed | tf_op | source)
XLA Modules:
  0.0 136.8 jit_solution(15743548548208357170)
XLA Ops:
  6.5 0.0 copy-start
  6.5 0.0 copy-start.3
  6.5 0.0 all-gather.3.cloned.1.call-start
  6.5 0.9 fusion.28
  7.5 0.7 copy-done
  8.2 0.0 copy-start.1
  8.2 2.4 %fusion.14 = bf16[80,1024]{1,0:T(8,128)(2,1)} fusion(bf16[1,1024,1024]{2,1,0:T(8,128)(2,1)S(1)} %copy-done, bf16[1,1024,80]{1,2,0:T(8,128)(2,1)} %param.8, f32[80]{0:T(128)S(1)} %get-tuple-element.26), kind=kOutput, calls=%fused_computation.13 | convolution fusion | flops 167936000 | bytes 2425152 | tf_op jit(solution)/shard_map/dot_general | solution.py:19
  10.6 0.0 all-gather.3.cloned.1.call-update
  10.6 0.0 all-gather.5.cloned.1.call-start
  10.6 0.0 copy-done.3
  10.7 8.3 %collective-permute-start.7 = (bf16[80,1024]{1,0:T(8,128)(2,1)S(1)}, bf16[80,1024]{1,0:T(8,128)(2,1)S(1)}, u32[]{:S(2)}, u32[]{:S(2)}) collective-permute-start(bf16[80,1024]{1,0:T(8,128)(2,1)S(1)} %bitcast.37), channel_id=1, source_target_pairs={{0,2},{2,0},{1,3},{3,1},{4,6},{6,4},{5,7},{7,5},{8,10},{10,8},{9,1... | collective-permute-start | bytes 491528 | tf_op jit(solution)/shard_map/ppermute | solution.py:41
  18.9 6.4 %collective-permute-done.7 = bf16[80,1024]{1,0:T(8,128)(2,1)S(1)} collective-permute-done((bf16[80,1024]{1,0:T(8,128)(2,1)S(1)}, bf16[80,1024]{1,0:T(8,128)(2,1)S(1)}, u32[]{:S(2)}, u32[]{:S(2)}) %collective-permute-start.7) | collective-permute-done | bytes 163872 | tf_op jit(solution)/shard_map/ppermute | solution.py:41
  25.4 0.0 copy-start.4
  25.4 1.4 %fusion.11 = bf16[80,1024]{1,0:T(8,128)(2,1)} fusion(bf16[80,1024]{1,0:T(8,128)(2,1)S(1)} %collective-permute-done.7, bf16[1,1024,1024]{2,1,0:T(8,128)(2,1)S(1)} %copy-done, f32[80]{0:T(128)S(1)} %get-tuple-element.25), kind=kOutput, calls=%fused_computation.12 | convolution fusion | flops 167936000 | bytes 2425152 | tf_op jit(solution)/shard_map/dot_general | solution.py:19
  26.8 0.0 all-gather.5.cloned.1.call-update
  26.8 0.0 copy-done.1
  26.9 6.4 %collective-permute-start.3 = (bf16[128,1024]{1,0:T(8,128)(2,1)S(1)}, bf16[128,1024]{1,0:T(8,128)(2,1)S(1)}, u32[]{:S(2)}, u32[]{:S(2)}) collective-permute-start(bf16[128,1024]{1,0:T(8,128)(2,1)S(1)} %dynamic-slice_bitcast_fusion), channel_id=1, source_target_pairs={{0,98},{32,0},{64,32},{96,64},{2,96},{34,2},{66,34},{98,66},{1,99}... | collective-permute-start | bytes 786440 | tf_op jit(solution)/shard_map/ppermute | solution.py:57
  33.3 2.5 %collective-permute-start.4 = (bf16[128,1024]{1,0:T(8,128)(2,1)S(1)}, bf16[128,1024]{1,0:T(8,128)(2,1)S(1)}, u32[]{:S(2)}, u32[]{:S(2)}) collective-permute-start(bf16[128,1024]{1,0:T(8,128)(2,1)S(1)} %dynamic-slice_bitcast_fusion), channel_id=1, source_target_pairs={{0,66},{32,98},{64,0},{96,32},{2,64},{34,96},{66,2},{98,34},{1,67}... | collective-permute-start | bytes 786440 | tf_op jit(solution)/shard_map/ppermute | solution.py:57
  35.8 2.5 %collective-permute-start.5 = (bf16[128,1024]{1,0:T(8,128)(2,1)S(1)}, bf16[128,1024]{1,0:T(8,128)(2,1)S(1)}, u32[]{:S(2)}, u32[]{:S(2)}) collective-permute-start(bf16[128,1024]{1,0:T(8,128)(2,1)S(1)} %dynamic-slice_bitcast_fusion), channel_id=1, source_target_pairs={{0,32},{32,64},{64,96},{96,2},{2,34},{34,66},{66,98},{98,0},{1,33}... | collective-permute-start | bytes 786440 | tf_op jit(solution)/shard_map/ppermute | solution.py:57
  38.3 0.5 collective-permute-done.3
  38.9 9.8 %collective-permute-done.4 = bf16[128,1024]{1,0:T(8,128)(2,1)S(1)} collective-permute-done((bf16[128,1024]{1,0:T(8,128)(2,1)S(1)}, bf16[128,1024]{1,0:T(8,128)(2,1)S(1)}, u32[]{:S(2)}, u32[]{:S(2)}) %collective-permute-start.4) | collective-permute-done | bytes 262176 | tf_op jit(solution)/shard_map/ppermute | solution.py:57
  48.7 0.0 collective-permute-done.5
  48.7 4.4 %collective-permute-start.6 = (bf16[384,1024]{1,0:T(8,128)(2,1)S(1)}, bf16[384,1024]{1,0:T(8,128)(2,1)}, u32[]{:S(2)}, u32[]{:S(2)}) collective-permute-start(bf16[384,1024]{1,0:T(8,128)(2,1)S(1)} %constant_dynamic-update-slice_fusion), channel_id=1, source_target_pairs={{0,1},{1,0},{2,3},{3,2},{4,5},{5,4},{6,7},{7,6},{8,9},{9,8},{10,11... | collective-permute-start | bytes 2359304 | tf_op jit(solution)/shard_map/ppermute | solution.py:59
  53.0 5.7 %collective-permute-start = (bf16[320,256]{1,0:T(8,128)(2,1)}, bf16[320,256]{1,0:T(8,128)(2,1)}, u32[]{:S(2)}, u32[]{:S(2)}) collective-permute-start(bf16[320,256]{1,0:T(8,128)(2,1)} %bitcast.38), channel_id=1, source_target_pairs={{32,0},{64,32},{96,64},{0,96},{33,1},{65,33},{97,65},{1,97},{34,2}... | collective-permute-start | bytes 491528 | tf_op jit(solution)/shard_map/ppermute | solution.py:54
  58.7 1.9 %collective-permute-start.1 = (bf16[320,256]{1,0:T(8,128)(2,1)}, bf16[320,256]{1,0:T(8,128)(2,1)}, u32[]{:S(2)}, u32[]{:S(2)}) collective-permute-start(bf16[320,256]{1,0:T(8,128)(2,1)} %bitcast.39), channel_id=1, source_target_pairs={{64,0},{96,32},{0,64},{32,96},{65,1},{97,33},{1,65},{33,97},{66,2}... | collective-permute-start | bytes 491528 | tf_op jit(solution)/shard_map/ppermute | solution.py:54
  60.6 2.2 %collective-permute-start.2 = (bf16[320,256]{1,0:T(8,128)(2,1)}, bf16[320,256]{1,0:T(8,128)(2,1)}, u32[]{:S(2)}, u32[]{:S(2)}) collective-permute-start(bf16[320,256]{1,0:T(8,128)(2,1)} %bitcast.40), channel_id=1, source_target_pairs={{96,0},{0,32},{32,64},{64,96},{97,1},{1,33},{33,65},{65,97},{98,2}... | collective-permute-start | bytes 491528 | tf_op jit(solution)/shard_map/ppermute | solution.py:54
  62.9 0.5 broadcast.3
  63.4 0.0 copy-done.4
  63.4 0.7 reduce.3
  64.1 0.1 dynamic-slice_convert_fusion
  64.2 0.1 convert_element_type.62
  64.3 0.0 collective-permute-done.6
  64.4 1.2 broadcast_select_fusion
  65.6 0.0 copy-start.5
  65.8 0.0 collective-permute-done
  65.8 8.4 %collective-permute-done.1 = bf16[320,256]{1,0:T(8,128)(2,1)} collective-permute-done((bf16[320,256]{1,0:T(8,128)(2,1)}, bf16[320,256]{1,0:T(8,128)(2,1)}, u32[]{:S(2)}, u32[]{:S(2)}) %collective-permute-start.1) | collective-permute-done | bytes 163872 | tf_op jit(solution)/shard_map/ppermute | solution.py:54
  74.2 0.0 collective-permute-done.2
  74.2 0.0 copy-done.5
  74.2 1.9 %fusion.4 = bf16[320,1024]{1,0:T(8,128)(2,1)S(1)} fusion(bf16[1024,1024]{1,0:T(8,128)(2,1)S(1)} %slice_dynamic-update-slice_fusion, bf16[320,256]{1,0:T(8,128)(2,1)} %collective-permute-done.2, bf16[320,256]{1,0:T(8,128)(2,1)} %collective-permute-done.1, bf16[320,256]{1,0:T(8,128)(2,1)} %collective-permute-done, bf16[320,256]{1,0:T(8,128)(2,1)S(1)} %bitcast.41, ...), kind=kOutput, calls=%fused_computation.9 | convolution fusion | flops 674365440 | bytes 3409152 | tf_op jit(solution)/shard_map/dot_general | solution.py:19
  76.2 0.0 copy-start.6
  76.2 0.0 all-gather.3.cloned.1.call-done
  76.2 3.9 %convolution_convert_fusion.1 = bf16[320,1280]{1,0:T(8,128)(2,1)} fusion(bf16[320,1024]{1,0:T(8,128)(2,1)S(1)} %fusion.4, bf16[1280,1024]{1,0:T(8,128)(2,1)} %all-gather.3.cloned.1.call-done), kind=kOutput, calls=%fused_computation.1 | convolution fusion | flops 839270400 | bytes 4096000 | tf_op jit(solution)/shard_map/dot_general | solution.py:19
  80.2 0.0 copy-done.6
  80.2 3.5 %all-to-all-start = ((bf16[4,80,1280]{2,1,0:T(8,128)(2,1)}), bf16[4,80,1280]{2,1,0:T(8,128)(2,1)S(1)}, u32[]{:S(2)}, u32[]{:S(2)}) async-start(bf16[4,80,1280]{2,1,0:T(8,128)(2,1)} %bitcast.36), calls=%async_computation | async-start | bytes 1638400 | tf_op jit(solution)/shard_map/all_to_all | solution.py:74
  83.7 20.7 %all-gather.5.cloned.1.call-done = bf16[1280,1024]{1,0:T(8,128)(2,1)} async-done(((bf16[80,1024]{1,0:T(8,128)(2,1)}), bf16[1280,1024]{1,0:T(8,128)(2,1)}) %all-gather.5.cloned.1.call-update) | async-done | bytes 2621456 | tf_op jit(solution)/shard_map/all_gather | solution.py:45
  104.4 3.9 %convolution_convert_fusion = bf16[320,1280]{1,0:T(8,128)(2,1)} fusion(bf16[320,1024]{1,0:T(8,128)(2,1)} %copy-done.6, bf16[1280,1024]{1,0:T(8,128)(2,1)} %all-gather.5.cloned.1.call-done), kind=kOutput, calls=%fused_computation | convolution fusion | flops 839270400 | bytes 4096000 | tf_op jit(solution)/shard_map/dot_general | solution.py:19
  108.3 0.0 all-to-all-done
  108.3 4.2 %all-to-all-start.1 = ((bf16[4,80,1280]{2,1,0:T(8,128)(2,1)}), bf16[4,80,1280]{2,1,0:T(8,128)(2,1)}, u32[]{:S(2)}, u32[]{:S(2)}) async-start(bf16[4,80,1280]{2,1,0:T(8,128)(2,1)} %bitcast.35), calls=%async_computation.1 | async-start | bytes 1638400 | tf_op jit(solution)/shard_map/all_to_all | solution.py:74
  112.5 0.1 convert_reduce_fusion.1
  112.6 12.3 %all-to-all-done.1 = bf16[4,80,1280]{2,1,0:T(8,128)(2,1)} async-done(((bf16[4,80,1280]{2,1,0:T(8,128)(2,1)}), bf16[4,80,1280]{2,1,0:T(8,128)(2,1)}, u32[]{:S(2)}, u32[]{:S(2)}) %all-to-all-start.1) | async-done | bytes 819232 | tf_op jit(solution)/shard_map/all_to_all | solution.py:74
  124.9 1.3 convert_reduce_fusion
  126.2 0.1 broadcast_select_fusion.2
  126.3 0.0 copy-start.2
  126.3 1.2 fusion.30
  127.5 1.6 %concatenate.15 = f32[80,2560]{1,0:T(8,128)S(1)} concatenate(f32[80,160]{1,0:T(8,128)} %get-tuple-element.27, f32[80,160]{1,0:T(8,128)} %get-tuple-element.16, f32[80,160]{1,0:T(8,128)} %get-tuple-element.28, f32[80,160]{1,0:T(8,128)} %get-tuple-element.15, f32[80,160]{1,0:T(8,128)} %get-tuple-element.29, f32[80,160]{1,0:T(8,128)} %get-tuple-element.14, ...), dimensions={1} | concatenate | bytes 1638400 | tf_op jit(solution)/shard_map/concatenate | solution.py:86
  129.1 0.0 copy-done.2
  129.1 0.8 subtract_convert_fusion
  (12 shorter events, 0.3 us)
Async XLA Ops:
  6.5 1.6 %copy-start = (bf16[1,1024,1024]{2,1,0:T(8,128)(2,1)S(1)}, bf16[1,1024,1024]{2,1,0:T(8,128)(2,1)}, u32[]{:S(2)}) copy-start(bf16[1,1024,1024]{2,1,0:T(8,128)(2,1)} %param.9) | copy-start | bytes 6291460
  6.5 4.1 %copy-start.3 = (bf16[1,1024,80]{1,2,0:T(8,128)(2,1)S(1)}, bf16[1,1024,80]{1,2,0:T(8,128)(2,1)}, u32[]{:S(2)}) copy-start(bf16[1,1024,80]{1,2,0:T(8,128)(2,1)} %param.8) | copy-start | bytes 491524
  6.5 69.7 %all-gather.3.cloned.1.call-start = ((), (), s32[]{:S(2)}) async-start(), calls=%async_computation.2 | async-start | bytes 2785280 | tf_op jit(solution)/shard_map/all_gather | solution.py:45
  8.2 18.7 %copy-start.1 = (bf16[1,256,1024]{2,1,0:T(8,128)(2,1)S(1)}, bf16[1,256,1024]{2,1,0:T(8,128)(2,1)}, u32[]{:S(2)}) copy-start(bf16[1,256,1024]{2,1,0:T(8,128)(2,1)} %param.7) | copy-start | bytes 1572868
  10.6 93.8 %all-gather.5.cloned.1.call-start = ((), (), s32[]{:S(2)}) async-start(), calls=%async_computation.3 | async-start | bytes 2785280 | tf_op jit(solution)/shard_map/all_gather | solution.py:45
  10.7 14.7 %collective-permute-start.7 = (bf16[80,1024]{1,0:T(8,128)(2,1)S(1)}, bf16[80,1024]{1,0:T(8,128)(2,1)S(1)}, u32[]{:S(2)}, u32[]{:S(2)}) collective-permute-start(bf16[80,1024]{1,0:T(8,128)(2,1)S(1)} %bitcast.37), channel_id=1, source_target_pairs={{0,2},{2,0},{1,3},{3,1},{4,6},{6,4},{5,7},{7,5},{8,10},{10,8},{9,1... | collective-permute-start | bytes 491528 | tf_op jit(solution)/shard_map/ppermute | solution.py:41
  25.4 38.0 %copy-start.4 = (s32[1,10240]{1,0:T(1,128)S(1)}, s32[1,10240]{1,0:T(1,128)}, u32[]{:S(2)}) copy-start(s32[1,10240]{1,0:T(1,128)} %param.10) | copy-start | bytes 122884
  26.9 12.0 %collective-permute-start.3 = (bf16[128,1024]{1,0:T(8,128)(2,1)S(1)}, bf16[128,1024]{1,0:T(8,128)(2,1)S(1)}, u32[]{:S(2)}, u32[]{:S(2)}) collective-permute-start(bf16[128,1024]{1,0:T(8,128)(2,1)S(1)} %dynamic-slice_bitcast_fusion), channel_id=1, source_target_pairs={{0,98},{32,0},{64,32},{96,64},{2,96},{34,2},{66,34},{98,66},{1,99}... | collective-permute-start | bytes 786440 | tf_op jit(solution)/shard_map/ppermute | solution.py:57
  33.3 15.3 %collective-permute-start.4 = (bf16[128,1024]{1,0:T(8,128)(2,1)S(1)}, bf16[128,1024]{1,0:T(8,128)(2,1)S(1)}, u32[]{:S(2)}, u32[]{:S(2)}) collective-permute-start(bf16[128,1024]{1,0:T(8,128)(2,1)S(1)} %dynamic-slice_bitcast_fusion), channel_id=1, source_target_pairs={{0,66},{32,98},{64,0},{96,32},{2,64},{34,96},{66,2},{98,34},{1,67}... | collective-permute-start | bytes 786440 | tf_op jit(solution)/shard_map/ppermute | solution.py:57
  35.8 12.9 %collective-permute-start.5 = (bf16[128,1024]{1,0:T(8,128)(2,1)S(1)}, bf16[128,1024]{1,0:T(8,128)(2,1)S(1)}, u32[]{:S(2)}, u32[]{:S(2)}) collective-permute-start(bf16[128,1024]{1,0:T(8,128)(2,1)S(1)} %dynamic-slice_bitcast_fusion), channel_id=1, source_target_pairs={{0,32},{32,64},{64,96},{96,2},{2,34},{34,66},{66,98},{98,0},{1,33}... | collective-permute-start | bytes 786440 | tf_op jit(solution)/shard_map/ppermute | solution.py:57
  48.7 15.7 %collective-permute-start.6 = (bf16[384,1024]{1,0:T(8,128)(2,1)S(1)}, bf16[384,1024]{1,0:T(8,128)(2,1)}, u32[]{:S(2)}, u32[]{:S(2)}) collective-permute-start(bf16[384,1024]{1,0:T(8,128)(2,1)S(1)} %constant_dynamic-update-slice_fusion), channel_id=1, source_target_pairs={{0,1},{1,0},{2,3},{3,2},{4,5},{5,4},{6,7},{7,6},{8,9},{9,8},{10,11... | collective-permute-start | bytes 2359304 | tf_op jit(solution)/shard_map/ppermute | solution.py:59
  53.0 12.7 %collective-permute-start = (bf16[320,256]{1,0:T(8,128)(2,1)}, bf16[320,256]{1,0:T(8,128)(2,1)}, u32[]{:S(2)}, u32[]{:S(2)}) collective-permute-start(bf16[320,256]{1,0:T(8,128)(2,1)} %bitcast.38), channel_id=1, source_target_pairs={{32,0},{64,32},{96,64},{0,96},{33,1},{65,33},{97,65},{1,97},{34,2}... | collective-permute-start | bytes 491528 | tf_op jit(solution)/shard_map/ppermute | solution.py:54
  58.7 15.5 %collective-permute-start.1 = (bf16[320,256]{1,0:T(8,128)(2,1)}, bf16[320,256]{1,0:T(8,128)(2,1)}, u32[]{:S(2)}, u32[]{:S(2)}) collective-permute-start(bf16[320,256]{1,0:T(8,128)(2,1)} %bitcast.39), channel_id=1, source_target_pairs={{64,0},{96,32},{0,64},{32,96},{65,1},{97,33},{1,65},{33,97},{66,2}... | collective-permute-start | bytes 491528 | tf_op jit(solution)/shard_map/ppermute | solution.py:54
  60.6 13.6 %collective-permute-start.2 = (bf16[320,256]{1,0:T(8,128)(2,1)}, bf16[320,256]{1,0:T(8,128)(2,1)}, u32[]{:S(2)}, u32[]{:S(2)}) collective-permute-start(bf16[320,256]{1,0:T(8,128)(2,1)} %bitcast.40), channel_id=1, source_target_pairs={{96,0},{0,32},{32,64},{64,96},{97,1},{1,33},{33,65},{65,97},{98,2}... | collective-permute-start | bytes 491528 | tf_op jit(solution)/shard_map/ppermute | solution.py:54
  65.6 8.6 %copy-start.5 = (bf16[1,4,80,256]{3,2,1,0:T(8,128)(2,1)S(1)}, bf16[1,4,80,256]{3,2,1,0:T(8,128)(2,1)}, u32[]{:S(2)}) copy-start(bf16[1,4,80,256]{3,2,1,0:T(8,128)(2,1)} %param.6) | copy-start | bytes 491524
  76.2 4.0 %copy-start.6 = (bf16[320,1024]{1,0:T(8,128)(2,1)}, bf16[320,1024]{1,0:T(8,128)(2,1)S(1)}, u32[]{:S(2)}) copy-start(bf16[320,1024]{1,0:T(8,128)(2,1)S(1)} %fusion.4) | copy-start | bytes 1966084
  80.2 28.1 %all-to-all-start = ((bf16[4,80,1280]{2,1,0:T(8,128)(2,1)}), bf16[4,80,1280]{2,1,0:T(8,128)(2,1)S(1)}, u32[]{:S(2)}, u32[]{:S(2)}) async-start(bf16[4,80,1280]{2,1,0:T(8,128)(2,1)} %bitcast.36), calls=%async_computation | async-start | bytes 1638400 | tf_op jit(solution)/shard_map/all_to_all | solution.py:74
  108.3 16.7 %all-to-all-start.1 = ((bf16[4,80,1280]{2,1,0:T(8,128)(2,1)}), bf16[4,80,1280]{2,1,0:T(8,128)(2,1)}, u32[]{:S(2)}, u32[]{:S(2)}) async-start(bf16[4,80,1280]{2,1,0:T(8,128)(2,1)} %bitcast.35), calls=%async_computation.1 | async-start | bytes 1638400 | tf_op jit(solution)/shard_map/all_to_all | solution.py:74
  126.3 2.8 %copy-start.2 = (bf16[80,2560]{1,0:T(8,128)(2,1)S(1)}, bf16[80,2560]{1,0:T(8,128)(2,1)}, u32[]{:S(2)}) copy-start(bf16[80,2560]{1,0:T(8,128)(2,1)} %param.11) | copy-start | bytes 1228804
Sparse Core Ops, SparseCore 0:
  10.7 49.6 all-gather.2
  62.5 41.8 all-gather.4

commit v2 on v1

v2 whole, which is shorter than its diff:
```python
import jax
import jax.numpy as jnp
from jax import lax
from jax.sharding import Mesh
from jax.sharding import PartitionSpec as P

AXES = ("layer", "row", "deep", "half", "core")
SWAP = [(0, 1), (1, 0)]


def dot(a, b, contract):
    return lax.dot_general(a, b, (contract, ((), ())), preferred_element_type=jnp.float32)


def spread(x, axis):
    copies = jnp.broadcast_to(x[None], (lax.axis_size(axis),) + x.shape)
    return lax.all_to_all(copies, axis, 0, 0, tiled=True)


def shards(
    lower_coupling, upper_inverse, upper_coupling, lower_inverse, row_pattern, ancestor_block
):
    groups, slab_rows = lower_coupling.shape[1:3]
    width = lower_inverse.shape[1]
    row_index = lax.axis_index("row")
    deep_index = lax.axis_index("deep")
    half_index = lax.axis_index("half")
    core_index = lax.axis_index("core")
    col_index = deep_index * 4 + half_index * 2 + core_index

    def mask(start):
        taken = lax.dynamic_slice_in_dim(row_pattern[0], start, slab_rows, 0)
        return taken.reshape(slab_rows, 1).astype(jnp.float32)

    def col_mask(half):
        return mask((row_index * 32 + deep_index * 4 + half * 2 + core_index) * slab_rows)

    def upper_panel(taken, half):
        solved = dot(taken, lower_inverse[0], ((1,), (1,))) * col_mask(half)
        return solved.astype(jnp.bfloat16)

    coupling_t = upper_coupling[0].T
    other_coupling_t = lax.ppermute(coupling_t, "half", SWAP)
    upper_own = lax.all_gather(upper_panel(coupling_t, half_index), "deep", axis=0, tiled=True)
    upper_other = spread(upper_panel(other_coupling_t, 1 - half_index), "deep")
    upper_other = upper_other.reshape(-1, width)

    coupling = lower_coupling[0].reshape(groups * slab_rows, -1)
    partial_value = dot(coupling, upper_inverse[0], ((1,), (0,))).astype(jnp.bfloat16)
    arrived = lax.all_to_all(
        partial_value.reshape(groups, slab_rows, width), "row", 0, 0, tiled=True
    )
    lower_mine = jnp.sum(arrived.astype(jnp.float32), axis=0)
    lower_mine = (lower_mine * mask((row_index * 32 + col_index) * slab_rows)).astype(jnp.bfloat16)
    lower_panel = spread(lower_mine, "row")
    lower_other = lax.ppermute(lower_panel, "core", SWAP)
    first = jnp.where(core_index == 0, lower_panel, lower_other)
    second = jnp.where(core_index == 0, lower_other, lower_panel)
    lower_panel = jnp.stack([first, second], axis=1).reshape(-1, width)

    def total(panel):
        contribution = dot(lower_panel, panel, ((1,), (1,))).astype(jnp.bfloat16)
        contribution = contribution.reshape(groups * 2, slab_rows, -1)
        arrived = lax.all_to_all(contribution, ("layer", "core"), 0, 0, tiled=True)
        arrived = arrived.reshape((groups, 2) + arrived.shape[1:])
        return jnp.sum(arrived.astype(jnp.float32), axis=0)

    total_own = total(upper_own)
    total_other = total(upper_other)
    low = jnp.where(half_index == 0, total_own, total_other)
    high = jnp.where(half_index == 0, total_other, total_own)
    strips = []
    for k in range(8):
        here = slice(k * slab_rows, (k + 1) * slab_rows)
        strips += [low[0, :, here], low[1, :, here], high[0, :, here], high[1, :, here]]
    summed = jnp.concatenate(strips, axis=1)
    return (ancestor_block.astype(jnp.float32) - summed).astype(jnp.bfloat16)


def solution(mesh):
    fine = Mesh(mesh.devices.reshape(4, 4, 8, 2, 2), AXES)
    col = ("deep", "half", "core")
    placed = (
        P("layer", None, col, "row"),
        P("layer", "row", None),
        P("layer", None, ("row",) + col),
        P("layer", None, None),
        P("layer", None),
        P(("layer",) + col, "row"),
    )
    return jax.shard_map(
        shards, mesh=fine, in_specs=placed, out_specs=P(("layer",) + col, "row"), check_vma=False
    )
```

time: 138 us -> 163 us (1.18)
  waiting for transfers between devices: 58.2 us -> 83.4 us
  starting transfers between devices: 41.6 us -> 44.3 us
  other arithmetic: 5.25 us -> 3.54 us
  matrix products: 13.6 us -> 11.9 us
    all_to_all x2 -> x5, waiting for transfers between devices: 12.3 us -> 65.3 us  [the longest x2 32.7 us: spread(): return lax.all_to_all(copies, axis, 0, 0, tiled=True)]
    all_to_all x2 -> x5, starting transfers between devices: 7.68 us -> 32.1 us  [the longest x2 16.4 us: spread(): return lax.all_to_all(copies, axis, 0, 0, tiled=True)]
    ppermute x8 -> x2, starting transfers between devices: 33.9 us -> 12.2 us  [the longest x1 8.56 us: shards(): other_coupling_t = lax.ppermute(coupling_t, 'half', SWAP)]
    all_gather x2 -> x1, waiting for transfers between devices: 20.7 us -> 0.95 us  [shards(): lax.all_gather(upper_panel(coupling_t, half_index), 'deep', axis=0, tiled...]
    ppermute x8 -> x2, waiting for transfers between devices: 25.1 us -> 17.1 us  [the longest x1 15.4 us: shards(): other_coupling_t = lax.ppermute(coupling_t, 'half', SWAP)]
    broadcast_in_dim x0 -> x2, local copies, waits for them, and re-layouts: none -> 2.14 us  [spread(): copies = jnp.broadcast_to(x[None], (lax.axis_size(axis),) + x.shape)]
    squeeze x0 -> x2, local copies, waits for them, and re-layouts: none -> 1.95 us  [the longest x1 1 us: shards(): low[1, :, here]]
    dot_general x5, matrix products: 13.6 us -> 11.9 us  [dot(): lax.dot_general(a, b, (contract, ((), ())), preferred_element_type=jnp.fl...]
  transfers between devices with their start and end apart: 12 -> 8, of which waited for: 6 -> 7; matrix products, arithmetic and copies ran while one was open for 10% -> 7% of each run, Pallas kernels for 0% -> 0%
where the time goes in v2:
time: 163 us; the launch traced here: 162 us
  waiting for transfers between devices  83.4 us (51%)
  starting transfers between devices  44.3 us (27%)
  between operations  13.5 us (8%)
  matrix products  11.9 us (7%)
  local copies, waits for them, and re-layouts  5.76 us (4%)
  other arithmetic  3.54 us (2%)
    all_to_all x2, waiting for transfers between devices, spread(): return lax.all_to_all(copies, axis, 0, 0, tiled=True)  32.7 us
    all_to_all x2, waiting for transfers between devices, total(): arrived = lax.all_to_all(contribution, ('layer', 'core'), 0, 0, tiled=True)  20.5 us
    all_to_all x2, starting transfers between devices, spread(): return lax.all_to_all(copies, axis, 0, 0, tiled=True)  16.4 us
    ppermute x1, waiting for transfers between devices, shards(): other_coupling_t = lax.ppermute(coupling_t, 'half', SWAP)  15.4 us
    all_to_all x1, waiting for transfers between devices, shards(): lax.all_to_all(partial_value.reshape(groups, slab_rows, width), 'row', 0,...  12.1 us
    dot_general x5, matrix products, dot(): lax.dot_general(a, b, (contract, ((), ())), preferred_element_type=jnp.fl...  11.9 us
    all_to_all x2, starting transfers between devices, total(): arrived = lax.all_to_all(contribution, ('layer', 'core'), 0, 0, tiled=True)  10.3 us
    ppermute x1, starting transfers between devices, shards(): other_coupling_t = lax.ppermute(coupling_t, 'half', SWAP)  8.56 us
  transfers between devices with their start and end apart: 8, of which 7 were waited for; matrix products, arithmetic and copies ran while one was open for 7% of the time, Pallas kernels for 0%

profile of v2, /device:TPU:1, one launch (start us, length us, event | category | flops | bytes accessed | tf_op | source)
XLA Modules:
  0.0 162.4 jit_solution(18189373859849727345)
XLA Ops:
  6.5 0.0 copy-start
  6.5 2.5 %convolution_convert_fusion.2 = bf16[320,1024]{1,0:T(8,128)(2,1)} fusion(bf16[320,256]{1,0:T(8,128)(2,1)} %bitcast.118, bf16[1,256,1024]{2,1,0:T(8,128)(2,1)} %param.7), kind=kOutput, calls=%fused_computation.8 | convolution fusion | flops 168099840 | bytes 1343488 | tf_op jit(solution)/shard_map/dot_general | solution.py:12
  9.0 5.4 %all-to-all-start = ((bf16[4,80,1024]{2,1,0:T(8,128)(2,1)}), bf16[4,80,1024]{2,1,0:T(8,128)(2,1)S(1)}, u32[]{:S(2)}, u32[]{:S(2)}) async-start(bf16[4,80,1024]{2,1,0:T(8,128)(2,1)} %bitcast.2), calls=%async_computation | async-start | bytes 1310720 | tf_op jit(solution)/shard_map/all_to_all | solution.py:50
  14.4 0.9 fusion.23
  15.3 12.1 %all-to-all-done = bf16[4,80,1024]{2,1,0:T(8,128)(2,1)S(1)} async-done(((bf16[4,80,1024]{2,1,0:T(8,128)(2,1)}), bf16[4,80,1024]{2,1,0:T(8,128)(2,1)S(1)}, u32[]{:S(2)}, u32[]{:S(2)}) %all-to-all-start) | async-done | bytes 655392 | tf_op jit(solution)/shard_map/all_to_all | solution.py:50
  27.4 0.1 convert_reduce_fusion.2
  27.5 0.0 copy-start.3
  27.5 0.1 multiply_convert_fusion
  27.6 0.9 broadcast_in_dim.4
  28.5 5.1 %all-to-all-start.1 = ((bf16[4,80,1024]{2,1,0:T(8,128)(2,1)}), bf16[4,80,1024]{2,1,0:T(8,128)(2,1)S(1)}, u32[]{:S(2)}, u32[]{:S(2)}) async-start(bf16[4,80,1024]{2,1,0:T(8,128)(2,1)} %broadcast_in_dim.4), calls=%async_computation.1 | async-start | bytes 1310720 | tf_op jit(solution)/shard_map/all_to_all | solution.py:17
  33.6 0.0 copy-done.3
  33.6 8.6 %collective-permute-start.1 = (bf16[80,1024]{1,0:T(8,128)(2,1)S(1)}, bf16[80,1024]{1,0:T(8,128)(2,1)S(1)}, u32[]{:S(2)}, u32[]{:S(2)}) collective-permute-start(bf16[80,1024]{1,0:T(8,128)(2,1)S(1)} %bitcast.119), channel_id=1, source_target_pairs={{0,2},{2,0},{1,3},{3,1},{4,6},{6,4},{5,7},{7,5},{8,10},{10,8},{9,1... | collective-permute-start | bytes 491528 | tf_op jit(solution)/shard_map/ppermute | solution.py:43
  42.2 15.4 %collective-permute-done.1 = bf16[80,1024]{1,0:T(8,128)(2,1)S(1)} collective-permute-done((bf16[80,1024]{1,0:T(8,128)(2,1)S(1)}, bf16[80,1024]{1,0:T(8,128)(2,1)S(1)}, u32[]{:S(2)}, u32[]{:S(2)}) %collective-permute-start.1) | collective-permute-done | bytes 163872 | tf_op jit(solution)/shard_map/ppermute | solution.py:43
  57.6 0.0 copy-done
  57.6 0.8 fusion.10
  58.4 0.0 all-to-all-done.1
  58.4 1.2 broadcast_in_dim.5
  59.6 11.2 %all-to-all-start.3 = ((bf16[8,80,1024]{2,1,0:T(8,128)(2,1)}), bf16[8,80,1024]{2,1,0:T(8,128)(2,1)}, u32[]{:S(2)}, u32[]{:S(2)}) async-start(bf16[8,80,1024]{2,1,0:T(8,128)(2,1)} %broadcast_in_dim.5), calls=%async_computation.3 | async-start | bytes 2621440 | tf_op jit(solution)/shard_map/all_to_all | solution.py:17
  70.9 0.0 all-gather.2.cloned.1.call-start
  70.9 1.4 fusion.13
  72.4 0.0 all-gather.2.cloned.1.call-update
  72.4 3.7 %collective-permute-start = (bf16[4,80,1024]{2,1,0:T(8,128)(2,1)S(1)}, bf16[4,80,1024]{2,1,0:T(8,128)(2,1)S(1)}, u32[]{:S(2)}, u32[]{:S(2)}) collective-permute-start(bf16[4,80,1024]{2,1,0:T(8,128)(2,1)S(1)} %all-to-all-done.1), channel_id=1, source_target_pairs={{0,1},{1,0},{2,3},{3,2},{4,5},{5,4},{6,7},{7,6},{8,9},{9,8},{10,11... | collective-permute-start | bytes 1966088 | tf_op jit(solution)/shard_map/ppermute | solution.py:56
  76.0 1.7 %collective-permute-done = bf16[4,80,1024]{2,1,0:T(8,128)(2,1)S(1)} collective-permute-done((bf16[4,80,1024]{2,1,0:T(8,128)(2,1)S(1)}, bf16[4,80,1024]{2,1,0:T(8,128)(2,1)S(1)}, u32[]{:S(2)}, u32[]{:S(2)}) %collective-permute-start) | collective-permute-done | bytes 655392 | tf_op jit(solution)/shard_map/ppermute | solution.py:56
  77.7 0.1 select_bitcast_fusion.1
  77.8 0.1 pad_maximum_fusion
  78.0 0.0 copy-start.1
  78.0 32.6 %all-to-all-done.3 = bf16[8,80,1024]{2,1,0:T(8,128)(2,1)} async-done(((bf16[8,80,1024]{2,1,0:T(8,128)(2,1)}), bf16[8,80,1024]{2,1,0:T(8,128)(2,1)}, u32[]{:S(2)}, u32[]{:S(2)}) %all-to-all-start.3) | async-done | bytes 1310752 | tf_op jit(solution)/shard_map/all_to_all | solution.py:17
  110.6 3.4 %convolution_convert_fusion = bf16[640,640]{1,0:T(8,128)(2,1)} fusion(bf16[640,1024]{1,0:T(8,128)(2,1)S(1)} %bitcast.114, bf16[640,1024]{1,0:T(8,128)(2,1)} %bitcast.15), kind=kOutput, calls=%fused_computation.6 | convolution fusion | flops 839270400 | bytes 3440640 | tf_op jit(solution)/shard_map/dot_general | solution.py:12
  114.1 0.0 copy-done.1
  114.1 5.3 %all-to-all-start.4 = ((bf16[8,80,640]{2,1,0:T(8,128)(2,1)}), bf16[8,80,640]{2,1,0:T(8,128)(2,1)S(1)}, u32[]{:S(2)}, u32[]{:S(2)}) async-start(bf16[8,80,640]{2,1,0:T(8,128)(2,1)} %bitcast.117), calls=%async_computation.4 | async-start | bytes 1638400 | tf_op jit(solution)/shard_map/all_to_all | solution.py:64
  119.4 1.0 all-gather.2.cloned.1.call-done
  120.3 3.8 %convolution_convert_fusion.1 = bf16[640,640]{1,0:T(8,128)(2,1)} fusion(bf16[640,1024]{1,0:T(8,128)(2,1)} %bitcast.115, bf16[640,1024]{1,0:T(8,128)(2,1)} %all-gather.2.cloned.1.call-done), kind=kOutput, calls=%fused_computation.7 | convolution fusion | flops 839270400 | bytes 3440640 | tf_op jit(solution)/shard_map/dot_general | solution.py:12
  124.1 7.9 %all-to-all-done.4 = bf16[8,80,640]{2,1,0:T(8,128)(2,1)S(1)} async-done(((bf16[8,80,640]{2,1,0:T(8,128)(2,1)}), bf16[8,80,640]{2,1,0:T(8,128)(2,1)S(1)}, u32[]{:S(2)}, u32[]{:S(2)}) %all-to-all-start.4) | async-done | bytes 819232 | tf_op jit(solution)/shard_map/all_to_all | solution.py:64
  132.0 5.0 %all-to-all-start.2 = ((bf16[8,80,640]{2,1,0:T(8,128)(2,1)}), bf16[8,80,640]{2,1,0:T(8,128)(2,1)}, u32[]{:S(2)}, u32[]{:S(2)}) async-start(bf16[8,80,640]{2,1,0:T(8,128)(2,1)} %bitcast.116), calls=%async_computation.2 | async-start | bytes 1638400 | tf_op jit(solution)/shard_map/all_to_all | solution.py:64
  137.0 0.1 convert_reduce_fusion
  137.1 12.7 %all-to-all-done.2 = bf16[8,80,640]{2,1,0:T(8,128)(2,1)} async-done(((bf16[8,80,640]{2,1,0:T(8,128)(2,1)}), bf16[8,80,640]{2,1,0:T(8,128)(2,1)}, u32[]{:S(2)}, u32[]{:S(2)}) %all-to-all-start.2) | async-done | bytes 819232 | tf_op jit(solution)/shard_map/all_to_all | solution.py:64
  149.7 1.3 convert_reduce_fusion.1
  151.0 0.1 broadcast_select_fusion
  151.1 1.0 slice_bitcast_fusion
  152.1 1.0 slice_bitcast_fusion.2
  153.1 0.0 copy-start.2
  153.1 1.6 %concatenate.3 = f32[80,2560]{1,0:T(8,128)S(1)} concatenate(f32[80,80]{1,0:T(8,128)} %get-tuple-element.40, f32[80,80]{1,0:T(8,128)} %get-tuple-element.39, f32[80,80]{1,0:T(8,128)} %get-tuple-element.24, f32[80,80]{1,0:T(8,128)} %get-tuple-element.23, f32[80,80]{1,0:T(8,128)} %get-tuple-element.38, f32[80,80]{1,0:T(8,128)} %get-tuple-element.37, f32[80,80]{1,0:T(8,128)} %get-tuple-element.22, ...), dimensions={1} | concatenate | bytes 1638400 | tf_op jit(solution)/shard_map/concatenate | solution.py:76
  154.7 0.0 copy-done.2
  154.7 0.8 subtract_convert_fusion
Async XLA Ops:
  6.5 51.1 %copy-start = (bf16[1,1024,1024]{2,1,0:T(8,128)(2,1)S(1)}, bf16[1,1024,1024]{2,1,0:T(8,128)(2,1)}, u32[]{:S(2)}) copy-start(bf16[1,1024,1024]{2,1,0:T(8,128)(2,1)} %param.9) | copy-start | bytes 6291460
  9.0 18.4 %all-to-all-start = ((bf16[4,80,1024]{2,1,0:T(8,128)(2,1)}), bf16[4,80,1024]{2,1,0:T(8,128)(2,1)S(1)}, u32[]{:S(2)}, u32[]{:S(2)}) async-start(bf16[4,80,1024]{2,1,0:T(8,128)(2,1)} %bitcast.2), calls=%async_computation | async-start | bytes 1310720 | tf_op jit(solution)/shard_map/all_to_all | solution.py:50
  27.5 6.2 %copy-start.3 = (bf16[1,1024,80]{1,2,0:T(8,128)(2,1)S(1)}, bf16[1,1024,80]{1,2,0:T(8,128)(2,1)}, u32[]{:S(2)}) copy-start(bf16[1,1024,80]{1,2,0:T(8,128)(2,1)} %param.8) | copy-start | bytes 491524
  28.5 29.9 %all-to-all-start.1 = ((bf16[4,80,1024]{2,1,0:T(8,128)(2,1)}), bf16[4,80,1024]{2,1,0:T(8,128)(2,1)S(1)}, u32[]{:S(2)}, u32[]{:S(2)}) async-start(bf16[4,80,1024]{2,1,0:T(8,128)(2,1)} %broadcast_in_dim.4), calls=%async_computation.1 | async-start | bytes 1310720 | tf_op jit(solution)/shard_map/all_to_all | solution.py:17
  33.6 24.0 %collective-permute-start.1 = (bf16[80,1024]{1,0:T(8,128)(2,1)S(1)}, bf16[80,1024]{1,0:T(8,128)(2,1)S(1)}, u32[]{:S(2)}, u32[]{:S(2)}) collective-permute-start(bf16[80,1024]{1,0:T(8,128)(2,1)S(1)} %bitcast.119), channel_id=1, source_target_pairs={{0,2},{2,0},{1,3},{3,1},{4,6},{6,4},{5,7},{7,5},{8,10},{10,8},{9,1... | collective-permute-start | bytes 491528 | tf_op jit(solution)/shard_map/ppermute | solution.py:43
  59.6 51.0 %all-to-all-start.3 = ((bf16[8,80,1024]{2,1,0:T(8,128)(2,1)}), bf16[8,80,1024]{2,1,0:T(8,128)(2,1)}, u32[]{:S(2)}, u32[]{:S(2)}) async-start(bf16[8,80,1024]{2,1,0:T(8,128)(2,1)} %broadcast_in_dim.5), calls=%async_computation.3 | async-start | bytes 2621440 | tf_op jit(solution)/shard_map/all_to_all | solution.py:17
  70.9 49.4 %all-gather.2.cloned.1.call-start = ((), (), s32[]{:S(2)}) async-start(), calls=%async_computation.5 | async-start | bytes 1474560 | tf_op jit(solution)/shard_map/all_gather | solution.py:44
  72.4 5.4 %collective-permute-start = (bf16[4,80,1024]{2,1,0:T(8,128)(2,1)S(1)}, bf16[4,80,1024]{2,1,0:T(8,128)(2,1)S(1)}, u32[]{:S(2)}, u32[]{:S(2)}) collective-permute-start(bf16[4,80,1024]{2,1,0:T(8,128)(2,1)S(1)} %all-to-all-done.1), channel_id=1, source_target_pairs={{0,1},{1,0},{2,3},{3,2},{4,5},{5,4},{6,7},{7,6},{8,9},{9,8},{10,11... | collective-permute-start | bytes 1966088 | tf_op jit(solution)/shard_map/ppermute | solution.py:56
  78.0 36.1 %copy-start.1 = (bf16[4,2,80,1024]{3,2,1,0:T(8,128)(2,1)}, bf16[4,2,80,1024]{3,2,1,0:T(8,128)(2,1)S(1)}, u32[]{:S(2)}) copy-start(bf16[4,2,80,1024]{3,2,1,0:T(8,128)(2,1)S(1)} %pad_maximum_fusion) | copy-start | bytes 3932164
  114.1 17.9 %all-to-all-start.4 = ((bf16[8,80,640]{2,1,0:T(8,128)(2,1)}), bf16[8,80,640]{2,1,0:T(8,128)(2,1)S(1)}, u32[]{:S(2)}, u32[]{:S(2)}) async-start(bf16[8,80,640]{2,1,0:T(8,128)(2,1)} %bitcast.117), calls=%async_computation.4 | async-start | bytes 1638400 | tf_op jit(solution)/shard_map/all_to_all | solution.py:64
  132.0 17.7 %all-to-all-start.2 = ((bf16[8,80,640]{2,1,0:T(8,128)(2,1)}), bf16[8,80,640]{2,1,0:T(8,128)(2,1)}, u32[]{:S(2)}, u32[]{:S(2)}) async-start(bf16[8,80,640]{2,1,0:T(8,128)(2,1)} %bitcast.116), calls=%async_computation.2 | async-start | bytes 1638400 | tf_op jit(solution)/shard_map/all_to_all | solution.py:64
  153.1 1.7 %copy-start.2 = (bf16[80,2560]{1,0:T(8,128)(2,1)S(1)}, bf16[80,2560]{1,0:T(8,128)(2,1)}, u32[]{:S(2)}) copy-start(bf16[80,2560]{1,0:T(8,128)(2,1)} %param.11) | copy-start | bytes 1228804
Sparse Core Ops, SparseCore 0:
  73.8 46.4 all-gather.1

commit v3 on v2

v3 whole, which is shorter than its diff:
```python
import jax
import jax.numpy as jnp
from jax import lax
from jax.experimental import pallas as pl
from jax.experimental.pallas import tpu as pltpu
from jax.sharding import Mesh
from jax.sharding import PartitionSpec as P

AXES = ("layer", "row", "deep", "half", "core")
SWAP = [(0, 1), (1, 0)]
STEPS = (2, 1, 3, 0)
PIECES = 4


def turn(size, step):
    return [(i, (i + step) % size) for i in range(size)]


def dot(a, b, contract):
    return lax.dot_general(a, b, (contract, ((), ())), preferred_element_type=jnp.float32)


def spread(x, axis):
    copies = jnp.broadcast_to(x[None], (lax.axis_size(axis),) + x.shape)
    return lax.all_to_all(copies, axis, 0, 0, tiled=True)


def multiply_kernel(place, lower, upper, out2, out1, out3, out0, rows, panel):
    strip = lower.shape[1]

    @pl.when(pl.program_id(0) == 0)
    def _():
        for k, step in enumerate(STEPS):
            rows[k * strip : (k + 1) * strip, :] = lower[place[step]]

    half = place[len(STEPS)]
    for z in range(panel.shape[0] // (4 * strip)):
        for core in range(2):
            start = (4 * z + 2 * core) * strip
            own = upper[start : start + strip, :]
            far = upper[start + strip : start + 2 * strip, :]
            low = (4 * z + core) * strip
            panel[low : low + strip, :] = jnp.where(half == 0, own, far)
            panel[low + 2 * strip : low + 3 * strip, :] = jnp.where(half == 0, far, own)
    value = dot(rows[...], panel[...], ((1,), (1,))).astype(out0.dtype)
    for k, out in enumerate((out2, out1, out3, out0)):
        out[...] = value[k * strip : (k + 1) * strip, :]


def multiply(place, lower, upper):
    strip, width = lower.shape[1:]
    columns = upper.shape[0]
    piece = columns // PIECES
    out = pl.BlockSpec((strip, piece), lambda i: (0, i))
    return pl.pallas_call(
        multiply_kernel,
        grid=(PIECES,),
        out_shape=(jax.ShapeDtypeStruct((strip, columns), jnp.bfloat16),) * len(STEPS),
        in_specs=[
            pl.BlockSpec(memory_space=pltpu.SMEM),
            pl.BlockSpec(lower.shape, lambda i: (0, 0, 0)),
            pl.BlockSpec((piece, width), lambda i: (i, 0)),
        ],
        out_specs=(out,) * len(STEPS),
        scratch_shapes=[
            pltpu.VMEM((len(STEPS) * strip, width), jnp.bfloat16),
            pltpu.VMEM((piece, width), jnp.bfloat16),
        ],
        compiler_params=pltpu.CompilerParams(vmem_limit_bytes=60 << 20),
    )(place, lower, upper)


def shards(
    lower_coupling, upper_inverse, upper_coupling, lower_inverse, row_pattern, ancestor_block
):
    groups, slab_rows = lower_coupling.shape[1:3]
    width = lower_inverse.shape[1]
    layer_index = lax.axis_index("layer")
    row_index = lax.axis_index("row")
    half_index = lax.axis_index("half")
    pair_index = lax.axis_index("deep") * 4 + lax.axis_index("core")

    def mask(start):
        taken = lax.dynamic_slice_in_dim(row_pattern[0], start * slab_rows, slab_rows, 0)
        return taken.reshape(slab_rows, 1).astype(jnp.float32)

    def upper_panel(taken, half):
        solved = dot(taken, lower_inverse[0], ((1,), (1,)))
        solved = solved * mask(row_index * 32 + pair_index + half * 2)
        return solved.astype(jnp.bfloat16)

    coupling_t = upper_coupling[0].T
    other_coupling_t = lax.ppermute(coupling_t, "half", SWAP)
    solved_own = upper_panel(coupling_t, half_index)
    solved_other = upper_panel(other_coupling_t, 1 - half_index)
    solved = jnp.concatenate([solved_own, solved_other], axis=0)
    upper = lax.all_gather(solved, ("deep", "core"), axis=0, tiled=True)

    coupling = lower_coupling[0].reshape(groups * slab_rows, -1)
    partial_value = dot(coupling, upper_inverse[0], ((1,), (0,))).astype(jnp.bfloat16)
    arrived = lax.all_to_all(
        partial_value.reshape(groups, slab_rows, width), "row", 0, 0, tiled=True
    )
    arrived, solved = lax.optimization_barrier((arrived, solved))
    lower_mine = jnp.sum(arrived.astype(jnp.float32), axis=0)
    lower_mine = lower_mine * mask(row_index * 32 + pair_index + half_index * 2)
    lower_panel = spread(lower_mine.astype(jnp.bfloat16), "row")

    targets = (layer_index + jnp.arange(groups)) % groups
    place = jnp.concatenate([targets, half_index[None]]).astype(jnp.int32)
    total = jnp.zeros((), jnp.float32)
    for step, part in zip(STEPS, multiply(place, lower_panel, upper)):
        if step:
            part = lax.ppermute(part, "layer", turn(groups, step))
        total = total + part.astype(jnp.float32)
    return (ancestor_block.astype(jnp.float32) - total).astype(jnp.bfloat16)


def solution(mesh):
    fine = Mesh(mesh.devices.reshape(4, 4, 8, 2, 2), AXES)
    col = ("deep", "half", "core")
    placed = (
        P("layer", None, col, "row"),
        P("layer", "row", None),
        P("layer", None, ("row",) + col),
        P("layer", None, None),
        P("layer", None),
        P(("layer",) + col, "row"),
    )
    return jax.shard_map(
        shards, mesh=fine, in_specs=placed, out_specs=P(("layer",) + col, "row"), check_vma=False
    )
```

time: 163 us -> 116 us (0.71)
  waiting for transfers between devices: 83.4 us -> 45.9 us
  starting transfers between devices: 44.3 us -> 23.1 us
  blocking collectives: 0 us -> 18.5 us
  matrix products: 11.9 us -> 2.78 us
  Pallas kernels: 0 us -> 6.03 us
  local copies, waits for them, and re-layouts: 5.76 us -> 0.98 us
    all_to_all x3 -> x0, waiting for transfers between devices: 32.6 us -> none  [the longest x2 20.5 us: total(): arrived = lax.all_to_all(contribution, ('layer', 'core'), 0, 0, tiled=True)]
    all_to_all x0 -> x1, blocking collectives: none -> 18.5 us  [shards(): lax.all_to_all(partial_value.reshape(groups, slab_rows, width), 'row', 0,...]
    all_to_all x2 -> x1, waiting for transfers between devices: 32.7 us -> 15.8 us  [spread(): return lax.all_to_all(copies, axis, 0, 0, tiled=True)]
    all_to_all x3 -> x0, starting transfers between devices: 15.7 us -> none  [the longest x2 10.3 us: total(): arrived = lax.all_to_all(contribution, ('layer', 'core'), 0, 0, tiled=True)]
    all_to_all x2 -> x1, starting transfers between devices: 16.4 us -> 3.48 us  [spread(): return lax.all_to_all(copies, axis, 0, 0, tiled=True)]
    all_gather x1, waiting for transfers between devices: 0.95 us -> 13.4 us  [shards(): upper = lax.all_gather(solved, ('deep', 'core'), axis=0, tiled=True)]
    ppermute x1, waiting for transfers between devices: 15.4 us -> 4.17 us  [shards(): other_coupling_t = lax.ppermute(coupling_t, 'half', SWAP)]
    ppermute x1 -> x3, waiting for transfers between devices: 1.7 us -> 12.5 us  [shards(): part = lax.ppermute(part, 'layer', turn(groups, step))]
  transfers between devices with their start and end apart: 8 -> 6, of which waited for: 7 -> 5; matrix products, arithmetic and copies ran while one was open for 7% -> 4% of each run, Pallas kernels for 0% -> 0%
where the time goes in v3:
time: 116 us; the launch traced here: 115 us
  waiting for transfers between devices  45.9 us (40%)
  starting transfers between devices  23.1 us (20%)
  blocking collectives  18.5 us (16%)
  between operations  13.5 us (12%)
  Pallas kernels  6.03 us (5%)
  other arithmetic  4.39 us (4%)
  matrix products  2.78 us (2%)
    all_to_all x1, blocking collectives, shards(): lax.all_to_all(partial_value.reshape(groups, slab_rows, width), 'row', 0,...  18.5 us
    all_to_all x1, waiting for transfers between devices, spread(): return lax.all_to_all(copies, axis, 0, 0, tiled=True)  15.8 us
    all_gather x1, waiting for transfers between devices, shards(): upper = lax.all_gather(solved, ('deep', 'core'), axis=0, tiled=True)  13.4 us
    ppermute x3, waiting for transfers between devices, shards(): part = lax.ppermute(part, 'layer', turn(groups, step))  12.5 us
    ppermute x3, starting transfers between devices, shards(): part = lax.ppermute(part, 'layer', turn(groups, step))  11.2 us
    ppermute x1, starting transfers between devices, shards(): other_coupling_t = lax.ppermute(coupling_t, 'half', SWAP)  8.4 us
    pallas_call x1, Pallas kernels, multiply(): pl.pallas_call(multiply_kernel, grid=(PIECES,), out_shape=(jax.ShapeDtype...  6.03 us
    ppermute x1, waiting for transfers between devices, shards(): other_coupling_t = lax.ppermute(coupling_t, 'half', SWAP)  4.17 us
  transfers between devices with their start and end apart: 6, of which 5 were waited for; matrix products, arithmetic and copies ran while one was open for 4% of the time, Pallas kernels for 0%

profile of v3, /device:TPU:1, one launch (start us, length us, event | category | flops | bytes accessed | tf_op | source)
XLA Modules:
  0.0 115.2 jit_solution(4998353682088235561)
XLA Ops:
  6.5 0.0 copy-start
  6.5 0.0 all-gather.2.cloned.1.call-start
  6.5 8.4 %collective-permute-start = (bf16[80,1024]{1,0:T(8,128)(2,1)}, bf16[80,1024]{1,0:T(8,128)(2,1)S(1)}, u32[]{:S(2)}, u32[]{:S(2)}) collective-permute-start(bf16[80,1024]{1,0:T(8,128)(2,1)} %bitcast.31), channel_id=1, source_target_pairs={{0,2},{2,0},{1,3},{3,1},{4,6},{6,4},{5,7},{7,5},{8,10},{10,8},{9,1... | collective-permute-start | bytes 491528 | tf_op jit(solution)/shard_map/ppermute | solution.py:93
  15.0 0.8 convert_bitcast_fusion.1
  15.8 0.0 copy-done
  15.8 1.7 %fusion.13 = bf16[80,1024]{1,0:T(8,128)(2,1)S(1)} fusion(bf16[1,1024,1024]{2,1,0:T(8,128)(2,1)S(1)} %copy-done, bf16[1,1024,80]{1,2,0:T(8,128)(2,1)} %param.8, f32[80]{0:T(128)S(1)} %get-tuple-element.15), kind=kOutput, calls=%fused_computation.9 | convolution fusion | flops 167936000 | bytes 2425152 | tf_op jit(solution)/shard_map/dot_general | solution.py:20
  17.5 0.0 copy-start.2
  17.5 0.0 copy-start.4
  17.5 4.2 %collective-permute-done = bf16[80,1024]{1,0:T(8,128)(2,1)S(1)} collective-permute-done((bf16[80,1024]{1,0:T(8,128)(2,1)}, bf16[80,1024]{1,0:T(8,128)(2,1)S(1)}, u32[]{:S(2)}, u32[]{:S(2)}) %collective-permute-start) | collective-permute-done | bytes 163872 | tf_op jit(solution)/shard_map/ppermute | solution.py:93
  21.7 0.8 fusion.10
  22.4 0.8 pad_maximum_fusion
  23.2 0.0 all-gather.2.cloned.1.call-update
  23.2 0.0 copy-done.2
  23.2 0.0 copy-done.4
  23.2 0.3 convolution_convert_fusion
  23.6 18.5 %all_to_all.10 = bf16[4,80,1024]{2,1,0:T(8,128)(2,1)S(1)} all-to-all(bf16[4,80,1024]{2,1,0:T(8,128)(2,1)S(1)} %bitcast.30), channel_id=1, replica_groups=mesh['layer'=4,'row'=4,'deep'=8,'half'=2,'core'=2] {'row'}, dimensions={0} | all-to-all | bytes 1310720 | tf_op jit(solution)/shard_map/all_to_all | solution.py:101
  42.1 0.1 convert_reduce_fusion
  42.2 0.1 multiply_convert_fusion
  42.3 1.0 broadcast_in_dim.10
  43.3 3.5 %all-to-all-start.1 = ((bf16[4,80,1024]{2,1,0:T(8,128)(2,1)}), bf16[4,80,1024]{2,1,0:T(8,128)(2,1)S(1)}, u32[]{:S(2)}, u32[]{:S(2)}) async-start(bf16[4,80,1024]{2,1,0:T(8,128)(2,1)} %broadcast_in_dim.10), calls=%async_computation.1 | async-start | bytes 1310720 | tf_op jit(solution)/shard_map/all_to_all | solution.py:25
  46.8 0.6 pad_add_fusion.place
  47.4 0.0 copy-start.3
  47.4 15.8 %all-to-all-done.1.lower = bf16[4,80,1024]{2,1,0:T(8,128)(2,1)S(1)} async-done(((bf16[4,80,1024]{2,1,0:T(8,128)(2,1)}), bf16[4,80,1024]{2,1,0:T(8,128)(2,1)S(1)}, u32[]{:S(2)}, u32[]{:S(2)}) %all-to-all-start.1) | async-done | bytes 655392 | tf_op jit(solution)/shard_map/all_to_all | solution.py:25
  63.1 0.0 copy-start.1
  63.1 13.4 %all-gather.2.cloned.1.call-done.upper = bf16[2560,1024]{1,0:T(8,128)(2,1)} async-done(((bf16[160,1024]{1,0:T(8,128)(2,1)}), bf16[2560,1024]{1,0:T(8,128)(2,1)}) %all-gather.2.cloned.1.call-update) | async-done | bytes 5242896 | tf_op jit(solution)/shard_map/all_gather | solution.py:97
  76.6 0.0 copy-done.1
  76.6 6.0 %shard_map.64 = (bf16[80,2560]{1,0:T(8,128)(2,1)}, bf16[80,2560]{1,0:T(8,128)(2,1)}, bf16[80,2560]{1,0:T(8,128)(2,1)}, bf16[80,2560]{1,0:T(8,128)(2,1)}) custom-call(s32[5]{0:T(128)} %pad_add_fusion.place, bf16[4,80,1024]{2,1,0:T(8,128)(2,1)} %copy-done.1, bf16[2560,1024]{1,0:T(8,128)(2,1)} %all-gather.2.cloned.1.call-done.upper), custom_call_target="tpu_custom_call" | custom-call | tf_op jit(solution)/shard_map/pallas_call | solution.py:55
  82.6 4.7 %collective-permute-start.1 = (bf16[80,2560]{1,0:T(8,128)(2,1)}, bf16[80,2560]{1,0:T(8,128)(2,1)S(1)}, u32[]{:S(2)}, u32[]{:S(2)}) collective-permute-start(bf16[80,2560]{1,0:T(8,128)(2,1)} %get-tuple-element.11), channel_id=1, source_target_pairs={{0,256},{128,384},{256,0},{384,128},{1,257},{129,385},{257,1},{385... | collective-permute-start | bytes 1228808 | tf_op jit(solution)/shard_map/ppermute | solution.py:114
  87.3 1.9 %collective-permute-start.2 = (bf16[80,2560]{1,0:T(8,128)(2,1)}, bf16[80,2560]{1,0:T(8,128)(2,1)S(1)}, u32[]{:S(2)}, u32[]{:S(2)}) collective-permute-start(bf16[80,2560]{1,0:T(8,128)(2,1)} %get-tuple-element.12), channel_id=1, source_target_pairs={{0,128},{128,256},{256,384},{384,0},{1,129},{129,257},{257,385},{3... | collective-permute-start | bytes 1228808 | tf_op jit(solution)/shard_map/ppermute | solution.py:114
  89.3 4.5 %collective-permute-start.3 = (bf16[80,2560]{1,0:T(8,128)(2,1)}, bf16[80,2560]{1,0:T(8,128)(2,1)S(1)}, u32[]{:S(2)}, u32[]{:S(2)}) collective-permute-start(bf16[80,2560]{1,0:T(8,128)(2,1)} %get-tuple-element.13), channel_id=1, source_target_pairs={{0,384},{128,0},{256,128},{384,256},{1,385},{129,1},{257,129},{385... | collective-permute-start | bytes 1228808 | tf_op jit(solution)/shard_map/ppermute | solution.py:114
  93.8 3.2 %collective-permute-done.1 = bf16[80,2560]{1,0:T(8,128)(2,1)S(1)} collective-permute-done((bf16[80,2560]{1,0:T(8,128)(2,1)}, bf16[80,2560]{1,0:T(8,128)(2,1)S(1)}, u32[]{:S(2)}, u32[]{:S(2)}) %collective-permute-start.1) | collective-permute-done | bytes 409632 | tf_op jit(solution)/shard_map/ppermute | solution.py:114
  97.1 9.3 %collective-permute-done.2 = bf16[80,2560]{1,0:T(8,128)(2,1)S(1)} collective-permute-done((bf16[80,2560]{1,0:T(8,128)(2,1)}, bf16[80,2560]{1,0:T(8,128)(2,1)S(1)}, u32[]{:S(2)}, u32[]{:S(2)}) %collective-permute-start.2) | collective-permute-done | bytes 409632 | tf_op jit(solution)/shard_map/ppermute | solution.py:114
  106.4 0.0 collective-permute-done.3
  106.4 0.0 copy-done.3
  106.4 2.0 %subtract_convert_fusion = bf16[80,2560]{1,0:T(8,128)(2,1)} fusion(bf16[80,2560]{1,0:T(8,128)(2,1)} %get-tuple-element.14, bf16[80,2560]{1,0:T(8,128)(2,1)S(1)} %collective-permute-done.3, bf16[80,2560]{1,0:T(8,128)(2,1)S(1)} %collective-permute-done.2, bf16[80,2560]{1,0:T(8,128)(2,1)S(1)} %collective-permute-done.1, bf16[80,2560]{1,0:T(8,128)(2,1)S(1)} %copy-done.3), kind=kLoop, calls=%fused_computation.10 | loop fusion | flops 2048000 | bytes 2457600 | tf_op jit(solution)/shard_map/convert_element_type | solution.py:116
  (1 shorter events, 0.0 us)
Async XLA Ops:
  6.5 9.3 %copy-start = (bf16[1,1024,1024]{2,1,0:T(8,128)(2,1)S(1)}, bf16[1,1024,1024]{2,1,0:T(8,128)(2,1)}, u32[]{:S(2)}) copy-start(bf16[1,1024,1024]{2,1,0:T(8,128)(2,1)} %param.9) | copy-start | bytes 6291460
  6.5 70.0 %all-gather.2.cloned.1.call-start = ((), (), s32[]{:S(2)}) async-start(), calls=%async_computation.2 | async-start | bytes 5570560 | tf_op jit(solution)/shard_map/all_gather | solution.py:97
  6.5 15.1 %collective-permute-start = (bf16[80,1024]{1,0:T(8,128)(2,1)}, bf16[80,1024]{1,0:T(8,128)(2,1)S(1)}, u32[]{:S(2)}, u32[]{:S(2)}) collective-permute-start(bf16[80,1024]{1,0:T(8,128)(2,1)} %bitcast.31), channel_id=1, source_target_pairs={{0,2},{2,0},{1,3},{3,1},{4,6},{6,4},{5,7},{7,5},{8,10},{10,8},{9,1... | collective-permute-start | bytes 491528 | tf_op jit(solution)/shard_map/ppermute | solution.py:93
  17.5 5.7 %copy-start.2 = (bf16[1,256,1024]{2,1,0:T(8,128)(2,1)S(1)}, bf16[1,256,1024]{2,1,0:T(8,128)(2,1)}, u32[]{:S(2)}) copy-start(bf16[1,256,1024]{2,1,0:T(8,128)(2,1)} %param.7) | copy-start | bytes 1572868
  17.5 5.7 %copy-start.4 = (bf16[1,4,80,256]{3,2,1,0:T(8,128)(2,1)S(1)}, bf16[1,4,80,256]{3,2,1,0:T(8,128)(2,1)}, u32[]{:S(2)}) copy-start(bf16[1,4,80,256]{3,2,1,0:T(8,128)(2,1)} %param.6) | copy-start | bytes 491524
  43.3 19.9 %all-to-all-start.1 = ((bf16[4,80,1024]{2,1,0:T(8,128)(2,1)}), bf16[4,80,1024]{2,1,0:T(8,128)(2,1)S(1)}, u32[]{:S(2)}, u32[]{:S(2)}) async-start(bf16[4,80,1024]{2,1,0:T(8,128)(2,1)} %broadcast_in_dim.10), calls=%async_computation.1 | async-start | bytes 1310720 | tf_op jit(solution)/shard_map/all_to_all | solution.py:25
  47.4 59.0 %copy-start.3 = (bf16[80,2560]{1,0:T(8,128)(2,1)S(1)}, bf16[80,2560]{1,0:T(8,128)(2,1)}, u32[]{:S(2)}) copy-start(bf16[80,2560]{1,0:T(8,128)(2,1)} %param.11) | copy-start | bytes 1228804
  63.1 13.4 %copy-start.1 = (bf16[4,80,1024]{2,1,0:T(8,128)(2,1)}, bf16[4,80,1024]{2,1,0:T(8,128)(2,1)S(1)}, u32[]{:S(2)}) copy-start(bf16[4,80,1024]{2,1,0:T(8,128)(2,1)S(1)} %all-to-all-done.1.lower) | copy-start | bytes 1966084
  82.6 14.5 %collective-permute-start.1 = (bf16[80,2560]{1,0:T(8,128)(2,1)}, bf16[80,2560]{1,0:T(8,128)(2,1)S(1)}, u32[]{:S(2)}, u32[]{:S(2)}) collective-permute-start(bf16[80,2560]{1,0:T(8,128)(2,1)} %get-tuple-element.11), channel_id=1, source_target_pairs={{0,256},{128,384},{256,0},{384,128},{1,257},{129,385},{257,1},{385... | collective-permute-start | bytes 1228808 | tf_op jit(solution)/shard_map/ppermute | solution.py:114
  87.3 19.0 %collective-permute-start.2 = (bf16[80,2560]{1,0:T(8,128)(2,1)}, bf16[80,2560]{1,0:T(8,128)(2,1)S(1)}, u32[]{:S(2)}, u32[]{:S(2)}) collective-permute-start(bf16[80,2560]{1,0:T(8,128)(2,1)} %get-tuple-element.12), channel_id=1, source_target_pairs={{0,128},{128,256},{256,384},{384,0},{1,129},{129,257},{257,385},{3... | collective-permute-start | bytes 1228808 | tf_op jit(solution)/shard_map/ppermute | solution.py:114
  89.3 17.1 %collective-permute-start.3 = (bf16[80,2560]{1,0:T(8,128)(2,1)}, bf16[80,2560]{1,0:T(8,128)(2,1)S(1)}, u32[]{:S(2)}, u32[]{:S(2)}) collective-permute-start(bf16[80,2560]{1,0:T(8,128)(2,1)} %get-tuple-element.13), channel_id=1, source_target_pairs={{0,384},{128,0},{256,128},{384,256},{1,385},{129,1},{257,129},{385... | collective-permute-start | bytes 1228808 | tf_op jit(solution)/shard_map/ppermute | solution.py:114
Sparse Core Ops, SparseCore 0:
  23.3 53.1 all-gather.1

commit v4 on v3

v4 whole, which is shorter than its diff:
```python
import jax
import jax.numpy as jnp
from jax import lax
from jax.experimental import pallas as pl
from jax.experimental.pallas import tpu as pltpu
from jax.sharding import Mesh
from jax.sharding import PartitionSpec as P

AXES = ("layer", "row", "deep", "half", "core")
SWAP = [(0, 1), (1, 0)]
PIECES = 4
SHARES = 4
MULTIPLY_VMEM = 48 << 20


def layer_pairs(step):
    pairs = []
    for x in range(4):
        pairs.append((x * 2, (x + step) % 4 * 2))
        pairs.append((x * 2 + 1, (x - step) % 4 * 2 + 1))
    return pairs


def dot(a, b, contract):
    return lax.dot_general(a, b, (contract, ((), ())), preferred_element_type=jnp.float32)


def spread(x, axis):
    copies = jnp.broadcast_to(x[None], (lax.axis_size(axis),) + x.shape)
    return lax.all_to_all(copies, axis, 0, 0, tiled=True)


def join_kernel(own, far, out):
    rows = own.shape[0]
    out[:rows, :] = own[...]
    out[rows:, :] = far[...]


def join(own, far):
    rows, width = own.shape
    vmem = pl.BlockSpec(memory_space=pltpu.VMEM)
    return pl.pallas_call(
        join_kernel,
        out_shape=jax.ShapeDtypeStruct((2 * rows, width), own.dtype),
        in_specs=[vmem] * 2,
        out_specs=vmem,
        compiler_params=pltpu.CompilerParams(vmem_limit_bytes=32 << 20),
    )(own, far)


def multiply_kernel(place, mask, lower, *refs):
    uppers, outs, (rows, panel) = refs[:SHARES], refs[SHARES:-2], refs[-2:]
    strip = lower.shape[1]

    @pl.when(pl.program_id(0) == 0)
    def _():
        for k in range(4):
            rows[k * strip : (k + 1) * strip, :] = lower[place[k]]

    half = place[4]
    share = uppers[0].shape[0] // strip
    for n in range(SHARES * share):
        z, core, k = n // 4, n // 2 % 2, n % 2
        to = (4 * z + core) * strip + jnp.where(half == k, 0, 2 * strip)
        block = uppers[n // share][n % share * strip : (n % share + 1) * strip, :]
        panel[pl.ds(pl.multiple_of(to, 16), strip), :] = block
    value = (dot(rows[...], panel[...], ((1,), (1,))) * mask[...]).astype(jnp.bfloat16)
    for k, out in enumerate(outs):
        out[...] = value[k * strip : (k + 1) * strip, :]


def multiply(place, mask, lower, upper):
    groups, strip, width = lower.shape
    columns = upper.shape[0]
    piece = columns // PIECES
    out = pl.BlockSpec((strip, piece), lambda i: (0, i))
    shares = [
        pl.BlockSpec((piece // SHARES, width), lambda i, k=k: (i * SHARES + k, 0))
        for k in range(SHARES)
    ]
    return pl.pallas_call(
        multiply_kernel,
        grid=(PIECES,),
        out_shape=(jax.ShapeDtypeStruct((strip, columns), jnp.bfloat16),) * groups,
        in_specs=[
            pl.BlockSpec(memory_space=pltpu.SMEM),
            pl.BlockSpec((1, piece), lambda i: (0, i)),
            pl.BlockSpec(lower.shape, lambda i: (0, 0, 0)),
        ] + shares,
        out_specs=(out,) * groups,
        scratch_shapes=[
            pltpu.VMEM((groups * strip, width), jnp.bfloat16),
            pltpu.VMEM((piece, width), jnp.bfloat16),
        ],
        compiler_params=pltpu.CompilerParams(vmem_limit_bytes=MULTIPLY_VMEM),
    )(place, mask, lower, *([upper] * SHARES))


def shards(
    lower_coupling, upper_inverse, upper_coupling, lower_inverse, row_pattern, ancestor_block
):
    groups, slab_rows = lower_coupling.shape[1:3]
    width = lower_inverse.shape[1]
    layer_index = lax.axis_index("layer")
    row_index = lax.axis_index("row")
    half_index = lax.axis_index("half")
    deep_index = lax.axis_index("deep")
    core_index = lax.axis_index("core")
    slab = ((row_index * 8 + deep_index) * 2 + half_index) * 2 + core_index

    coupling_t = upper_coupling[0].T
    other = lax.ppermute(coupling_t, "half", SWAP)
    solver = dot(upper_inverse[0], lower_inverse[0], ((1,), (0,))).astype(jnp.bfloat16)
    coupling = lower_coupling[0].reshape(groups * slab_rows, -1)
    partial_value = dot(coupling, solver, ((1,), (0,))).astype(jnp.bfloat16)
    other, partial_value = lax.optimization_barrier((other, partial_value))
    both = join(coupling_t, other)
    upper = lax.all_gather(both, ("deep", "core"), axis=0, tiled=True)
    partial_value, both = lax.optimization_barrier((partial_value, both))
    arrived = lax.all_to_all(
        partial_value.reshape(groups, slab_rows, width), "row", 0, 0, tiled=True
    )
    row_mask = lax.dynamic_slice_in_dim(row_pattern[0], slab * slab_rows, slab_rows, 0)
    row_mask = row_mask.reshape(slab_rows, 1).astype(jnp.float32)
    lower_mine = jnp.sum(arrived.astype(jnp.float32), axis=0) * row_mask
    lower_panel = spread(lower_mine.astype(jnp.bfloat16), "row")
    mask = lax.dynamic_slice_in_dim(
        row_pattern[0], row_index * (groups * 8 * slab_rows), groups * 8 * slab_rows, 0
    )
    mask = mask.reshape(1, -1).astype(jnp.float32)

    onward = jnp.where(core_index == 0, 1, 3)
    targets = (layer_index + jnp.stack([2 * onward, 3 * onward, onward, 0 * onward])) % groups
    place = jnp.concatenate([targets, half_index[None]]).astype(jnp.int32)
    across, back, near, kept = multiply(place, mask, lower_panel, upper)
    across = lax.ppermute(across, ("layer", "core"), layer_pairs(1))
    back = lax.ppermute(back, ("layer", "core"), layer_pairs(-1))
    near = (near.astype(jnp.float32) + across.astype(jnp.float32)).astype(jnp.bfloat16)
    near = lax.ppermute(near, ("layer", "core"), layer_pairs(1))
    total = kept.astype(jnp.float32) + back.astype(jnp.float32) + near.astype(jnp.float32)
    return (ancestor_block.astype(jnp.float32) - total).astype(jnp.bfloat16)


def solution(mesh):
    fine = Mesh(mesh.devices.reshape(4, 4, 8, 2, 2), AXES)
    col = ("deep", "half", "core")
    placed = (
        P("layer", None, col, "row"),
        P("layer", "row", None),
        P("layer", None, ("row",) + col),
        P("layer", None, None),
        P("layer", None),
        P(("layer",) + col, "row"),
    )
    return jax.shard_map(
        shards, mesh=fine, in_specs=placed, out_specs=P(("layer",) + col, "row"), check_vma=False
    )
```

time: 116 us -> 111 us (0.957)
  blocking collectives: 18.5 us -> 0 us
  waiting for transfers between devices: 45.9 us -> 54.6 us
  starting transfers between devices: 23.1 us -> 28.4 us
  other arithmetic: 4.39 us -> 2.87 us
    all_to_all x1 -> x0, blocking collectives: 18.5 us -> none  [shards(): lax.all_to_all(partial_value.reshape(groups, slab_rows, width), 'row', 0,...]
    all_to_all x0 -> x1, waiting for transfers between devices: none -> 12.1 us  [shards(): lax.all_to_all(partial_value.reshape(groups, slab_rows, width), 'row', 0,...]
    ppermute x4, waiting for transfers between devices: 16.7 us -> 12.7 us  [the longest x1 4.86 us: shards(): near = lax.ppermute(near, ('layer', 'core'), layer_pairs(1))]
    all_gather x1, waiting for transfers between devices: 13.4 us -> 17 us  [shards(): upper = lax.all_gather(both, ('deep', 'core'), axis=0, tiled=True)]
    all_to_all x0 -> x1, starting transfers between devices: none -> 3.49 us  [shards(): lax.all_to_all(partial_value.reshape(groups, slab_rows, width), 'row', 0,...]
    all_to_all x1, waiting for transfers between devices: 15.8 us -> 12.8 us  [spread(): return lax.all_to_all(copies, axis, 0, 0, tiled=True)]
    all_to_all x1, starting transfers between devices: 3.48 us -> 5.03 us  [spread(): return lax.all_to_all(copies, axis, 0, 0, tiled=True)]
    dot_general x3 -> x1, matrix products: 2.78 us -> 2.95 us  [dot(): lax.dot_general(a, b, (contract, ((), ())), preferred_element_type=jnp.fl...]
  transfers between devices with their start and end apart: 6 -> 7, of which waited for: 5 -> 6; matrix products, arithmetic and copies ran while one was open for 4% -> 5% of each run, Pallas kernels for 0% -> 0%
where the time goes in v4:
time: 111 us; the launch traced here: 109 us
  waiting for transfers between devices  54.6 us (49%)
  starting transfers between devices  28.4 us (26%)
  between operations  13.5 us (12%)
  Pallas kernels  5.98 us (5%)
  matrix products  2.95 us (3%)
  other arithmetic  2.87 us (3%)
    all_gather x1, waiting for transfers between devices, shards(): upper = lax.all_gather(both, ('deep', 'core'), axis=0, tiled=True)  17 us
    all_to_all x1, waiting for transfers between devices, spread(): return lax.all_to_all(copies, axis, 0, 0, tiled=True)  12.8 us
    all_to_all x1, waiting for transfers between devices, shards(): lax.all_to_all(partial_value.reshape(groups, slab_rows, width), 'row', 0,...  12.1 us
    ppermute x1, starting transfers between devices, shards(): other = lax.ppermute(coupling_t, 'half', SWAP)  8.4 us
    ppermute x1, starting transfers between devices, shards(): near = lax.ppermute(near, ('layer', 'core'), layer_pairs(1))  5.32 us
    pallas_call x1, Pallas kernels, multiply(): pl.pallas_call(multiply_kernel, grid=(PIECES,), out_shape=(jax.ShapeDtype...  5.23 us
    all_to_all x1, starting transfers between devices, spread(): return lax.all_to_all(copies, axis, 0, 0, tiled=True)  5.03 us
    ppermute x1, waiting for transfers between devices, shards(): near = lax.ppermute(near, ('layer', 'core'), layer_pairs(1))  4.86 us
  transfers between devices with their start and end apart: 7, of which 6 were waited for; matrix products, arithmetic and copies ran while one was open for 5% of the time, Pallas kernels for 0%

profile of v4, /device:TPU:1, one launch (start us, length us, event | category | flops | bytes accessed | tf_op | source)
XLA Modules:
  0.0 109.3 jit_solution(17903206952313914773)
XLA Ops:
  6.5 0.0 copy-start
  6.5 0.0 copy-start.1
  6.5 0.0 all-gather.2.cloned.1.call-start
  6.5 8.4 %collective-permute-start = (bf16[80,1024]{1,0:T(8,128)(2,1)}, bf16[80,1024]{1,0:T(8,128)(2,1)S(1)}, u32[]{:S(2)}, u32[]{:S(2)}) collective-permute-start(bf16[80,1024]{1,0:T(8,128)(2,1)} %bitcast.25), channel_id=1, source_target_pairs={{0,2},{2,0},{1,3},{3,1},{4,6},{6,4},{5,7},{7,5},{8,10},{10,8},{9,1... | collective-permute-start | bytes 491528 | tf_op jit(solution)/shard_map/ppermute | solution.py:112
  15.0 0.0 copy-done
  15.0 2.9 %fusion.5 = bf16[320,1024]{1,0:T(8,128)(2,1)} fusion(bf16[320,256]{1,0:T(8,128)(2,1)} %bitcast.27, bf16[1,1024,1024]{2,1,0:T(8,128)(2,1)S(1)} %copy-done, bf16[1,256,1024]{2,1,0:T(8,128)(2,1)} %param.7), kind=kOutput, calls=%fused_computation.5 | convolution fusion | flops 705232896 | bytes 3440640 | tf_op jit(solution)/shard_map/dot_general | solution.py:25
  17.9 3.8 %collective-permute-done.far = bf16[80,1024]{1,0:T(8,128)(2,1)S(1)} collective-permute-done((bf16[80,1024]{1,0:T(8,128)(2,1)}, bf16[80,1024]{1,0:T(8,128)(2,1)S(1)}, u32[]{:S(2)}, u32[]{:S(2)}) %collective-permute-start) | collective-permute-done | bytes 163872 | tf_op jit(solution)/shard_map/ppermute | solution.py:112
  21.7 0.0 copy-done.1
  21.7 0.7 shard_map.64
  22.4 0.0 all-gather.2.cloned.1.call-update
  22.5 3.5 %all-to-all-start = ((bf16[4,80,1024]{2,1,0:T(8,128)(2,1)}), bf16[4,80,1024]{2,1,0:T(8,128)(2,1)S(1)}, u32[]{:S(2)}, u32[]{:S(2)}) async-start(bf16[4,80,1024]{2,1,0:T(8,128)(2,1)} %bitcast.11), calls=%async_computation | async-start | bytes 1310720 | tf_op jit(solution)/shard_map/all_to_all | solution.py:120
  26.0 0.8 convert_bitcast_fusion
  26.7 12.1 %all-to-all-done = bf16[4,80,1024]{2,1,0:T(8,128)(2,1)S(1)} async-done(((bf16[4,80,1024]{2,1,0:T(8,128)(2,1)}), bf16[4,80,1024]{2,1,0:T(8,128)(2,1)S(1)}, u32[]{:S(2)}, u32[]{:S(2)}) %all-to-all-start) | async-done | bytes 655392 | tf_op jit(solution)/shard_map/all_to_all | solution.py:120
  38.9 0.1 convert_reduce_fusion
  39.0 0.1 multiply_convert_fusion
  39.1 1.0 broadcast_in_dim.10
  40.0 5.0 %all-to-all-start.1 = ((bf16[4,80,1024]{2,1,0:T(8,128)(2,1)}), bf16[4,80,1024]{2,1,0:T(8,128)(2,1)S(1)}, u32[]{:S(2)}, u32[]{:S(2)}) async-start(bf16[4,80,1024]{2,1,0:T(8,128)(2,1)} %broadcast_in_dim.10), calls=%async_computation.1 | async-start | bytes 1310720 | tf_op jit(solution)/shard_map/all_to_all | solution.py:30
  45.0 0.1 and_select_fusion
  45.1 0.1 pad_add_fusion.place
  45.2 0.7 dynamic-slice_convert_fusion.mask
  45.9 0.0 copy-start.2
  45.9 12.8 %all-to-all-done.1.lower = bf16[4,80,1024]{2,1,0:T(8,128)(2,1)S(1)} async-done(((bf16[4,80,1024]{2,1,0:T(8,128)(2,1)}), bf16[4,80,1024]{2,1,0:T(8,128)(2,1)S(1)}, u32[]{:S(2)}, u32[]{:S(2)}) %all-to-all-start.1) | async-done | bytes 655392 | tf_op jit(solution)/shard_map/all_to_all | solution.py:30
  58.7 17.0 %all-gather.2.cloned.1.call-done.refs_0_.refs_1_.refs_2_.refs_3_ = bf16[2560,1024]{1,0:T(8,128)(2,1)} async-done(((bf16[160,1024]{1,0:T(8,128)(2,1)}), bf16[2560,1024]{1,0:T(8,128)(2,1)}) %all-gather.2.cloned.1.call-update) | async-done | bytes 5242896 | tf_op jit(solution)/shard_map/all_gather | solution.py:118
  75.7 5.2 %shard_map.65 = (bf16[80,2560]{1,0:T(8,128)(2,1)S(1)}, bf16[80,2560]{1,0:T(8,128)(2,1)S(1)}, bf16[80,2560]{1,0:T(8,128)(2,1)S(1)}, bf16[80,2560]{1,0:T(8,128)(2,1)S(1)}) custom-call(s32[5]{0:T(128)S(1)} %pad_add_fusion.place, f32[1,2560]{1,0:T(1,128)S(1)} %dynamic-slice_convert_fusion.mask, bf16[4,80,1024]{2,1,0:T(8,128)(2,1)S(1)} %all-to-all-done.1.lower, ...), custom_call_target="tpu_custom_call" | custom-call | tf_op jit(solution)/shard_map/pallas_call | solution.py:81
  81.0 4.3 %collective-permute-start.2 = (bf16[80,2560]{1,0:T(8,128)(2,1)S(1)}, bf16[80,2560]{1,0:T(8,128)(2,1)S(1)}, u32[]{:S(2)}, u32[]{:S(2)}) collective-permute-start(bf16[80,2560]{1,0:T(8,128)(2,1)S(1)} %get-tuple-element.18), channel_id=1, source_target_pairs={{0,128},{1,385},{128,256},{129,1},{256,384},{257,129},{384,0},{385... | collective-permute-start | bytes 1228808 | tf_op jit(solution)/shard_map/ppermute | solution.py:136
  85.2 1.9 %collective-permute-start.1 = (bf16[80,2560]{1,0:T(8,128)(2,1)S(1)}, bf16[80,2560]{1,0:T(8,128)(2,1)S(1)}, u32[]{:S(2)}, u32[]{:S(2)}) collective-permute-start(bf16[80,2560]{1,0:T(8,128)(2,1)S(1)} %get-tuple-element.16), channel_id=1, source_target_pairs={{0,384},{1,129},{128,0},{129,257},{256,128},{257,385},{384,256},{3... | collective-permute-start | bytes 1228808 | tf_op jit(solution)/shard_map/ppermute | solution.py:137
  87.2 4.0 %collective-permute-done.2 = bf16[80,2560]{1,0:T(8,128)(2,1)S(1)} collective-permute-done((bf16[80,2560]{1,0:T(8,128)(2,1)S(1)}, bf16[80,2560]{1,0:T(8,128)(2,1)S(1)}, u32[]{:S(2)}, u32[]{:S(2)}) %collective-permute-start.2) | collective-permute-done | bytes 409632 | tf_op jit(solution)/shard_map/ppermute | solution.py:136
  91.2 0.1 add_convert_fusion
  91.3 5.3 %collective-permute-start.3 = (bf16[80,2560]{1,0:T(8,128)(2,1)S(1)}, bf16[80,2560]{1,0:T(8,128)(2,1)S(1)}, u32[]{:S(2)}, u32[]{:S(2)}) collective-permute-start(bf16[80,2560]{1,0:T(8,128)(2,1)S(1)} %add_convert_fusion), channel_id=1, source_target_pairs={{0,128},{1,385},{128,256},{129,1},{256,384},{257,129},{384,0},{385... | collective-permute-start | bytes 1228808 | tf_op jit(solution)/shard_map/ppermute | solution.py:139
  96.6 0.0 collective-permute-done.1
  96.7 4.9 %collective-permute-done.3 = bf16[80,2560]{1,0:T(8,128)(2,1)S(1)} collective-permute-done((bf16[80,2560]{1,0:T(8,128)(2,1)S(1)}, bf16[80,2560]{1,0:T(8,128)(2,1)S(1)}, u32[]{:S(2)}, u32[]{:S(2)}) %collective-permute-start.3) | collective-permute-done | bytes 409632 | tf_op jit(solution)/shard_map/ppermute | solution.py:139
  101.5 0.0 copy-done.2
  101.5 1.0 subtract_convert_fusion
Async XLA Ops:
  6.5 8.4 %copy-start = (bf16[1,1024,1024]{2,1,0:T(8,128)(2,1)S(1)}, bf16[1,1024,1024]{2,1,0:T(8,128)(2,1)}, u32[]{:S(2)}) copy-start(bf16[1,1024,1024]{2,1,0:T(8,128)(2,1)} %param.9) | copy-start | bytes 6291460
  6.5 15.1 %copy-start.1 = (bf16[1,1024,80]{1,2,0:T(8,128)(2,1)S(1)}, bf16[1,1024,80]{1,2,0:T(8,128)(2,1)}, u32[]{:S(2)}) copy-start(bf16[1,1024,80]{1,2,0:T(8,128)(2,1)} %param.8) | copy-start | bytes 491524
  6.5 69.2 %all-gather.2.cloned.1.call-start = ((), (), s32[]{:S(2)}) async-start(), calls=%async_computation.2 | async-start | bytes 5570560 | tf_op jit(solution)/shard_map/all_gather | solution.py:118
  6.5 15.1 %collective-permute-start = (bf16[80,1024]{1,0:T(8,128)(2,1)}, bf16[80,1024]{1,0:T(8,128)(2,1)S(1)}, u32[]{:S(2)}, u32[]{:S(2)}) collective-permute-start(bf16[80,1024]{1,0:T(8,128)(2,1)} %bitcast.25), channel_id=1, source_target_pairs={{0,2},{2,0},{1,3},{3,1},{4,6},{6,4},{5,7},{7,5},{8,10},{10,8},{9,1... | collective-permute-start | bytes 491528 | tf_op jit(solution)/shard_map/ppermute | solution.py:112
  22.5 16.4 %all-to-all-start = ((bf16[4,80,1024]{2,1,0:T(8,128)(2,1)}), bf16[4,80,1024]{2,1,0:T(8,128)(2,1)S(1)}, u32[]{:S(2)}, u32[]{:S(2)}) async-start(bf16[4,80,1024]{2,1,0:T(8,128)(2,1)} %bitcast.11), calls=%async_computation | async-start | bytes 1310720 | tf_op jit(solution)/shard_map/all_to_all | solution.py:120
  40.0 18.7 %all-to-all-start.1 = ((bf16[4,80,1024]{2,1,0:T(8,128)(2,1)}), bf16[4,80,1024]{2,1,0:T(8,128)(2,1)S(1)}, u32[]{:S(2)}, u32[]{:S(2)}) async-start(bf16[4,80,1024]{2,1,0:T(8,128)(2,1)} %broadcast_in_dim.10), calls=%async_computation.1 | async-start | bytes 1310720 | tf_op jit(solution)/shard_map/all_to_all | solution.py:30
  45.9 55.6 %copy-start.2 = (bf16[80,2560]{1,0:T(8,128)(2,1)S(1)}, bf16[80,2560]{1,0:T(8,128)(2,1)}, u32[]{:S(2)}) copy-start(bf16[80,2560]{1,0:T(8,128)(2,1)} %param.11) | copy-start | bytes 1228804
  81.0 10.3 %collective-permute-start.2 = (bf16[80,2560]{1,0:T(8,128)(2,1)S(1)}, bf16[80,2560]{1,0:T(8,128)(2,1)S(1)}, u32[]{:S(2)}, u32[]{:S(2)}) collective-permute-start(bf16[80,2560]{1,0:T(8,128)(2,1)S(1)} %get-tuple-element.18), channel_id=1, source_target_pairs={{0,128},{1,385},{128,256},{129,1},{256,384},{257,129},{384,0},{385... | collective-permute-start | bytes 1228808 | tf_op jit(solution)/shard_map/ppermute | solution.py:136
  85.2 11.4 %collective-permute-start.1 = (bf16[80,2560]{1,0:T(8,128)(2,1)S(1)}, bf16[80,2560]{1,0:T(8,128)(2,1)S(1)}, u32[]{:S(2)}, u32[]{:S(2)}) collective-permute-start(bf16[80,2560]{1,0:T(8,128)(2,1)S(1)} %get-tuple-element.16), channel_id=1, source_target_pairs={{0,384},{1,129},{128,0},{129,257},{256,128},{257,385},{384,256},{3... | collective-permute-start | bytes 1228808 | tf_op jit(solution)/shard_map/ppermute | solution.py:137
  91.3 10.2 %collective-permute-start.3 = (bf16[80,2560]{1,0:T(8,128)(2,1)S(1)}, bf16[80,2560]{1,0:T(8,128)(2,1)S(1)}, u32[]{:S(2)}, u32[]{:S(2)}) collective-permute-start(bf16[80,2560]{1,0:T(8,128)(2,1)S(1)} %add_convert_fusion), channel_id=1, source_target_pairs={{0,128},{1,385},{128,256},{129,1},{256,384},{257,129},{384,0},{385... | collective-permute-start | bytes 1228808 | tf_op jit(solution)/shard_map/ppermute | solution.py:139
Sparse Core Ops, SparseCore 0:
  22.6 53.0 all-gather.1

commit v5 on v4

--- a/solution.py
+++ b/solution.py
@@ -65,15 +65,32 @@
         block = uppers[n // share][n % share * strip : (n % share + 1) * strip, :]
         panel[pl.ds(pl.multiple_of(to, 16), strip), :] = block
     value = (dot(rows[...], panel[...], ((1,), (1,))) * mask[...]).astype(jnp.bfloat16)
-    for k, out in enumerate(outs):
-        out[...] = value[k * strip : (k + 1) * strip, :]
+    across_a, across_b, near_a, near_b, back, kept = outs
+
+    @pl.when(pl.program_id(0) < PIECES // 2)
+    def _():
+        across_a[...] = value[:strip, :]
+        near_a[...] = value[2 * strip : 3 * strip, :]
+
+    @pl.when(pl.program_id(0) >= PIECES // 2)
+    def _():
+        across_b[...] = value[:strip, :]
+        near_b[...] = value[2 * strip : 3 * strip, :]
+
+    back[...] = value[strip : 2 * strip, :]
+    kept[...] = value[3 * strip :, :]
 
 
 def multiply(place, mask, lower, upper):
     groups, strip, width = lower.shape
     columns = upper.shape[0]
     piece = columns // PIECES
+    half = PIECES // 2
     out = pl.BlockSpec((strip, piece), lambda i: (0, i))
+    first = pl.BlockSpec((strip, piece), lambda i: (0, jnp.minimum(i, half - 1)))
+    second = pl.BlockSpec((strip, piece), lambda i: (0, jnp.maximum(i - half, 0)))
+    part = jax.ShapeDtypeStruct((strip, columns // 2), jnp.bfloat16)
+    whole = jax.ShapeDtypeStruct((strip, columns), jnp.bfloat16)
     shares = [
         pl.BlockSpec((piece // SHARES, width), lambda i, k=k: (i * SHARES + k, 0))
         for k in range(SHARES)
@@ -81,13 +98,13 @@
     return pl.pallas_call(
         multiply_kernel,
         grid=(PIECES,),
-        out_shape=(jax.ShapeDtypeStruct((strip, columns), jnp.bfloat16),) * groups,
+        out_shape=(part,) * 4 + (whole,) * 2,
         in_specs=[
             pl.BlockSpec(memory_space=pltpu.SMEM),
             pl.BlockSpec((1, piece), lambda i: (0, i)),
             pl.BlockSpec(lower.shape, lambda i: (0, 0, 0)),
         ] + shares,
-        out_specs=(out,) * groups,
+        out_specs=(first, second, first, second, out, out),
         scratch_shapes=[
             pltpu.VMEM((groups * strip, width), jnp.bfloat16),
             pltpu.VMEM((piece, width), jnp.bfloat16),
@@ -132,13 +149,18 @@
     onward = jnp.where(core_index == 0, 1, 3)
     targets = (layer_index + jnp.stack([2 * onward, 3 * onward, onward, 0 * onward])) % groups
     place = jnp.concatenate([targets, half_index[None]]).astype(jnp.int32)
-    across, back, near, kept = multiply(place, mask, lower_panel, upper)
-    across = lax.ppermute(across, ("layer", "core"), layer_pairs(1))
+    across_a, across_b, near_a, near_b, back, kept = multiply(place, mask, lower_panel, upper)
+    across = [lax.ppermute(part, ("layer", "core"), layer_pairs(1)) for part in (across_a, across_b)]
     back = lax.ppermute(back, ("layer", "core"), layer_pairs(-1))
-    near = (near.astype(jnp.float32) + across.astype(jnp.float32)).astype(jnp.bfloat16)
-    near = lax.ppermute(near, ("layer", "core"), layer_pairs(1))
-    total = kept.astype(jnp.float32) + back.astype(jnp.float32) + near.astype(jnp.float32)
-    return (ancestor_block.astype(jnp.float32) - total).astype(jnp.bfloat16)
+    total = kept.astype(jnp.float32) + back.astype(jnp.float32)
+    total = ancestor_block.astype(jnp.float32) - total
+    halves = []
+    for k, (near, part) in enumerate(zip((near_a, near_b), across)):
+        near = (near.astype(jnp.float32) + part.astype(jnp.float32)).astype(jnp.bfloat16)
+        near = lax.ppermute(near, ("layer", "core"), layer_pairs(1))
+        columns = near.shape[1]
+        halves.append(total[:, k * columns : (k + 1) * columns] - near.astype(jnp.float32))
+    return jnp.concatenate(halves, axis=1).astype(jnp.bfloat16)
 
 
 def solution(mesh):

time: 111 us -> 110 us (level); the launches traced: 109 us -> 110 us
  starting transfers between devices: 28.4 us -> 31.9 us
  waiting for transfers between devices: 54.6 us -> 51.1 us
    ppermute x1 -> x2, waiting for transfers between devices: 4.04 us -> 0.01 us  [shards(): lax.ppermute(part, ('layer', 'core'), layer_pairs(1))]
    ppermute x1 -> x2, starting transfers between devices: 4.28 us -> 6.54 us  [shards(): lax.ppermute(part, ('layer', 'core'), layer_pairs(1))]
    ppermute x1, waiting for transfers between devices: 0.01 us -> 1.33 us  [shards(): back = lax.ppermute(back, ('layer', 'core'), layer_pairs(-1))]
    ppermute x1, starting transfers between devices: 1.92 us -> 3.03 us  [shards(): back = lax.ppermute(back, ('layer', 'core'), layer_pairs(-1))]
    ppermute x1 -> x2, waiting for transfers between devices: 4.86 us -> 4 us  [shards(): near = lax.ppermute(near, ('layer', 'core'), layer_pairs(1))]
    ppermute x1 -> x2, starting transfers between devices: 5.32 us -> 5.38 us  [shards(): near = lax.ppermute(near, ('layer', 'core'), layer_pairs(1))]
  transfers between devices with their start and end apart: 7 -> 9, of which waited for: 6 -> 7; matrix products, arithmetic and copies ran while one was open for 5% -> 5% of each run, Pallas kernels for 0% -> 0%
where the time goes in v5:
time: 110 us
  waiting for transfers between devices  51.1 us (46%)
  starting transfers between devices  31.9 us (29%)
  between operations  13.5 us (12%)
  Pallas kernels  6.23 us (6%)
  matrix products  2.94 us (3%)
  other arithmetic  2.91 us (3%)
    all_gather x1, waiting for transfers between devices, shards(): upper = lax.all_gather(both, ('deep', 'core'), axis=0, tiled=True)  17 us
    all_to_all x1, waiting for transfers between devices, spread(): return lax.all_to_all(copies, axis, 0, 0, tiled=True)  12.8 us
    all_to_all x1, waiting for transfers between devices, shards(): lax.all_to_all(partial_value.reshape(groups, slab_rows, width), 'row', 0,...  12.1 us
    ppermute x1, starting transfers between devices, shards(): other = lax.ppermute(coupling_t, 'half', SWAP)  8.4 us
    ppermute x2, starting transfers between devices, shards(): lax.ppermute(part, ('layer', 'core'), layer_pairs(1))  6.54 us
    pallas_call x1, Pallas kernels, multiply(): pl.pallas_call(multiply_kernel, grid=(PIECES,), out_shape=(part,) * 4 + (...  5.49 us
    ppermute x2, starting transfers between devices, shards(): near = lax.ppermute(near, ('layer', 'core'), layer_pairs(1))  5.38 us
    all_to_all x1, starting transfers between devices, spread(): return lax.all_to_all(copies, axis, 0, 0, tiled=True)  5.03 us
  transfers between devices with their start and end apart: 9, of which 7 were waited for; matrix products, arithmetic and copies ran while one was open for 5% of the time, Pallas kernels for 0%

profile of v5, /device:TPU:1, one launch (start us, length us, event | category | flops | bytes accessed | tf_op | source)
XLA Modules:
  0.0 109.6 jit_solution(10961621269488387898)
XLA Ops:
  6.5 0.0 copy-start
  6.5 0.0 copy-start.1
  6.5 0.0 all-gather.2.cloned.1.call-start
  6.5 8.4 %collective-permute-start = (bf16[80,1024]{1,0:T(8,128)(2,1)}, bf16[80,1024]{1,0:T(8,128)(2,1)S(1)}, u32[]{:S(2)}, u32[]{:S(2)}) collective-permute-start(bf16[80,1024]{1,0:T(8,128)(2,1)} %bitcast.25), channel_id=1, source_target_pairs={{0,2},{2,0},{1,3},{3,1},{4,6},{6,4},{5,7},{7,5},{8,10},{10,8},{9,1... | collective-permute-start | bytes 491528 | tf_op jit(solution)/shard_map/ppermute | solution.py:129
  15.0 0.0 copy-done
  15.0 2.9 %fusion.5 = bf16[320,1024]{1,0:T(8,128)(2,1)} fusion(bf16[320,256]{1,0:T(8,128)(2,1)} %bitcast.27, bf16[1,1024,1024]{2,1,0:T(8,128)(2,1)S(1)} %copy-done, bf16[1,256,1024]{2,1,0:T(8,128)(2,1)} %param.7), kind=kOutput, calls=%fused_computation.5 | convolution fusion | flops 705232896 | bytes 3440640 | tf_op jit(solution)/shard_map/dot_general | solution.py:25
  17.9 3.8 %collective-permute-done.far = bf16[80,1024]{1,0:T(8,128)(2,1)S(1)} collective-permute-done((bf16[80,1024]{1,0:T(8,128)(2,1)}, bf16[80,1024]{1,0:T(8,128)(2,1)S(1)}, u32[]{:S(2)}, u32[]{:S(2)}) %collective-permute-start) | collective-permute-done | bytes 163872 | tf_op jit(solution)/shard_map/ppermute | solution.py:129
  21.7 0.0 copy-done.1
  21.7 0.7 shard_map.64
  22.4 0.0 all-gather.2.cloned.1.call-update
  22.5 3.5 %all-to-all-start = ((bf16[4,80,1024]{2,1,0:T(8,128)(2,1)}), bf16[4,80,1024]{2,1,0:T(8,128)(2,1)S(1)}, u32[]{:S(2)}, u32[]{:S(2)}) async-start(bf16[4,80,1024]{2,1,0:T(8,128)(2,1)} %bitcast.11), calls=%async_computation | async-start | bytes 1310720 | tf_op jit(solution)/shard_map/all_to_all | solution.py:137
  26.0 0.8 convert_bitcast_fusion
  26.7 12.1 %all-to-all-done = bf16[4,80,1024]{2,1,0:T(8,128)(2,1)S(1)} async-done(((bf16[4,80,1024]{2,1,0:T(8,128)(2,1)}), bf16[4,80,1024]{2,1,0:T(8,128)(2,1)S(1)}, u32[]{:S(2)}, u32[]{:S(2)}) %all-to-all-start) | async-done | bytes 655392 | tf_op jit(solution)/shard_map/all_to_all | solution.py:137
  38.9 0.1 convert_reduce_fusion
  39.0 0.1 multiply_convert_fusion
  39.1 0.9 broadcast_in_dim.10
  40.0 5.0 %all-to-all-start.1 = ((bf16[4,80,1024]{2,1,0:T(8,128)(2,1)}), bf16[4,80,1024]{2,1,0:T(8,128)(2,1)S(1)}, u32[]{:S(2)}, u32[]{:S(2)}) async-start(bf16[4,80,1024]{2,1,0:T(8,128)(2,1)} %broadcast_in_dim.10), calls=%async_computation.1 | async-start | bytes 1310720 | tf_op jit(solution)/shard_map/all_to_all | solution.py:30
  45.0 0.1 and_select_fusion
  45.1 0.1 pad_add_fusion.place
  45.2 0.7 dynamic-slice_convert_fusion.mask
  45.9 0.0 copy-start.2
  45.9 12.8 %all-to-all-done.1.lower = bf16[4,80,1024]{2,1,0:T(8,128)(2,1)S(1)} async-done(((bf16[4,80,1024]{2,1,0:T(8,128)(2,1)}), bf16[4,80,1024]{2,1,0:T(8,128)(2,1)S(1)}, u32[]{:S(2)}, u32[]{:S(2)}) %all-to-all-start.1) | async-done | bytes 655392 | tf_op jit(solution)/shard_map/all_to_all | solution.py:30
  58.7 17.0 %all-gather.2.cloned.1.call-done.refs_0_.refs_1_.refs_2_.refs_3_ = bf16[2560,1024]{1,0:T(8,128)(2,1)} async-done(((bf16[160,1024]{1,0:T(8,128)(2,1)}), bf16[2560,1024]{1,0:T(8,128)(2,1)}) %all-gather.2.cloned.1.call-update) | async-done | bytes 5242896 | tf_op jit(solution)/shard_map/all_gather | solution.py:135
  75.8 5.5 %shard_map.65 = (bf16[80,1280]{1,0:T(8,128)(2,1)S(1)}, bf16[80,1280]{1,0:T(8,128)(2,1)S(1)}, bf16[80,1280]{1,0:T(8,128)(2,1)S(1)}, bf16[80,1280]{1,0:T(8,128)(2,...) custom-call(s32[5]{0:T(128)S(1)} %pad_add_fusion.place, ...), custom_call_target="tpu_custom_call" | custom-call | tf_op jit(solution)/shard_map/pallas_call | solution.py:98
  81.3 4.3 %collective-permute-start.2 = (bf16[80,1280]{1,0:T(8,128)(2,1)S(1)}, bf16[80,1280]{1,0:T(8,128)(2,1)S(1)}, u32[]{:S(2)}, u32[]{:S(2)}) collective-permute-start(bf16[80,1280]{1,0:T(8,128)(2,1)S(1)} %get-tuple-element.20), channel_id=1, source_target_pairs={{0,128},{1,385},{128,256},{129,1},{256,384},{257,129},{384,0},{385... | collective-permute-start | bytes 614408 | tf_op jit(solution)/shard_map/ppermute | solution.py:153
  85.6 2.3 %collective-permute-start.4 = (bf16[80,1280]{1,0:T(8,128)(2,1)S(1)}, bf16[80,1280]{1,0:T(8,128)(2,1)S(1)}, u32[]{:S(2)}, u32[]{:S(2)}) collective-permute-start(bf16[80,1280]{1,0:T(8,128)(2,1)S(1)} %get-tuple-element.22), channel_id=1, source_target_pairs={{0,128},{1,385},{128,256},{129,1},{256,384},{257,129},{384,0},{385... | collective-permute-start | bytes 614408 | tf_op jit(solution)/shard_map/ppermute | solution.py:153
  87.8 3.0 %collective-permute-start.1 = (bf16[80,2560]{1,0:T(8,128)(2,1)S(1)}, bf16[80,2560]{1,0:T(8,128)(2,1)S(1)}, u32[]{:S(2)}, u32[]{:S(2)}) collective-permute-start(bf16[80,2560]{1,0:T(8,128)(2,1)S(1)} %get-tuple-element.18), channel_id=1, source_target_pairs={{0,384},{1,129},{128,0},{129,257},{256,128},{257,385},{384,256},{3... | collective-permute-start | bytes 1228808 | tf_op jit(solution)/shard_map/ppermute | solution.py:154
  90.9 0.0 collective-permute-done.2
  90.9 0.1 add_convert_fusion.1
  90.9 3.5 %collective-permute-start.3 = (bf16[80,1280]{1,0:T(8,128)(2,1)S(1)}, bf16[80,1280]{1,0:T(8,128)(2,1)S(1)}, u32[]{:S(2)}, u32[]{:S(2)}) collective-permute-start(bf16[80,1280]{1,0:T(8,128)(2,1)S(1)} %add_convert_fusion.1), channel_id=1, source_target_pairs={{0,128},{1,385},{128,256},{129,1},{256,384},{257,129},{384,0},{385... | collective-permute-start | bytes 614408 | tf_op jit(solution)/shard_map/ppermute | solution.py:160
  94.4 0.0 collective-permute-done.4
  94.4 0.1 add_convert_fusion
  94.5 1.9 %collective-permute-start.5 = (bf16[80,1280]{1,0:T(8,128)(2,1)S(1)}, bf16[80,1280]{1,0:T(8,128)(2,1)S(1)}, u32[]{:S(2)}, u32[]{:S(2)}) collective-permute-start(bf16[80,1280]{1,0:T(8,128)(2,1)S(1)} %add_convert_fusion), channel_id=1, source_target_pairs={{0,128},{1,385},{128,256},{129,1},{256,384},{257,129},{384,0},{385... | collective-permute-start | bytes 614408 | tf_op jit(solution)/shard_map/ppermute | solution.py:160
  96.4 1.3 %collective-permute-done.1 = bf16[80,2560]{1,0:T(8,128)(2,1)S(1)} collective-permute-done((bf16[80,2560]{1,0:T(8,128)(2,1)S(1)}, bf16[80,2560]{1,0:T(8,128)(2,1)S(1)}, u32[]{:S(2)}, u32[]{:S(2)}) %collective-permute-start.1) | collective-permute-done | bytes 409632 | tf_op jit(solution)/shard_map/ppermute | solution.py:154
  97.7 0.0 copy-done.2
  97.7 0.1 add_subtract_fusion
  97.9 1.8 %collective-permute-done.3 = bf16[80,1280]{1,0:T(8,128)(2,1)S(1)} collective-permute-done((bf16[80,1280]{1,0:T(8,128)(2,1)S(1)}, bf16[80,1280]{1,0:T(8,128)(2,1)S(1)}, u32[]{:S(2)}, u32[]{:S(2)}) %collective-permute-start.3) | collective-permute-done | bytes 204832 | tf_op jit(solution)/shard_map/ppermute | solution.py:160
  99.7 2.2 %collective-permute-done.5 = bf16[80,1280]{1,0:T(8,128)(2,1)S(1)} collective-permute-done((bf16[80,1280]{1,0:T(8,128)(2,1)S(1)}, bf16[80,1280]{1,0:T(8,128)(2,1)S(1)}, u32[]{:S(2)}, u32[]{:S(2)}) %collective-permute-start.5) | collective-permute-done | bytes 204832 | tf_op jit(solution)/shard_map/ppermute | solution.py:160
  101.9 0.1 fusion.11
  102.0 0.8 pad_maximum_fusion
Async XLA Ops:
  6.5 8.4 %copy-start = (bf16[1,1024,1024]{2,1,0:T(8,128)(2,1)S(1)}, bf16[1,1024,1024]{2,1,0:T(8,128)(2,1)}, u32[]{:S(2)}) copy-start(bf16[1,1024,1024]{2,1,0:T(8,128)(2,1)} %param.9) | copy-start | bytes 6291460
  6.5 15.1 %copy-start.1 = (bf16[1,1024,80]{1,2,0:T(8,128)(2,1)S(1)}, bf16[1,1024,80]{1,2,0:T(8,128)(2,1)}, u32[]{:S(2)}) copy-start(bf16[1,1024,80]{1,2,0:T(8,128)(2,1)} %param.8) | copy-start | bytes 491524
  6.5 69.2 %all-gather.2.cloned.1.call-start = ((), (), s32[]{:S(2)}) async-start(), calls=%async_computation.2 | async-start | bytes 5570560 | tf_op jit(solution)/shard_map/all_gather | solution.py:135
  6.5 15.1 %collective-permute-start = (bf16[80,1024]{1,0:T(8,128)(2,1)}, bf16[80,1024]{1,0:T(8,128)(2,1)S(1)}, u32[]{:S(2)}, u32[]{:S(2)}) collective-permute-start(bf16[80,1024]{1,0:T(8,128)(2,1)} %bitcast.25), channel_id=1, source_target_pairs={{0,2},{2,0},{1,3},{3,1},{4,6},{6,4},{5,7},{7,5},{8,10},{10,8},{9,1... | collective-permute-start | bytes 491528 | tf_op jit(solution)/shard_map/ppermute | solution.py:129
  22.5 16.4 %all-to-all-start = ((bf16[4,80,1024]{2,1,0:T(8,128)(2,1)}), bf16[4,80,1024]{2,1,0:T(8,128)(2,1)S(1)}, u32[]{:S(2)}, u32[]{:S(2)}) async-start(bf16[4,80,1024]{2,1,0:T(8,128)(2,1)} %bitcast.11), calls=%async_computation | async-start | bytes 1310720 | tf_op jit(solution)/shard_map/all_to_all | solution.py:137
  40.0 18.7 %all-to-all-start.1 = ((bf16[4,80,1024]{2,1,0:T(8,128)(2,1)}), bf16[4,80,1024]{2,1,0:T(8,128)(2,1)S(1)}, u32[]{:S(2)}, u32[]{:S(2)}) async-start(bf16[4,80,1024]{2,1,0:T(8,128)(2,1)} %broadcast_in_dim.10), calls=%async_computation.1 | async-start | bytes 1310720 | tf_op jit(solution)/shard_map/all_to_all | solution.py:30
  45.9 51.8 %copy-start.2 = (bf16[80,2560]{1,0:T(8,128)(2,1)S(1)}, bf16[80,2560]{1,0:T(8,128)(2,1)}, u32[]{:S(2)}) copy-start(bf16[80,2560]{1,0:T(8,128)(2,1)} %param.11) | copy-start | bytes 1228804
  81.3 9.6 %collective-permute-start.2 = (bf16[80,1280]{1,0:T(8,128)(2,1)S(1)}, bf16[80,1280]{1,0:T(8,128)(2,1)S(1)}, u32[]{:S(2)}, u32[]{:S(2)}) collective-permute-start(bf16[80,1280]{1,0:T(8,128)(2,1)S(1)} %get-tuple-element.20), channel_id=1, source_target_pairs={{0,128},{1,385},{128,256},{129,1},{256,384},{257,129},{384,0},{385... | collective-permute-start | bytes 614408 | tf_op jit(solution)/shard_map/ppermute | solution.py:153
  85.6 8.8 %collective-permute-start.4 = (bf16[80,1280]{1,0:T(8,128)(2,1)S(1)}, bf16[80,1280]{1,0:T(8,128)(2,1)S(1)}, u32[]{:S(2)}, u32[]{:S(2)}) collective-permute-start(bf16[80,1280]{1,0:T(8,128)(2,1)S(1)} %get-tuple-element.22), channel_id=1, source_target_pairs={{0,128},{1,385},{128,256},{129,1},{256,384},{257,129},{384,0},{385... | collective-permute-start | bytes 614408 | tf_op jit(solution)/shard_map/ppermute | solution.py:153
  87.8 9.9 %collective-permute-start.1 = (bf16[80,2560]{1,0:T(8,128)(2,1)S(1)}, bf16[80,2560]{1,0:T(8,128)(2,1)S(1)}, u32[]{:S(2)}, u32[]{:S(2)}) collective-permute-start(bf16[80,2560]{1,0:T(8,128)(2,1)S(1)} %get-tuple-element.18), channel_id=1, source_target_pairs={{0,384},{1,129},{128,0},{129,257},{256,128},{257,385},{384,256},{3... | collective-permute-start | bytes 1228808 | tf_op jit(solution)/shard_map/ppermute | solution.py:154
  90.9 8.8 %collective-permute-start.3 = (bf16[80,1280]{1,0:T(8,128)(2,1)S(1)}, bf16[80,1280]{1,0:T(8,128)(2,1)S(1)}, u32[]{:S(2)}, u32[]{:S(2)}) collective-permute-start(bf16[80,1280]{1,0:T(8,128)(2,1)S(1)} %add_convert_fusion.1), channel_id=1, source_target_pairs={{0,128},{1,385},{128,256},{129,1},{256,384},{257,129},{384,0},{385... | collective-permute-start | bytes 614408 | tf_op jit(solution)/shard_map/ppermute | solution.py:160
  94.5 7.4 %collective-permute-start.5 = (bf16[80,1280]{1,0:T(8,128)(2,1)S(1)}, bf16[80,1280]{1,0:T(8,128)(2,1)S(1)}, u32[]{:S(2)}, u32[]{:S(2)}) collective-permute-start(bf16[80,1280]{1,0:T(8,128)(2,1)S(1)} %add_convert_fusion), channel_id=1, source_target_pairs={{0,128},{1,385},{128,256},{129,1},{256,384},{257,129},{384,0},{385... | collective-permute-start | bytes 614408 | tf_op jit(solution)/shard_map/ppermute | solution.py:160
Sparse Core Ops, SparseCore 0:
  22.6 53.1 all-gather.1

commit v6 on v5

--- a/solution.py
+++ b/solution.py
@@ -8,7 +8,7 @@
 
 AXES = ("layer", "row", "deep", "half", "core")
 SWAP = [(0, 1), (1, 0)]
-PIECES = 4
+PIECES = 2
 SHARES = 4
 MULTIPLY_VMEM = 48 << 20
 

time: 110 us -> 109 us (level)
  no operation moved by 1% of the time
where the time goes in v6:
time: 109 us
  waiting for transfers between devices  51.1 us (47%)
  starting transfers between devices  31.9 us (29%)
  between operations  13.5 us (12%)
  Pallas kernels  5.41 us (5%)
  matrix products  2.94 us (3%)
  other arithmetic  2.91 us (3%)
    all_gather x1, waiting for transfers between devices, shards(): upper = lax.all_gather(both, ('deep', 'core'), axis=0, tiled=True)  17 us
    all_to_all x1, waiting for transfers between devices, spread(): return lax.all_to_all(copies, axis, 0, 0, tiled=True)  12.8 us
    all_to_all x1, waiting for transfers between devices, shards(): lax.all_to_all(partial_value.reshape(groups, slab_rows, width), 'row', 0,...  12.1 us
    ppermute x1, starting transfers between devices, shards(): other = lax.ppermute(coupling_t, 'half', SWAP)  8.4 us
    ppermute x2, starting transfers between devices, shards(): lax.ppermute(part, ('layer', 'core'), layer_pairs(1))  6.54 us
    ppermute x2, starting transfers between devices, shards(): near = lax.ppermute(near, ('layer', 'core'), layer_pairs(1))  5.38 us
    all_to_all x1, starting transfers between devices, spread(): return lax.all_to_all(copies, axis, 0, 0, tiled=True)  5.03 us
    pallas_call x1, Pallas kernels, multiply(): pl.pallas_call(multiply_kernel, grid=(PIECES,), out_shape=(part,) * 4 + (...  4.66 us
  transfers between devices with their start and end apart: 9, of which 7 were waited for; matrix products, arithmetic and copies ran while one was open for 5% of the time, Pallas kernels for 0%

profile of v6, /device:TPU:1, one launch (start us, length us, event | category | flops | bytes accessed | tf_op | source)
XLA Modules:
  0.0 108.8 jit_solution(5773454329659006840)
XLA Ops:
  6.5 0.0 copy-start
  6.5 0.0 copy-start.1
  6.5 0.0 all-gather.2.cloned.1.call-start
  6.5 8.4 %collective-permute-start = (bf16[80,1024]{1,0:T(8,128)(2,1)}, bf16[80,1024]{1,0:T(8,128)(2,1)S(1)}, u32[]{:S(2)}, u32[]{:S(2)}) collective-permute-start(bf16[80,1024]{1,0:T(8,128)(2,1)} %bitcast.25), channel_id=1, source_target_pairs={{0,2},{2,0},{1,3},{3,1},{4,6},{6,4},{5,7},{7,5},{8,10},{10,8},{9,1... | collective-permute-start | bytes 491528 | tf_op jit(solution)/shard_map/ppermute | solution.py:129
  15.0 0.0 copy-done
  15.0 2.9 %fusion.5 = bf16[320,1024]{1,0:T(8,128)(2,1)} fusion(bf16[320,256]{1,0:T(8,128)(2,1)} %bitcast.27, bf16[1,1024,1024]{2,1,0:T(8,128)(2,1)S(1)} %copy-done, bf16[1,256,1024]{2,1,0:T(8,128)(2,1)} %param.7), kind=kOutput, calls=%fused_computation.5 | convolution fusion | flops 705232896 | bytes 3440640 | tf_op jit(solution)/shard_map/dot_general | solution.py:25
  17.9 3.8 %collective-permute-done.far = bf16[80,1024]{1,0:T(8,128)(2,1)S(1)} collective-permute-done((bf16[80,1024]{1,0:T(8,128)(2,1)}, bf16[80,1024]{1,0:T(8,128)(2,1)S(1)}, u32[]{:S(2)}, u32[]{:S(2)}) %collective-permute-start) | collective-permute-done | bytes 163872 | tf_op jit(solution)/shard_map/ppermute | solution.py:129
  21.7 0.0 copy-done.1
  21.7 0.7 shard_map.64
  22.4 0.0 all-gather.2.cloned.1.call-update
  22.5 3.5 %all-to-all-start = ((bf16[4,80,1024]{2,1,0:T(8,128)(2,1)}), bf16[4,80,1024]{2,1,0:T(8,128)(2,1)S(1)}, u32[]{:S(2)}, u32[]{:S(2)}) async-start(bf16[4,80,1024]{2,1,0:T(8,128)(2,1)} %bitcast.11), calls=%async_computation | async-start | bytes 1310720 | tf_op jit(solution)/shard_map/all_to_all | solution.py:137
  26.0 0.8 convert_bitcast_fusion
  26.7 12.1 %all-to-all-done = bf16[4,80,1024]{2,1,0:T(8,128)(2,1)S(1)} async-done(((bf16[4,80,1024]{2,1,0:T(8,128)(2,1)}), bf16[4,80,1024]{2,1,0:T(8,128)(2,1)S(1)}, u32[]{:S(2)}, u32[]{:S(2)}) %all-to-all-start) | async-done | bytes 655392 | tf_op jit(solution)/shard_map/all_to_all | solution.py:137
  38.9 0.1 convert_reduce_fusion
  39.0 0.1 multiply_convert_fusion
  39.1 0.9 broadcast_in_dim.10
  40.0 5.0 %all-to-all-start.1 = ((bf16[4,80,1024]{2,1,0:T(8,128)(2,1)}), bf16[4,80,1024]{2,1,0:T(8,128)(2,1)S(1)}, u32[]{:S(2)}, u32[]{:S(2)}) async-start(bf16[4,80,1024]{2,1,0:T(8,128)(2,1)} %broadcast_in_dim.10), calls=%async_computation.1 | async-start | bytes 1310720 | tf_op jit(solution)/shard_map/all_to_all | solution.py:30
  45.0 0.1 and_select_fusion
  45.1 0.1 pad_add_fusion.place
  45.2 0.7 dynamic-slice_convert_fusion.mask
  45.9 0.0 copy-start.2
  45.9 12.8 %all-to-all-done.1.lower = bf16[4,80,1024]{2,1,0:T(8,128)(2,1)S(1)} async-done(((bf16[4,80,1024]{2,1,0:T(8,128)(2,1)}), bf16[4,80,1024]{2,1,0:T(8,128)(2,1)S(1)}, u32[]{:S(2)}, u32[]{:S(2)}) %all-to-all-start.1) | async-done | bytes 655392 | tf_op jit(solution)/shard_map/all_to_all | solution.py:30
  58.7 17.0 %all-gather.2.cloned.1.call-done.refs_0_.refs_1_.refs_2_.refs_3_ = bf16[2560,1024]{1,0:T(8,128)(2,1)} async-done(((bf16[160,1024]{1,0:T(8,128)(2,1)}), bf16[2560,1024]{1,0:T(8,128)(2,1)}) %all-gather.2.cloned.1.call-update) | async-done | bytes 5242896 | tf_op jit(solution)/shard_map/all_gather | solution.py:135
  75.8 4.7 %shard_map.65 = (bf16[80,1280]{1,0:T(8,128)(2,1)S(1)}, bf16[80,1280]{1,0:T(8,128)(2,1)S(1)}, bf16[80,1280]{1,0:T(8,128)(2,1)S(1)}, bf16[80,1280]{1,0:T(8,128)(2,...) custom-call(s32[5]{0:T(128)S(1)} %pad_add_fusion.place, ...), custom_call_target="tpu_custom_call" | custom-call | tf_op jit(solution)/shard_map/pallas_call | solution.py:98
  80.4 4.3 %collective-permute-start.2 = (bf16[80,1280]{1,0:T(8,128)(2,1)S(1)}, bf16[80,1280]{1,0:T(8,128)(2,1)S(1)}, u32[]{:S(2)}, u32[]{:S(2)}) collective-permute-start(bf16[80,1280]{1,0:T(8,128)(2,1)S(1)} %get-tuple-element.20), channel_id=1, source_target_pairs={{0,128},{1,385},{128,256},{129,1},{256,384},{257,129},{384,0},{385... | collective-permute-start | bytes 614408 | tf_op jit(solution)/shard_map/ppermute | solution.py:153
  84.7 2.2 %collective-permute-start.4 = (bf16[80,1280]{1,0:T(8,128)(2,1)S(1)}, bf16[80,1280]{1,0:T(8,128)(2,1)S(1)}, u32[]{:S(2)}, u32[]{:S(2)}) collective-permute-start(bf16[80,1280]{1,0:T(8,128)(2,1)S(1)} %get-tuple-element.22), channel_id=1, source_target_pairs={{0,128},{1,385},{128,256},{129,1},{256,384},{257,129},{384,0},{385... | collective-permute-start | bytes 614408 | tf_op jit(solution)/shard_map/ppermute | solution.py:153
  87.0 3.0 %collective-permute-start.1 = (bf16[80,2560]{1,0:T(8,128)(2,1)S(1)}, bf16[80,2560]{1,0:T(8,128)(2,1)S(1)}, u32[]{:S(2)}, u32[]{:S(2)}) collective-permute-start(bf16[80,2560]{1,0:T(8,128)(2,1)S(1)} %get-tuple-element.18), channel_id=1, source_target_pairs={{0,384},{1,129},{128,0},{129,257},{256,128},{257,385},{384,256},{3... | collective-permute-start | bytes 1228808 | tf_op jit(solution)/shard_map/ppermute | solution.py:154
  90.0 0.0 collective-permute-done.2
  90.1 0.1 add_convert_fusion.1
  90.1 3.5 %collective-permute-start.3 = (bf16[80,1280]{1,0:T(8,128)(2,1)S(1)}, bf16[80,1280]{1,0:T(8,128)(2,1)S(1)}, u32[]{:S(2)}, u32[]{:S(2)}) collective-permute-start(bf16[80,1280]{1,0:T(8,128)(2,1)S(1)} %add_convert_fusion.1), channel_id=1, source_target_pairs={{0,128},{1,385},{128,256},{129,1},{256,384},{257,129},{384,0},{385... | collective-permute-start | bytes 614408 | tf_op jit(solution)/shard_map/ppermute | solution.py:160
  93.6 0.0 collective-permute-done.4
  93.6 0.1 add_convert_fusion
  93.6 1.9 %collective-permute-start.5 = (bf16[80,1280]{1,0:T(8,128)(2,1)S(1)}, bf16[80,1280]{1,0:T(8,128)(2,1)S(1)}, u32[]{:S(2)}, u32[]{:S(2)}) collective-permute-start(bf16[80,1280]{1,0:T(8,128)(2,1)S(1)} %add_convert_fusion), channel_id=1, source_target_pairs={{0,128},{1,385},{128,256},{129,1},{256,384},{257,129},{384,0},{385... | collective-permute-start | bytes 614408 | tf_op jit(solution)/shard_map/ppermute | solution.py:160
  95.6 1.3 %collective-permute-done.1 = bf16[80,2560]{1,0:T(8,128)(2,1)S(1)} collective-permute-done((bf16[80,2560]{1,0:T(8,128)(2,1)S(1)}, bf16[80,2560]{1,0:T(8,128)(2,1)S(1)}, u32[]{:S(2)}, u32[]{:S(2)}) %collective-permute-start.1) | collective-permute-done | bytes 409632 | tf_op jit(solution)/shard_map/ppermute | solution.py:154
  96.9 0.0 copy-done.2
  96.9 0.1 add_subtract_fusion
  97.1 1.8 %collective-permute-done.3 = bf16[80,1280]{1,0:T(8,128)(2,1)S(1)} collective-permute-done((bf16[80,1280]{1,0:T(8,128)(2,1)S(1)}, bf16[80,1280]{1,0:T(8,128)(2,1)S(1)}, u32[]{:S(2)}, u32[]{:S(2)}) %collective-permute-start.3) | collective-permute-done | bytes 204832 | tf_op jit(solution)/shard_map/ppermute | solution.py:160
  98.9 2.2 %collective-permute-done.5 = bf16[80,1280]{1,0:T(8,128)(2,1)S(1)} collective-permute-done((bf16[80,1280]{1,0:T(8,128)(2,1)S(1)}, bf16[80,1280]{1,0:T(8,128)(2,1)S(1)}, u32[]{:S(2)}, u32[]{:S(2)}) %collective-permute-start.5) | collective-permute-done | bytes 204832 | tf_op jit(solution)/shard_map/ppermute | solution.py:160
  101.1 0.1 fusion.11
  101.1 0.8 pad_maximum_fusion
Async XLA Ops:
  6.5 8.4 %copy-start = (bf16[1,1024,1024]{2,1,0:T(8,128)(2,1)S(1)}, bf16[1,1024,1024]{2,1,0:T(8,128)(2,1)}, u32[]{:S(2)}) copy-start(bf16[1,1024,1024]{2,1,0:T(8,128)(2,1)} %param.9) | copy-start | bytes 6291460
  6.5 15.1 %copy-start.1 = (bf16[1,1024,80]{1,2,0:T(8,128)(2,1)S(1)}, bf16[1,1024,80]{1,2,0:T(8,128)(2,1)}, u32[]{:S(2)}) copy-start(bf16[1,1024,80]{1,2,0:T(8,128)(2,1)} %param.8) | copy-start | bytes 491524
  6.5 69.2 %all-gather.2.cloned.1.call-start = ((), (), s32[]{:S(2)}) async-start(), calls=%async_computation.2 | async-start | bytes 5570560 | tf_op jit(solution)/shard_map/all_gather | solution.py:135
  6.5 15.1 %collective-permute-start = (bf16[80,1024]{1,0:T(8,128)(2,1)}, bf16[80,1024]{1,0:T(8,128)(2,1)S(1)}, u32[]{:S(2)}, u32[]{:S(2)}) collective-permute-start(bf16[80,1024]{1,0:T(8,128)(2,1)} %bitcast.25), channel_id=1, source_target_pairs={{0,2},{2,0},{1,3},{3,1},{4,6},{6,4},{5,7},{7,5},{8,10},{10,8},{9,1... | collective-permute-start | bytes 491528 | tf_op jit(solution)/shard_map/ppermute | solution.py:129
  22.5 16.4 %all-to-all-start = ((bf16[4,80,1024]{2,1,0:T(8,128)(2,1)}), bf16[4,80,1024]{2,1,0:T(8,128)(2,1)S(1)}, u32[]{:S(2)}, u32[]{:S(2)}) async-start(bf16[4,80,1024]{2,1,0:T(8,128)(2,1)} %bitcast.11), calls=%async_computation | async-start | bytes 1310720 | tf_op jit(solution)/shard_map/all_to_all | solution.py:137
  40.0 18.7 %all-to-all-start.1 = ((bf16[4,80,1024]{2,1,0:T(8,128)(2,1)}), bf16[4,80,1024]{2,1,0:T(8,128)(2,1)S(1)}, u32[]{:S(2)}, u32[]{:S(2)}) async-start(bf16[4,80,1024]{2,1,0:T(8,128)(2,1)} %broadcast_in_dim.10), calls=%async_computation.1 | async-start | bytes 1310720 | tf_op jit(solution)/shard_map/all_to_all | solution.py:30
  45.9 51.0 %copy-start.2 = (bf16[80,2560]{1,0:T(8,128)(2,1)S(1)}, bf16[80,2560]{1,0:T(8,128)(2,1)}, u32[]{:S(2)}) copy-start(bf16[80,2560]{1,0:T(8,128)(2,1)} %param.11) | copy-start | bytes 1228804
  80.4 9.6 %collective-permute-start.2 = (bf16[80,1280]{1,0:T(8,128)(2,1)S(1)}, bf16[80,1280]{1,0:T(8,128)(2,1)S(1)}, u32[]{:S(2)}, u32[]{:S(2)}) collective-permute-start(bf16[80,1280]{1,0:T(8,128)(2,1)S(1)} %get-tuple-element.20), channel_id=1, source_target_pairs={{0,128},{1,385},{128,256},{129,1},{256,384},{257,129},{384,0},{385... | collective-permute-start | bytes 614408 | tf_op jit(solution)/shard_map/ppermute | solution.py:153
  84.7 8.8 %collective-permute-start.4 = (bf16[80,1280]{1,0:T(8,128)(2,1)S(1)}, bf16[80,1280]{1,0:T(8,128)(2,1)S(1)}, u32[]{:S(2)}, u32[]{:S(2)}) collective-permute-start(bf16[80,1280]{1,0:T(8,128)(2,1)S(1)} %get-tuple-element.22), channel_id=1, source_target_pairs={{0,128},{1,385},{128,256},{129,1},{256,384},{257,129},{384,0},{385... | collective-permute-start | bytes 614408 | tf_op jit(solution)/shard_map/ppermute | solution.py:153
  87.0 9.9 %collective-permute-start.1 = (bf16[80,2560]{1,0:T(8,128)(2,1)S(1)}, bf16[80,2560]{1,0:T(8,128)(2,1)S(1)}, u32[]{:S(2)}, u32[]{:S(2)}) collective-permute-start(bf16[80,2560]{1,0:T(8,128)(2,1)S(1)} %get-tuple-element.18), channel_id=1, source_target_pairs={{0,384},{1,129},{128,0},{129,257},{256,128},{257,385},{384,256},{3... | collective-permute-start | bytes 1228808 | tf_op jit(solution)/shard_map/ppermute | solution.py:154
  90.1 8.8 %collective-permute-start.3 = (bf16[80,1280]{1,0:T(8,128)(2,1)S(1)}, bf16[80,1280]{1,0:T(8,128)(2,1)S(1)}, u32[]{:S(2)}, u32[]{:S(2)}) collective-permute-start(bf16[80,1280]{1,0:T(8,128)(2,1)S(1)} %add_convert_fusion.1), channel_id=1, source_target_pairs={{0,128},{1,385},{128,256},{129,1},{256,384},{257,129},{384,0},{385... | collective-permute-start | bytes 614408 | tf_op jit(solution)/shard_map/ppermute | solution.py:160
  93.6 7.4 %collective-permute-start.5 = (bf16[80,1280]{1,0:T(8,128)(2,1)S(1)}, bf16[80,1280]{1,0:T(8,128)(2,1)S(1)}, u32[]{:S(2)}, u32[]{:S(2)}) collective-permute-start(bf16[80,1280]{1,0:T(8,128)(2,1)S(1)} %add_convert_fusion), channel_id=1, source_target_pairs={{0,128},{1,385},{128,256},{129,1},{256,384},{257,129},{384,0},{385... | collective-permute-start | bytes 614408 | tf_op jit(solution)/shard_map/ppermute | solution.py:160
Sparse Core Ops, SparseCore 0:
  22.6 53.1 all-gather.1

commit v7 on v6

--- a/solution.py
+++ b/solution.py
@@ -1,3 +1,5 @@
+import functools
+
 import jax
 import jax.numpy as jnp
 from jax import lax
@@ -48,14 +50,14 @@
     )(own, far)
 
 
-def multiply_kernel(place, mask, lower, *refs):
+def multiply_kernel(first, place, mask, lower, *refs):
     uppers, outs, (rows, panel) = refs[:SHARES], refs[SHARES:-2], refs[-2:]
     strip = lower.shape[1]
 
     @pl.when(pl.program_id(0) == 0)
     def _():
-        for k in range(4):
-            rows[k * strip : (k + 1) * strip, :] = lower[place[k]]
+        for k in range(rows.shape[0] // strip):
+            rows[k * strip : (k + 1) * strip, :] = lower[place[first + k]]
 
     half = place[4]
     share = uppers[0].shape[0] // strip
@@ -65,7 +67,10 @@
         block = uppers[n // share][n % share * strip : (n % share + 1) * strip, :]
         panel[pl.ds(pl.multiple_of(to, 16), strip), :] = block
     value = (dot(rows[...], panel[...], ((1,), (1,))) * mask[...]).astype(jnp.bfloat16)
-    across_a, across_b, near_a, near_b, back, kept = outs
+    if first:
+        outs[0][...] = value
+        return
+    across_a, across_b, near_a, near_b, back = outs
 
     @pl.when(pl.program_id(0) < PIECES // 2)
     def _():
@@ -78,10 +83,9 @@
         near_b[...] = value[2 * strip : 3 * strip, :]
 
     back[...] = value[strip : 2 * strip, :]
-    kept[...] = value[3 * strip :, :]
 
 
-def multiply(place, mask, lower, upper):
+def multiply(kept, place, mask, lower, upper):
     groups, strip, width = lower.shape
     columns = upper.shape[0]
     piece = columns // PIECES
@@ -96,17 +100,17 @@
         for k in range(SHARES)
     ]
     return pl.pallas_call(
-        multiply_kernel,
+        functools.partial(multiply_kernel, 3 if kept else 0),
         grid=(PIECES,),
-        out_shape=(part,) * 4 + (whole,) * 2,
+        out_shape=(whole,) if kept else (part,) * 4 + (whole,),
         in_specs=[
             pl.BlockSpec(memory_space=pltpu.SMEM),
             pl.BlockSpec((1, piece), lambda i: (0, i)),
             pl.BlockSpec(lower.shape, lambda i: (0, 0, 0)),
         ] + shares,
-        out_specs=(first, second, first, second, out, out),
+        out_specs=(out,) if kept else (first, second, first, second, out),
         scratch_shapes=[
-            pltpu.VMEM((groups * strip, width), jnp.bfloat16),
+            pltpu.VMEM(((1 if kept else 3) * strip, width), jnp.bfloat16),
             pltpu.VMEM((piece, width), jnp.bfloat16),
         ],
         compiler_params=pltpu.CompilerParams(vmem_limit_bytes=MULTIPLY_VMEM),
@@ -133,7 +137,6 @@
     other, partial_value = lax.optimization_barrier((other, partial_value))
     both = join(coupling_t, other)
     upper = lax.all_gather(both, ("deep", "core"), axis=0, tiled=True)
-    partial_value, both = lax.optimization_barrier((partial_value, both))
     arrived = lax.all_to_all(
         partial_value.reshape(groups, slab_rows, width), "row", 0, 0, tiled=True
     )
@@ -149,17 +152,23 @@
     onward = jnp.where(core_index == 0, 1, 3)
     targets = (layer_index + jnp.stack([2 * onward, 3 * onward, onward, 0 * onward])) % groups
     place = jnp.concatenate([targets, half_index[None]]).astype(jnp.int32)
-    across_a, across_b, near_a, near_b, back, kept = multiply(place, mask, lower_panel, upper)
+    across_a, across_b, near_a, near_b, back = multiply(False, place, mask, lower_panel, upper)
     across = [lax.ppermute(part, ("layer", "core"), layer_pairs(1)) for part in (across_a, across_b)]
     back = lax.ppermute(back, ("layer", "core"), layer_pairs(-1))
+    near = [
+        (near.astype(jnp.float32) + part.astype(jnp.float32)).astype(jnp.bfloat16)
+        for near, part in zip((near_a, near_b), across)
+    ]
+    lower_panel, near[1] = lax.optimization_barrier((lower_panel, near[1]))
+    (kept,) = multiply(True, place, mask, lower_panel, upper)
+    near = [lax.ppermute(part, ("layer", "core"), layer_pairs(1)) for part in near]
     total = kept.astype(jnp.float32) + back.astype(jnp.float32)
     total = ancestor_block.astype(jnp.float32) - total
-    halves = []
-    for k, (near, part) in enumerate(zip((near_a, near_b), across)):
-        near = (near.astype(jnp.float32) + part.astype(jnp.float32)).astype(jnp.bfloat16)
-        near = lax.ppermute(near, ("layer", "core"), layer_pairs(1))
-        columns = near.shape[1]
-        halves.append(total[:, k * columns : (k + 1) * columns] - near.astype(jnp.float32))
+    columns = near[0].shape[1]
+    halves = [
+        total[:, k * columns : (k + 1) * columns] - part.astype(jnp.float32)
+        for k, part in enumerate(near)
+    ]
     return jnp.concatenate(halves, axis=1).astype(jnp.bfloat16)
 
 

time: 109 us -> 109 us (level)
  waiting for transfers between devices: 51.1 us -> 47 us
  Pallas kernels: 5.41 us -> 8.98 us
    ppermute x2 -> x4, starting transfers between devices: 6.54 us -> 12.1 us  [shards(): lax.ppermute(part, ('layer', 'core'), layer_pairs(1))]
    ppermute x2 -> x0, starting transfers between devices: 5.38 us -> none  [shards(): near = lax.ppermute(near, ('layer', 'core'), layer_pairs(1))]
    ppermute x2 -> x0, waiting for transfers between devices: 4.01 us -> none  [shards(): near = lax.ppermute(near, ('layer', 'core'), layer_pairs(1))]
    pallas_call x1 -> x2, Pallas kernels: 4.66 us -> 8.24 us  [multiply(): pl.pallas_call(functools.partial(multiply_kernel, 3 if kept else 0), grid...]
    ppermute x1, waiting for transfers between devices: 1.33 us -> 0.01 us  [shards(): back = lax.ppermute(back, ('layer', 'core'), layer_pairs(-1))]
    ppermute x2 -> x4, waiting for transfers between devices: 0.01 us -> 1.24 us  [shards(): lax.ppermute(part, ('layer', 'core'), layer_pairs(1))]
  transfers between devices with their start and end apart: 9 -> 9, of which waited for: 7 -> 5; matrix products, arithmetic and copies ran while one was open for 5% -> 5% of each run, Pallas kernels for 0% -> 4%
where the time goes in v7:
time: 109 us; the launch traced here: 108 us
  waiting for transfers between devices  47 us (43%)
  starting transfers between devices  32 us (29%)
  between operations  13.6 us (12%)
  Pallas kernels  8.98 us (8%)
  matrix products  2.94 us (3%)
  other arithmetic  2.92 us (3%)
    all_gather x1, waiting for transfers between devices, shards(): upper = lax.all_gather(both, ('deep', 'core'), axis=0, tiled=True)  17 us
    all_to_all x1, waiting for transfers between devices, spread(): return lax.all_to_all(copies, axis, 0, 0, tiled=True)  12.8 us
    all_to_all x1, waiting for transfers between devices, shards(): lax.all_to_all(partial_value.reshape(groups, slab_rows, width), 'row', 0,...  12.1 us
    ppermute x4, starting transfers between devices, shards(): lax.ppermute(part, ('layer', 'core'), layer_pairs(1))  12.1 us
    ppermute x1, starting transfers between devices, shards(): other = lax.ppermute(coupling_t, 'half', SWAP)  8.4 us
    pallas_call x2, Pallas kernels, multiply(): pl.pallas_call(functools.partial(multiply_kernel, 3 if kept else 0), grid...  8.24 us
    all_to_all x1, starting transfers between devices, spread(): return lax.all_to_all(copies, axis, 0, 0, tiled=True)  5.03 us
    ppermute x1, waiting for transfers between devices, shards(): other = lax.ppermute(coupling_t, 'half', SWAP)  3.78 us
  transfers between devices with their start and end apart: 9, of which 5 were waited for; matrix products, arithmetic and copies ran while one was open for 5% of the time, Pallas kernels for 4%

profile of v7, /device:TPU:1, one launch (start us, length us, event | category | flops | bytes accessed | tf_op | source)
XLA Modules:
  0.0 108.4 jit_solution(2886851232437786543)
XLA Ops:
  6.5 0.0 copy-start
  6.5 0.0 copy-start.1
  6.5 0.0 all-gather.2.cloned.1.call-start
  6.5 8.4 %collective-permute-start = (bf16[80,1024]{1,0:T(8,128)(2,1)}, bf16[80,1024]{1,0:T(8,128)(2,1)S(1)}, u32[]{:S(2)}, u32[]{:S(2)}) collective-permute-start(bf16[80,1024]{1,0:T(8,128)(2,1)} %bitcast.25), channel_id=1, source_target_pairs={{0,2},{2,0},{1,3},{3,1},{4,6},{6,4},{5,7},{7,5},{8,10},{10,8},{9,1... | collective-permute-start | bytes 491528 | tf_op jit(solution)/shard_map/ppermute | solution.py:133
  15.0 0.0 copy-done
  15.0 2.9 %fusion.5 = bf16[320,1024]{1,0:T(8,128)(2,1)} fusion(bf16[320,256]{1,0:T(8,128)(2,1)} %bitcast.27, bf16[1,1024,1024]{2,1,0:T(8,128)(2,1)S(1)} %copy-done, bf16[1,256,1024]{2,1,0:T(8,128)(2,1)} %param.7), kind=kOutput, calls=%fused_computation.5 | convolution fusion | flops 705232896 | bytes 3440640 | tf_op jit(solution)/shard_map/dot_general | solution.py:27
  17.9 3.8 %collective-permute-done.far = bf16[80,1024]{1,0:T(8,128)(2,1)S(1)} collective-permute-done((bf16[80,1024]{1,0:T(8,128)(2,1)}, bf16[80,1024]{1,0:T(8,128)(2,1)S(1)}, u32[]{:S(2)}, u32[]{:S(2)}) %collective-permute-start) | collective-permute-done | bytes 163872 | tf_op jit(solution)/shard_map/ppermute | solution.py:133
  21.7 0.0 copy-done.1
  21.7 0.7 shard_map.64
  22.4 0.0 all-gather.2.cloned.1.call-update
  22.5 3.5 %all-to-all-start = ((bf16[4,80,1024]{2,1,0:T(8,128)(2,1)}), bf16[4,80,1024]{2,1,0:T(8,128)(2,1)S(1)}, u32[]{:S(2)}, u32[]{:S(2)}) async-start(bf16[4,80,1024]{2,1,0:T(8,128)(2,1)} %bitcast.10), calls=%async_computation | async-start | bytes 1310720 | tf_op jit(solution)/shard_map/all_to_all | solution.py:140
  26.0 0.8 convert_bitcast_fusion
  26.7 12.1 %all-to-all-done = bf16[4,80,1024]{2,1,0:T(8,128)(2,1)S(1)} async-done(((bf16[4,80,1024]{2,1,0:T(8,128)(2,1)}), bf16[4,80,1024]{2,1,0:T(8,128)(2,1)S(1)}, u32[]{:S(2)}, u32[]{:S(2)}) %all-to-all-start) | async-done | bytes 655392 | tf_op jit(solution)/shard_map/all_to_all | solution.py:140
  38.9 0.1 convert_reduce_fusion
  39.0 0.1 multiply_convert_fusion
  39.1 0.9 broadcast_in_dim.10
  40.0 5.0 %all-to-all-start.1 = ((bf16[4,80,1024]{2,1,0:T(8,128)(2,1)}), bf16[4,80,1024]{2,1,0:T(8,128)(2,1)S(1)}, u32[]{:S(2)}, u32[]{:S(2)}) async-start(bf16[4,80,1024]{2,1,0:T(8,128)(2,1)} %broadcast_in_dim.10), calls=%async_computation.1 | async-start | bytes 1310720 | tf_op jit(solution)/shard_map/all_to_all | solution.py:32
  45.0 0.1 and_select_fusion
  45.1 0.1 pad_add_fusion.place
  45.2 0.7 dynamic-slice_convert_fusion.mask
  45.9 12.8 %all-to-all-done.1.lower = bf16[4,80,1024]{2,1,0:T(8,128)(2,1)S(1)} async-done(((bf16[4,80,1024]{2,1,0:T(8,128)(2,1)}), bf16[4,80,1024]{2,1,0:T(8,128)(2,1)S(1)}, u32[]{:S(2)}, u32[]{:S(2)}) %all-to-all-start.1) | async-done | bytes 655392 | tf_op jit(solution)/shard_map/all_to_all | solution.py:32
  58.7 17.0 %all-gather.2.cloned.1.call-done.refs_0_.refs_1_.refs_2_.refs_3_ = bf16[2560,1024]{1,0:T(8,128)(2,1)} async-done(((bf16[160,1024]{1,0:T(8,128)(2,1)}), bf16[2560,1024]{1,0:T(8,128)(2,1)}) %all-gather.2.cloned.1.call-update) | async-done | bytes 5242896 | tf_op jit(solution)/shard_map/all_gather | solution.py:139
  75.8 4.3 %shard_map.65 = (bf16[80,1280]{1,0:T(8,128)(2,1)S(1)}, bf16[80,1280]{1,0:T(8,128)(2,1)S(1)}, bf16[80,1280]{1,0:T(8,128)(2,1)S(1)}, bf16[80,1280]{1,0:T(8,128)(2,1)S(1)}, bf16[80,2560]{1,0:T(8,128)(2,1)S(1)}) custom-call(s32[5]{0:T(128)S(1)} %pad_add_fusion.place, f32[1,2560]{1,0:T(1,128)S(1)} %dynamic-slice_convert_fusion.mask, ...), custom_call_target="tpu_custom_call" | custom-call | tf_op jit(solution)/shard_map/pallas_call | solution.py:102
  80.1 4.3 %collective-permute-start.1 = (bf16[80,1280]{1,0:T(8,128)(2,1)S(1)}, bf16[80,1280]{1,0:T(8,128)(2,1)S(1)}, u32[]{:S(2)}, u32[]{:S(2)}) collective-permute-start(bf16[80,1280]{1,0:T(8,128)(2,1)S(1)} %get-tuple-element.17), channel_id=1, source_target_pairs={{0,128},{1,385},{128,256},{129,1},{256,384},{257,129},{384,0},{385... | collective-permute-start | bytes 614408 | tf_op jit(solution)/shard_map/ppermute | solution.py:156
  84.4 2.2 %collective-permute-start.3 = (bf16[80,1280]{1,0:T(8,128)(2,1)S(1)}, bf16[80,1280]{1,0:T(8,128)(2,1)S(1)}, u32[]{:S(2)}, u32[]{:S(2)}) collective-permute-start(bf16[80,1280]{1,0:T(8,128)(2,1)S(1)} %get-tuple-element.21), channel_id=1, source_target_pairs={{0,128},{1,385},{128,256},{129,1},{256,384},{257,129},{384,0},{385... | collective-permute-start | bytes 614408 | tf_op jit(solution)/shard_map/ppermute | solution.py:156
  86.6 3.0 %collective-permute-start.2 = (bf16[80,2560]{1,0:T(8,128)(2,1)S(1)}, bf16[80,2560]{1,0:T(8,128)(2,1)S(1)}, u32[]{:S(2)}, u32[]{:S(2)}) collective-permute-start(bf16[80,2560]{1,0:T(8,128)(2,1)S(1)} %get-tuple-element.19), channel_id=1, source_target_pairs={{0,384},{1,129},{128,0},{129,257},{256,128},{257,385},{384,256},{3... | collective-permute-start | bytes 1228808 | tf_op jit(solution)/shard_map/ppermute | solution.py:157
  89.7 0.0 collective-permute-done.1
  89.7 0.1 add_convert_fusion.1
  89.8 3.5 %collective-permute-start.5 = (bf16[80,1280]{1,0:T(8,128)(2,1)S(1)}, bf16[80,1280]{1,0:T(8,128)(2,1)S(1)}, u32[]{:S(2)}, u32[]{:S(2)}) collective-permute-start(bf16[80,1280]{1,0:T(8,128)(2,1)S(1)} %add_convert_fusion.1), channel_id=1, source_target_pairs={{0,128},{1,385},{128,256},{129,1},{256,384},{257,129},{384,0},{385... | collective-permute-start | bytes 614408 | tf_op jit(solution)/shard_map/ppermute | solution.py:164
  93.2 0.0 collective-permute-done.3
  93.2 0.1 add_convert_fusion
  93.3 0.0 copy-start.2
  93.3 2.1 %collective-permute-start.4 = (bf16[80,1280]{1,0:T(8,128)(2,1)S(1)}, bf16[80,1280]{1,0:T(8,128)(2,1)S(1)}, u32[]{:S(2)}, u32[]{:S(2)}) collective-permute-start(bf16[80,1280]{1,0:T(8,128)(2,1)S(1)} %add_convert_fusion), channel_id=1, source_target_pairs={{0,128},{1,385},{128,256},{129,1},{256,384},{257,129},{384,0},{385... | collective-permute-start | bytes 614408 | tf_op jit(solution)/shard_map/ppermute | solution.py:164
  95.4 3.9 %shard_map.66 = bf16[80,2560]{1,0:T(8,128)(2,1)S(1)} custom-call(s32[5]{0:T(128)S(1)} %pad_add_fusion.place, f32[1,2560]{1,0:T(1,128)S(1)} %dynamic-slice_convert_fusion.mask, bf16[4,80,1024]{2,1,0:T(8,128)(2,1)S(1)} %all-to-all-done.1.lower, bf16[2560,1024]{1,0:T(8,128)(2,1)} %all-gather.2.cloned.1.call-done.refs_0_.refs_1_.refs_2_.refs_3_, ...), custom_call_target="tpu_custom_call" | custom-call | tf_op jit(solution)/shard_map/pallas_call | solution.py:102
  99.3 0.0 collective-permute-done.2
  99.3 0.0 copy-done.2
  99.3 0.1 add_subtract_fusion
  99.5 0.0 collective-permute-done.5
  99.5 1.2 %collective-permute-done.4 = bf16[80,1280]{1,0:T(8,128)(2,1)S(1)} collective-permute-done((bf16[80,1280]{1,0:T(8,128)(2,1)S(1)}, bf16[80,1280]{1,0:T(8,128)(2,1)S(1)}, u32[]{:S(2)}, u32[]{:S(2)}) %collective-permute-start.4) | collective-permute-done | bytes 204832 | tf_op jit(solution)/shard_map/ppermute | solution.py:164
  100.7 0.1 fusion.11
  100.8 0.8 pad_maximum_fusion
Async XLA Ops:
  6.5 8.4 %copy-start = (bf16[1,1024,1024]{2,1,0:T(8,128)(2,1)S(1)}, bf16[1,1024,1024]{2,1,0:T(8,128)(2,1)}, u32[]{:S(2)}) copy-start(bf16[1,1024,1024]{2,1,0:T(8,128)(2,1)} %param.9) | copy-start | bytes 6291460
  6.5 15.1 %copy-start.1 = (bf16[1,1024,80]{1,2,0:T(8,128)(2,1)S(1)}, bf16[1,1024,80]{1,2,0:T(8,128)(2,1)}, u32[]{:S(2)}) copy-start(bf16[1,1024,80]{1,2,0:T(8,128)(2,1)} %param.8) | copy-start | bytes 491524
  6.5 69.2 %all-gather.2.cloned.1.call-start = ((), (), s32[]{:S(2)}) async-start(), calls=%async_computation.2 | async-start | bytes 5570560 | tf_op jit(solution)/shard_map/all_gather | solution.py:139
  6.5 15.1 %collective-permute-start = (bf16[80,1024]{1,0:T(8,128)(2,1)}, bf16[80,1024]{1,0:T(8,128)(2,1)S(1)}, u32[]{:S(2)}, u32[]{:S(2)}) collective-permute-start(bf16[80,1024]{1,0:T(8,128)(2,1)} %bitcast.25), channel_id=1, source_target_pairs={{0,2},{2,0},{1,3},{3,1},{4,6},{6,4},{5,7},{7,5},{8,10},{10,8},{9,1... | collective-permute-start | bytes 491528 | tf_op jit(solution)/shard_map/ppermute | solution.py:133
  22.5 16.4 %all-to-all-start = ((bf16[4,80,1024]{2,1,0:T(8,128)(2,1)}), bf16[4,80,1024]{2,1,0:T(8,128)(2,1)S(1)}, u32[]{:S(2)}, u32[]{:S(2)}) async-start(bf16[4,80,1024]{2,1,0:T(8,128)(2,1)} %bitcast.10), calls=%async_computation | async-start | bytes 1310720 | tf_op jit(solution)/shard_map/all_to_all | solution.py:140
  40.0 18.7 %all-to-all-start.1 = ((bf16[4,80,1024]{2,1,0:T(8,128)(2,1)}), bf16[4,80,1024]{2,1,0:T(8,128)(2,1)S(1)}, u32[]{:S(2)}, u32[]{:S(2)}) async-start(bf16[4,80,1024]{2,1,0:T(8,128)(2,1)} %broadcast_in_dim.10), calls=%async_computation.1 | async-start | bytes 1310720 | tf_op jit(solution)/shard_map/all_to_all | solution.py:32
  80.1 9.6 %collective-permute-start.1 = (bf16[80,1280]{1,0:T(8,128)(2,1)S(1)}, bf16[80,1280]{1,0:T(8,128)(2,1)S(1)}, u32[]{:S(2)}, u32[]{:S(2)}) collective-permute-start(bf16[80,1280]{1,0:T(8,128)(2,1)S(1)} %get-tuple-element.17), channel_id=1, source_target_pairs={{0,128},{1,385},{128,256},{129,1},{256,384},{257,129},{384,0},{385... | collective-permute-start | bytes 614408 | tf_op jit(solution)/shard_map/ppermute | solution.py:156
  84.4 8.8 %collective-permute-start.3 = (bf16[80,1280]{1,0:T(8,128)(2,1)S(1)}, bf16[80,1280]{1,0:T(8,128)(2,1)S(1)}, u32[]{:S(2)}, u32[]{:S(2)}) collective-permute-start(bf16[80,1280]{1,0:T(8,128)(2,1)S(1)} %get-tuple-element.21), channel_id=1, source_target_pairs={{0,128},{1,385},{128,256},{129,1},{256,384},{257,129},{384,0},{385... | collective-permute-start | bytes 614408 | tf_op jit(solution)/shard_map/ppermute | solution.py:156
  86.6 12.7 %collective-permute-start.2 = (bf16[80,2560]{1,0:T(8,128)(2,1)S(1)}, bf16[80,2560]{1,0:T(8,128)(2,1)S(1)}, u32[]{:S(2)}, u32[]{:S(2)}) collective-permute-start(bf16[80,2560]{1,0:T(8,128)(2,1)S(1)} %get-tuple-element.19), channel_id=1, source_target_pairs={{0,384},{1,129},{128,0},{129,257},{256,128},{257,385},{384,256},{3... | collective-permute-start | bytes 1228808 | tf_op jit(solution)/shard_map/ppermute | solution.py:157
  89.8 9.7 %collective-permute-start.5 = (bf16[80,1280]{1,0:T(8,128)(2,1)S(1)}, bf16[80,1280]{1,0:T(8,128)(2,1)S(1)}, u32[]{:S(2)}, u32[]{:S(2)}) collective-permute-start(bf16[80,1280]{1,0:T(8,128)(2,1)S(1)} %add_convert_fusion.1), channel_id=1, source_target_pairs={{0,128},{1,385},{128,256},{129,1},{256,384},{257,129},{384,0},{385... | collective-permute-start | bytes 614408 | tf_op jit(solution)/shard_map/ppermute | solution.py:164
  93.3 6.0 %copy-start.2 = (bf16[80,2560]{1,0:T(8,128)(2,1)S(1)}, bf16[80,2560]{1,0:T(8,128)(2,1)}, u32[]{:S(2)}) copy-start(bf16[80,2560]{1,0:T(8,128)(2,1)} %param.11) | copy-start | bytes 1228804
  93.3 7.4 %collective-permute-start.4 = (bf16[80,1280]{1,0:T(8,128)(2,1)S(1)}, bf16[80,1280]{1,0:T(8,128)(2,1)S(1)}, u32[]{:S(2)}, u32[]{:S(2)}) collective-permute-start(bf16[80,1280]{1,0:T(8,128)(2,1)S(1)} %add_convert_fusion), channel_id=1, source_target_pairs={{0,128},{1,385},{128,256},{129,1},{256,384},{257,129},{384,0},{385... | collective-permute-start | bytes 614408 | tf_op jit(solution)/shard_map/ppermute | solution.py:164
Sparse Core Ops, SparseCore 0:
  22.6 53.1 all-gather.1

commit v8 on v7

--- a/solution.py
+++ b/solution.py
@@ -32,22 +32,41 @@
     return lax.all_to_all(copies, axis, 0, 0, tiled=True)
 
 
-def join_kernel(own, far, out):
-    rows = own.shape[0]
-    out[:rows, :] = own[...]
-    out[rows:, :] = far[...]
-
-
-def join(own, far):
+def place_kernel(rows, held, part, out, sem):
+    count = part.shape[0]
+    copy = pltpu.make_async_copy(part, out.at[rows : rows + count, :], sem)
+    copy.start()
+    copy.wait()
+
+
+def stage_kernel(part, out):
+    count = part.shape[0]
+    out[:count, :] = part[...]
+    out[count:, :] = jnp.zeros_like(part)
+
+
+def stage(own):
     rows, width = own.shape
     vmem = pl.BlockSpec(memory_space=pltpu.VMEM)
     return pl.pallas_call(
-        join_kernel,
+        stage_kernel,
         out_shape=jax.ShapeDtypeStruct((2 * rows, width), own.dtype),
-        in_specs=[vmem] * 2,
+        in_specs=[vmem],
         out_specs=vmem,
         compiler_params=pltpu.CompilerParams(vmem_limit_bytes=32 << 20),
-    )(own, far)
+    )(own)
+
+
+def put_far(held, far):
+    return pl.pallas_call(
+        functools.partial(place_kernel, far.shape[0]),
+        out_shape=jax.ShapeDtypeStruct(held.shape, held.dtype),
+        in_specs=[pl.BlockSpec(memory_space=pl.ANY)] * 2,
+        out_specs=pl.BlockSpec(memory_space=pl.ANY),
+        scratch_shapes=[pltpu.SemaphoreType.DMA],
+        input_output_aliases={0: 0},
+        compiler_params=pltpu.CompilerParams(vmem_limit_bytes=32 << 20),
+    )(held, far)
 
 
 def multiply_kernel(first, place, mask, lower, *refs):
@@ -134,8 +153,9 @@
     solver = dot(upper_inverse[0], lower_inverse[0], ((1,), (0,))).astype(jnp.bfloat16)
     coupling = lower_coupling[0].reshape(groups * slab_rows, -1)
     partial_value = dot(coupling, solver, ((1,), (0,))).astype(jnp.bfloat16)
-    other, partial_value = lax.optimization_barrier((other, partial_value))
-    both = join(coupling_t, other)
+    held = stage(coupling_t)
+    other, partial_value, held = lax.optimization_barrier((other, partial_value, held))
+    both = put_far(held, other)
     upper = lax.all_gather(both, ("deep", "core"), axis=0, tiled=True)
     arrived = lax.all_to_all(
         partial_value.reshape(groups, slab_rows, width), "row", 0, 0, tiled=True

time: 109 us -> 109 us (level)
  waiting for transfers between devices: 47 us -> 45.4 us
    ppermute x1, waiting for transfers between devices: 3.78 us -> 2.12 us  [shards(): other = lax.ppermute(coupling_t, 'half', SWAP)]
where the time goes in v8:
time: 109 us; the launch traced here: 108 us
  waiting for transfers between devices  45.4 us (42%)
  starting transfers between devices  32 us (29%)
  between operations  13.6 us (12%)
  Pallas kernels  9.67 us (9%)
  matrix products  2.93 us (3%)
  other arithmetic  2.92 us (3%)
  local copies, waits for them, and re-layouts  1.87 us (2%)
    all_gather x1, waiting for transfers between devices, shards(): upper = lax.all_gather(both, ('deep', 'core'), axis=0, tiled=True)  17 us
    all_to_all x1, waiting for transfers between devices, spread(): return lax.all_to_all(copies, axis, 0, 0, tiled=True)  12.8 us
    all_to_all x1, waiting for transfers between devices, shards(): lax.all_to_all(partial_value.reshape(groups, slab_rows, width), 'row', 0,...  12.1 us
    ppermute x4, starting transfers between devices, shards(): lax.ppermute(part, ('layer', 'core'), layer_pairs(1))  12.1 us
    ppermute x1, starting transfers between devices, shards(): other = lax.ppermute(coupling_t, 'half', SWAP)  8.4 us
    pallas_call x2, Pallas kernels, multiply(): pl.pallas_call(functools.partial(multiply_kernel, 3 if kept else 0), grid...  8.25 us
    all_to_all x1, starting transfers between devices, spread(): return lax.all_to_all(copies, axis, 0, 0, tiled=True)  5.03 us
    all_to_all x1, starting transfers between devices, shards(): lax.all_to_all(partial_value.reshape(groups, slab_rows, width), 'row', 0,...  3.49 us
  transfers between devices with their start and end apart: 9, of which 5 were waited for; matrix products, arithmetic and copies ran while one was open for 5% of the time, Pallas kernels for 4%

profile of v8, /device:TPU:1, one launch (start us, length us, event | category | flops | bytes accessed | tf_op | source)
XLA Modules:
  0.0 108.3 jit_solution(9987215851137382751)
XLA Ops:
  6.5 0.0 copy-start
  6.5 0.0 all-gather.2.cloned.1.call-start
  6.5 8.4 %collective-permute-start = (bf16[80,1024]{1,0:T(8,128)(2,1)}, bf16[80,1024]{1,0:T(8,128)(2,1)S(1)}, u32[]{:S(2)}, u32[]{:S(2)}) collective-permute-start(bf16[80,1024]{1,0:T(8,128)(2,1)} %bitcast.25), channel_id=1, source_target_pairs={{0,2},{2,0},{1,3},{3,1},{4,6},{6,4},{5,7},{7,5},{8,10},{10,8},{9,1... | collective-permute-start | bytes 491528 | tf_op jit(solution)/shard_map/ppermute | solution.py:152
  14.9 0.0 copy-start.1
  15.0 0.9 copy-done.1
  15.9 0.7 shard_map.64.held
  16.6 0.0 copy-done
  16.6 2.9 %fusion.5 = bf16[320,1024]{1,0:T(8,128)(2,1)} fusion(bf16[320,256]{1,0:T(8,128)(2,1)} %bitcast.27, bf16[1,1024,1024]{2,1,0:T(8,128)(2,1)S(1)} %copy-done, bf16[1,256,1024]{2,1,0:T(8,128)(2,1)} %param.7), kind=kOutput, calls=%fused_computation.5 | convolution fusion | flops 705232896 | bytes 3440640 | tf_op jit(solution)/shard_map/dot_general | solution.py:27
  19.6 2.1 %collective-permute-done.part = bf16[80,1024]{1,0:T(8,128)(2,1)S(1)} collective-permute-done((bf16[80,1024]{1,0:T(8,128)(2,1)}, bf16[80,1024]{1,0:T(8,128)(2,1)S(1)}, u32[]{:S(2)}, u32[]{:S(2)}) %collective-permute-start) | collective-permute-done | bytes 163872 | tf_op jit(solution)/shard_map/ppermute | solution.py:152
  21.7 0.7 shard_map.65
  22.4 0.0 all-gather.2.cloned.1.call-update
  22.4 3.5 %all-to-all-start = ((bf16[4,80,1024]{2,1,0:T(8,128)(2,1)}), bf16[4,80,1024]{2,1,0:T(8,128)(2,1)S(1)}, u32[]{:S(2)}, u32[]{:S(2)}) async-start(bf16[4,80,1024]{2,1,0:T(8,128)(2,1)} %bitcast.11), calls=%async_computation | async-start | bytes 1310720 | tf_op jit(solution)/shard_map/all_to_all | solution.py:160
  25.9 0.8 convert_bitcast_fusion
  26.7 12.1 %all-to-all-done = bf16[4,80,1024]{2,1,0:T(8,128)(2,1)S(1)} async-done(((bf16[4,80,1024]{2,1,0:T(8,128)(2,1)}), bf16[4,80,1024]{2,1,0:T(8,128)(2,1)S(1)}, u32[]{:S(2)}, u32[]{:S(2)}) %all-to-all-start) | async-done | bytes 655392 | tf_op jit(solution)/shard_map/all_to_all | solution.py:160
  38.8 0.1 convert_reduce_fusion
  38.9 0.1 multiply_convert_fusion
  39.0 0.9 broadcast_in_dim.10
  39.9 5.0 %all-to-all-start.1 = ((bf16[4,80,1024]{2,1,0:T(8,128)(2,1)}), bf16[4,80,1024]{2,1,0:T(8,128)(2,1)S(1)}, u32[]{:S(2)}, u32[]{:S(2)}) async-start(bf16[4,80,1024]{2,1,0:T(8,128)(2,1)} %broadcast_in_dim.10), calls=%async_computation.1 | async-start | bytes 1310720 | tf_op jit(solution)/shard_map/all_to_all | solution.py:32
  45.0 0.1 and_select_fusion
  45.0 0.1 pad_add_fusion.place
  45.1 0.7 dynamic-slice_convert_fusion.mask
  45.8 12.8 %all-to-all-done.1.lower = bf16[4,80,1024]{2,1,0:T(8,128)(2,1)S(1)} async-done(((bf16[4,80,1024]{2,1,0:T(8,128)(2,1)}), bf16[4,80,1024]{2,1,0:T(8,128)(2,1)S(1)}, u32[]{:S(2)}, u32[]{:S(2)}) %all-to-all-start.1) | async-done | bytes 655392 | tf_op jit(solution)/shard_map/all_to_all | solution.py:32
  58.7 17.0 %all-gather.2.cloned.1.call-done.refs_0_.refs_1_.refs_2_.refs_3_ = bf16[2560,1024]{1,0:T(8,128)(2,1)} async-done(((bf16[160,1024]{1,0:T(8,128)(2,1)}), bf16[2560,1024]{1,0:T(8,128)(2,1)}) %all-gather.2.cloned.1.call-update) | async-done | bytes 5242896 | tf_op jit(solution)/shard_map/all_gather | solution.py:159
  75.7 4.3 %shard_map.66 = (bf16[80,1280]{1,0:T(8,128)(2,1)S(1)}, bf16[80,1280]{1,0:T(8,128)(2,1)S(1)}, bf16[80,1280]{1,0:T(8,128)(2,1)S(1)}, bf16[80,1280]{1,0:T(8,128)(2,1)S(1)}, bf16[80,2560]{1,0:T(8,128)(2,1)S(1)}) custom-call(s32[5]{0:T(128)S(1)} %pad_add_fusion.place, f32[1,2560]{1,0:T(1,128)S(1)} %dynamic-slice_convert_fusion.mask, ...), custom_call_target="tpu_custom_call" | custom-call | tf_op jit(solution)/shard_map/pallas_call | solution.py:121
  80.0 4.3 %collective-permute-start.1 = (bf16[80,1280]{1,0:T(8,128)(2,1)S(1)}, bf16[80,1280]{1,0:T(8,128)(2,1)S(1)}, u32[]{:S(2)}, u32[]{:S(2)}) collective-permute-start(bf16[80,1280]{1,0:T(8,128)(2,1)S(1)} %get-tuple-element.19), channel_id=1, source_target_pairs={{0,128},{1,385},{128,256},{129,1},{256,384},{257,129},{384,0},{385... | collective-permute-start | bytes 614408 | tf_op jit(solution)/shard_map/ppermute | solution.py:176
  84.3 2.3 %collective-permute-start.3 = (bf16[80,1280]{1,0:T(8,128)(2,1)S(1)}, bf16[80,1280]{1,0:T(8,128)(2,1)S(1)}, u32[]{:S(2)}, u32[]{:S(2)}) collective-permute-start(bf16[80,1280]{1,0:T(8,128)(2,1)S(1)} %get-tuple-element.23), channel_id=1, source_target_pairs={{0,128},{1,385},{128,256},{129,1},{256,384},{257,129},{384,0},{385... | collective-permute-start | bytes 614408 | tf_op jit(solution)/shard_map/ppermute | solution.py:176
  86.6 3.0 %collective-permute-start.2 = (bf16[80,2560]{1,0:T(8,128)(2,1)S(1)}, bf16[80,2560]{1,0:T(8,128)(2,1)S(1)}, u32[]{:S(2)}, u32[]{:S(2)}) collective-permute-start(bf16[80,2560]{1,0:T(8,128)(2,1)S(1)} %get-tuple-element.21), channel_id=1, source_target_pairs={{0,384},{1,129},{128,0},{129,257},{256,128},{257,385},{384,256},{3... | collective-permute-start | bytes 1228808 | tf_op jit(solution)/shard_map/ppermute | solution.py:177
  89.6 0.0 collective-permute-done.1
  89.6 0.1 add_convert_fusion.1
  89.7 3.5 %collective-permute-start.5 = (bf16[80,1280]{1,0:T(8,128)(2,1)S(1)}, bf16[80,1280]{1,0:T(8,128)(2,1)S(1)}, u32[]{:S(2)}, u32[]{:S(2)}) collective-permute-start(bf16[80,1280]{1,0:T(8,128)(2,1)S(1)} %add_convert_fusion.1), channel_id=1, source_target_pairs={{0,128},{1,385},{128,256},{129,1},{256,384},{257,129},{384,0},{385... | collective-permute-start | bytes 614408 | tf_op jit(solution)/shard_map/ppermute | solution.py:184
  93.2 0.0 collective-permute-done.3
  93.2 0.1 add_convert_fusion
  93.2 0.0 copy-start.2
  93.2 2.1 %collective-permute-start.4 = (bf16[80,1280]{1,0:T(8,128)(2,1)S(1)}, bf16[80,1280]{1,0:T(8,128)(2,1)S(1)}, u32[]{:S(2)}, u32[]{:S(2)}) collective-permute-start(bf16[80,1280]{1,0:T(8,128)(2,1)S(1)} %add_convert_fusion), channel_id=1, source_target_pairs={{0,128},{1,385},{128,256},{129,1},{256,384},{257,129},{384,0},{385... | collective-permute-start | bytes 614408 | tf_op jit(solution)/shard_map/ppermute | solution.py:184
  95.3 3.9 %shard_map.67 = bf16[80,2560]{1,0:T(8,128)(2,1)S(1)} custom-call(s32[5]{0:T(128)S(1)} %pad_add_fusion.place, f32[1,2560]{1,0:T(1,128)S(1)} %dynamic-slice_convert_fusion.mask, bf16[4,80,1024]{2,1,0:T(8,128)(2,1)S(1)} %all-to-all-done.1.lower, bf16[2560,1024]{1,0:T(8,128)(2,1)} %all-gather.2.cloned.1.call-done.refs_0_.refs_1_.refs_2_.refs_3_, ...), custom_call_target="tpu_custom_call" | custom-call | tf_op jit(solution)/shard_map/pallas_call | solution.py:121
  99.2 0.0 collective-permute-done.2
  99.3 0.0 copy-done.2
  99.3 0.1 add_subtract_fusion
  99.4 0.0 collective-permute-done.5
  99.4 1.2 %collective-permute-done.4 = bf16[80,1280]{1,0:T(8,128)(2,1)S(1)} collective-permute-done((bf16[80,1280]{1,0:T(8,128)(2,1)S(1)}, bf16[80,1280]{1,0:T(8,128)(2,1)S(1)}, u32[]{:S(2)}, u32[]{:S(2)}) %collective-permute-start.4) | collective-permute-done | bytes 204832 | tf_op jit(solution)/shard_map/ppermute | solution.py:184
  100.6 0.1 fusion.11
  100.7 0.8 pad_maximum_fusion
Async XLA Ops:
  6.5 10.1 %copy-start = (bf16[1,1024,1024]{2,1,0:T(8,128)(2,1)S(1)}, bf16[1,1024,1024]{2,1,0:T(8,128)(2,1)}, u32[]{:S(2)}) copy-start(bf16[1,1024,1024]{2,1,0:T(8,128)(2,1)} %param.9) | copy-start | bytes 6291460
  6.5 69.2 %all-gather.2.cloned.1.call-start = ((), (), s32[]{:S(2)}) async-start(), calls=%async_computation.2 | async-start | bytes 5570560 | tf_op jit(solution)/shard_map/all_gather | solution.py:159
  6.5 15.1 %collective-permute-start = (bf16[80,1024]{1,0:T(8,128)(2,1)}, bf16[80,1024]{1,0:T(8,128)(2,1)S(1)}, u32[]{:S(2)}, u32[]{:S(2)}) collective-permute-start(bf16[80,1024]{1,0:T(8,128)(2,1)} %bitcast.25), channel_id=1, source_target_pairs={{0,2},{2,0},{1,3},{3,1},{4,6},{6,4},{5,7},{7,5},{8,10},{10,8},{9,1... | collective-permute-start | bytes 491528 | tf_op jit(solution)/shard_map/ppermute | solution.py:152
  14.9 0.9 copy-start.1
  22.4 16.4 %all-to-all-start = ((bf16[4,80,1024]{2,1,0:T(8,128)(2,1)}), bf16[4,80,1024]{2,1,0:T(8,128)(2,1)S(1)}, u32[]{:S(2)}, u32[]{:S(2)}) async-start(bf16[4,80,1024]{2,1,0:T(8,128)(2,1)} %bitcast.11), calls=%async_computation | async-start | bytes 1310720 | tf_op jit(solution)/shard_map/all_to_all | solution.py:160
  39.9 18.7 %all-to-all-start.1 = ((bf16[4,80,1024]{2,1,0:T(8,128)(2,1)}), bf16[4,80,1024]{2,1,0:T(8,128)(2,1)S(1)}, u32[]{:S(2)}, u32[]{:S(2)}) async-start(bf16[4,80,1024]{2,1,0:T(8,128)(2,1)} %broadcast_in_dim.10), calls=%async_computation.1 | async-start | bytes 1310720 | tf_op jit(solution)/shard_map/all_to_all | solution.py:32
  80.0 9.6 %collective-permute-start.1 = (bf16[80,1280]{1,0:T(8,128)(2,1)S(1)}, bf16[80,1280]{1,0:T(8,128)(2,1)S(1)}, u32[]{:S(2)}, u32[]{:S(2)}) collective-permute-start(bf16[80,1280]{1,0:T(8,128)(2,1)S(1)} %get-tuple-element.19), channel_id=1, source_target_pairs={{0,128},{1,385},{128,256},{129,1},{256,384},{257,129},{384,0},{385... | collective-permute-start | bytes 614408 | tf_op jit(solution)/shard_map/ppermute | solution.py:176
  84.3 8.8 %collective-permute-start.3 = (bf16[80,1280]{1,0:T(8,128)(2,1)S(1)}, bf16[80,1280]{1,0:T(8,128)(2,1)S(1)}, u32[]{:S(2)}, u32[]{:S(2)}) collective-permute-start(bf16[80,1280]{1,0:T(8,128)(2,1)S(1)} %get-tuple-element.23), channel_id=1, source_target_pairs={{0,128},{1,385},{128,256},{129,1},{256,384},{257,129},{384,0},{385... | collective-permute-start | bytes 614408 | tf_op jit(solution)/shard_map/ppermute | solution.py:176
  86.6 12.7 %collective-permute-start.2 = (bf16[80,2560]{1,0:T(8,128)(2,1)S(1)}, bf16[80,2560]{1,0:T(8,128)(2,1)S(1)}, u32[]{:S(2)}, u32[]{:S(2)}) collective-permute-start(bf16[80,2560]{1,0:T(8,128)(2,1)S(1)} %get-tuple-element.21), channel_id=1, source_target_pairs={{0,384},{1,129},{128,0},{129,257},{256,128},{257,385},{384,256},{3... | collective-permute-start | bytes 1228808 | tf_op jit(solution)/shard_map/ppermute | solution.py:177
  89.7 9.7 %collective-permute-start.5 = (bf16[80,1280]{1,0:T(8,128)(2,1)S(1)}, bf16[80,1280]{1,0:T(8,128)(2,1)S(1)}, u32[]{:S(2)}, u32[]{:S(2)}) collective-permute-start(bf16[80,1280]{1,0:T(8,128)(2,1)S(1)} %add_convert_fusion.1), channel_id=1, source_target_pairs={{0,128},{1,385},{128,256},{129,1},{256,384},{257,129},{384,0},{385... | collective-permute-start | bytes 614408 | tf_op jit(solution)/shard_map/ppermute | solution.py:184
  93.2 6.0 %copy-start.2 = (bf16[80,2560]{1,0:T(8,128)(2,1)S(1)}, bf16[80,2560]{1,0:T(8,128)(2,1)}, u32[]{:S(2)}) copy-start(bf16[80,2560]{1,0:T(8,128)(2,1)} %param.11) | copy-start | bytes 1228804
  93.2 7.4 %collective-permute-start.4 = (bf16[80,1280]{1,0:T(8,128)(2,1)S(1)}, bf16[80,1280]{1,0:T(8,128)(2,1)S(1)}, u32[]{:S(2)}, u32[]{:S(2)}) collective-permute-start(bf16[80,1280]{1,0:T(8,128)(2,1)S(1)} %add_convert_fusion), channel_id=1, source_target_pairs={{0,128},{1,385},{128,256},{129,1},{256,384},{257,129},{384,0},{385... | collective-permute-start | bytes 614408 | tf_op jit(solution)/shard_map/ppermute | solution.py:184
Sparse Core Ops, SparseCore 0:
  22.5 53.1 all-gather.1

commit v9 on v8

--- a/solution.py
+++ b/solution.py
@@ -11,7 +11,7 @@
 AXES = ("layer", "row", "deep", "half", "core")
 SWAP = [(0, 1), (1, 0)]
 PIECES = 2
-SHARES = 4
+SHARES = 2
 MULTIPLY_VMEM = 48 << 20
 
 

time: 109 us -> 109 us (level)
  no operation moved by 1% of the time
where the time goes in v9:
time: 109 us; the launch traced here: 108 us
  waiting for transfers between devices  45.4 us (42%)
  starting transfers between devices  32 us (29%)
  between operations  13.6 us (12%)
  Pallas kernels  9.64 us (9%)
  matrix products  2.93 us (3%)
  other arithmetic  2.92 us (3%)
  local copies, waits for them, and re-layouts  1.87 us (2%)
    all_gather x1, waiting for transfers between devices, shards(): upper = lax.all_gather(both, ('deep', 'core'), axis=0, tiled=True)  17 us
    all_to_all x1, waiting for transfers between devices, spread(): return lax.all_to_all(copies, axis, 0, 0, tiled=True)  12.8 us
    all_to_all x1, waiting for transfers between devices, shards(): lax.all_to_all(partial_value.reshape(groups, slab_rows, width), 'row', 0,...  12.1 us
    ppermute x4, starting transfers between devices, shards(): lax.ppermute(part, ('layer', 'core'), layer_pairs(1))  12.1 us
    ppermute x1, starting transfers between devices, shards(): other = lax.ppermute(coupling_t, 'half', SWAP)  8.4 us
    pallas_call x2, Pallas kernels, multiply(): pl.pallas_call(functools.partial(multiply_kernel, 3 if kept else 0), grid...  8.22 us
    all_to_all x1, starting transfers between devices, spread(): return lax.all_to_all(copies, axis, 0, 0, tiled=True)  5.03 us
    all_to_all x1, starting transfers between devices, shards(): lax.all_to_all(partial_value.reshape(groups, slab_rows, width), 'row', 0,...  3.49 us
  transfers between devices with their start and end apart: 9, of which 5 were waited for; matrix products, arithmetic and copies ran while one was open for 5% of the time, Pallas kernels for 4%

profile of v9, /device:TPU:1, one launch (start us, length us, event | category | flops | bytes accessed | tf_op | source)
XLA Modules:
  0.0 108.3 jit_solution(7677650662129943105)
XLA Ops:
  6.5 0.0 copy-start
  6.5 0.0 all-gather.2.cloned.1.call-start
  6.5 8.4 %collective-permute-start = (bf16[80,1024]{1,0:T(8,128)(2,1)}, bf16[80,1024]{1,0:T(8,128)(2,1)S(1)}, u32[]{:S(2)}, u32[]{:S(2)}) collective-permute-start(bf16[80,1024]{1,0:T(8,128)(2,1)} %bitcast.25), channel_id=1, source_target_pairs={{0,2},{2,0},{1,3},{3,1},{4,6},{6,4},{5,7},{7,5},{8,10},{10,8},{9,1... | collective-permute-start | bytes 491528 | tf_op jit(solution)/shard_map/ppermute | solution.py:152
  14.9 0.0 copy-start.1
  15.0 0.9 copy-done.1
  15.9 0.7 shard_map.64.held
  16.6 0.0 copy-done
  16.6 2.9 %fusion.5 = bf16[320,1024]{1,0:T(8,128)(2,1)} fusion(bf16[320,256]{1,0:T(8,128)(2,1)} %bitcast.27, bf16[1,1024,1024]{2,1,0:T(8,128)(2,1)S(1)} %copy-done, bf16[1,256,1024]{2,1,0:T(8,128)(2,1)} %param.7), kind=kOutput, calls=%fused_computation.5 | convolution fusion | flops 705232896 | bytes 3440640 | tf_op jit(solution)/shard_map/dot_general | solution.py:27
  19.6 2.1 %collective-permute-done.part = bf16[80,1024]{1,0:T(8,128)(2,1)S(1)} collective-permute-done((bf16[80,1024]{1,0:T(8,128)(2,1)}, bf16[80,1024]{1,0:T(8,128)(2,1)S(1)}, u32[]{:S(2)}, u32[]{:S(2)}) %collective-permute-start) | collective-permute-done | bytes 163872 | tf_op jit(solution)/shard_map/ppermute | solution.py:152
  21.7 0.7 shard_map.65
  22.4 0.0 all-gather.2.cloned.1.call-update
  22.4 3.5 %all-to-all-start = ((bf16[4,80,1024]{2,1,0:T(8,128)(2,1)}), bf16[4,80,1024]{2,1,0:T(8,128)(2,1)S(1)}, u32[]{:S(2)}, u32[]{:S(2)}) async-start(bf16[4,80,1024]{2,1,0:T(8,128)(2,1)} %bitcast.11), calls=%async_computation | async-start | bytes 1310720 | tf_op jit(solution)/shard_map/all_to_all | solution.py:160
  25.9 0.8 convert_bitcast_fusion
  26.7 12.1 %all-to-all-done = bf16[4,80,1024]{2,1,0:T(8,128)(2,1)S(1)} async-done(((bf16[4,80,1024]{2,1,0:T(8,128)(2,1)}), bf16[4,80,1024]{2,1,0:T(8,128)(2,1)S(1)}, u32[]{:S(2)}, u32[]{:S(2)}) %all-to-all-start) | async-done | bytes 655392 | tf_op jit(solution)/shard_map/all_to_all | solution.py:160
  38.8 0.1 convert_reduce_fusion
  38.9 0.1 multiply_convert_fusion
  39.0 0.9 broadcast_in_dim.10
  39.9 5.0 %all-to-all-start.1 = ((bf16[4,80,1024]{2,1,0:T(8,128)(2,1)}), bf16[4,80,1024]{2,1,0:T(8,128)(2,1)S(1)}, u32[]{:S(2)}, u32[]{:S(2)}) async-start(bf16[4,80,1024]{2,1,0:T(8,128)(2,1)} %broadcast_in_dim.10), calls=%async_computation.1 | async-start | bytes 1310720 | tf_op jit(solution)/shard_map/all_to_all | solution.py:32
  45.0 0.1 and_select_fusion
  45.0 0.1 pad_add_fusion.place
  45.1 0.7 dynamic-slice_convert_fusion.mask
  45.8 12.8 %all-to-all-done.1.lower = bf16[4,80,1024]{2,1,0:T(8,128)(2,1)S(1)} async-done(((bf16[4,80,1024]{2,1,0:T(8,128)(2,1)}), bf16[4,80,1024]{2,1,0:T(8,128)(2,1)S(1)}, u32[]{:S(2)}, u32[]{:S(2)}) %all-to-all-start.1) | async-done | bytes 655392 | tf_op jit(solution)/shard_map/all_to_all | solution.py:32
  58.7 17.0 %all-gather.2.cloned.1.call-done.refs_0_.refs_1_ = bf16[2560,1024]{1,0:T(8,128)(2,1)} async-done(((bf16[160,1024]{1,0:T(8,128)(2,1)}), bf16[2560,1024]{1,0:T(8,128)(2,1)}) %all-gather.2.cloned.1.call-update) | async-done | bytes 5242896 | tf_op jit(solution)/shard_map/all_gather | solution.py:159
  75.7 4.3 %shard_map.66 = (bf16[80,1280]{1,0:T(8,128)(2,1)S(1)}, bf16[80,1280]{1,0:T(8,128)(2,1)S(1)}, bf16[80,1280]{1,0:T(8,128)(2,1)S(1)}, bf16[80,1280]{1,0:T(8,128)(2,1)S(1)}, bf16[80,2560]{1,0:T(8,128)(2,1)S(1)}) custom-call(s32[5]{0:T(128)S(1)} %pad_add_fusion.place, f32[1,2560]{1,0:T(1,128)S(1)} %dynamic-slice_convert_fusion.mask, ...), custom_call_target="tpu_custom_call" | custom-call | tf_op jit(solution)/shard_map/pallas_call | solution.py:121
  80.0 4.3 %collective-permute-start.1 = (bf16[80,1280]{1,0:T(8,128)(2,1)S(1)}, bf16[80,1280]{1,0:T(8,128)(2,1)S(1)}, u32[]{:S(2)}, u32[]{:S(2)}) collective-permute-start(bf16[80,1280]{1,0:T(8,128)(2,1)S(1)} %get-tuple-element.19), channel_id=1, source_target_pairs={{0,128},{1,385},{128,256},{129,1},{256,384},{257,129},{384,0},{385... | collective-permute-start | bytes 614408 | tf_op jit(solution)/shard_map/ppermute | solution.py:176
  84.3 2.3 %collective-permute-start.3 = (bf16[80,1280]{1,0:T(8,128)(2,1)S(1)}, bf16[80,1280]{1,0:T(8,128)(2,1)S(1)}, u32[]{:S(2)}, u32[]{:S(2)}) collective-permute-start(bf16[80,1280]{1,0:T(8,128)(2,1)S(1)} %get-tuple-element.23), channel_id=1, source_target_pairs={{0,128},{1,385},{128,256},{129,1},{256,384},{257,129},{384,0},{385... | collective-permute-start | bytes 614408 | tf_op jit(solution)/shard_map/ppermute | solution.py:176
  86.6 3.0 %collective-permute-start.2 = (bf16[80,2560]{1,0:T(8,128)(2,1)S(1)}, bf16[80,2560]{1,0:T(8,128)(2,1)S(1)}, u32[]{:S(2)}, u32[]{:S(2)}) collective-permute-start(bf16[80,2560]{1,0:T(8,128)(2,1)S(1)} %get-tuple-element.21), channel_id=1, source_target_pairs={{0,384},{1,129},{128,0},{129,257},{256,128},{257,385},{384,256},{3... | collective-permute-start | bytes 1228808 | tf_op jit(solution)/shard_map/ppermute | solution.py:177
  89.6 0.0 collective-permute-done.1
  89.6 0.1 add_convert_fusion.1
  89.7 3.5 %collective-permute-start.5 = (bf16[80,1280]{1,0:T(8,128)(2,1)S(1)}, bf16[80,1280]{1,0:T(8,128)(2,1)S(1)}, u32[]{:S(2)}, u32[]{:S(2)}) collective-permute-start(bf16[80,1280]{1,0:T(8,128)(2,1)S(1)} %add_convert_fusion.1), channel_id=1, source_target_pairs={{0,128},{1,385},{128,256},{129,1},{256,384},{257,129},{384,0},{385... | collective-permute-start | bytes 614408 | tf_op jit(solution)/shard_map/ppermute | solution.py:184
  93.2 0.0 collective-permute-done.3
  93.2 0.1 add_convert_fusion
  93.2 0.0 copy-start.2
  93.2 2.1 %collective-permute-start.4 = (bf16[80,1280]{1,0:T(8,128)(2,1)S(1)}, bf16[80,1280]{1,0:T(8,128)(2,1)S(1)}, u32[]{:S(2)}, u32[]{:S(2)}) collective-permute-start(bf16[80,1280]{1,0:T(8,128)(2,1)S(1)} %add_convert_fusion), channel_id=1, source_target_pairs={{0,128},{1,385},{128,256},{129,1},{256,384},{257,129},{384,0},{385... | collective-permute-start | bytes 614408 | tf_op jit(solution)/shard_map/ppermute | solution.py:184
  95.3 3.9 %shard_map.67 = bf16[80,2560]{1,0:T(8,128)(2,1)S(1)} custom-call(s32[5]{0:T(128)S(1)} %pad_add_fusion.place, f32[1,2560]{1,0:T(1,128)S(1)} %dynamic-slice_convert_fusion.mask, bf16[4,80,1024]{2,1,0:T(8,128)(2,1)S(1)} %all-to-all-done.1.lower, bf16[2560,1024]{1,0:T(8,128)(2,1)} %all-gather.2.cloned.1.call-done.refs_0_.refs_1_, ...), custom_call_target="tpu_custom_call" | custom-call | tf_op jit(solution)/shard_map/pallas_call | solution.py:121
  99.2 0.0 collective-permute-done.2
  99.2 0.0 copy-done.2
  99.2 0.1 add_subtract_fusion
  99.4 0.0 collective-permute-done.5
  99.4 1.2 %collective-permute-done.4 = bf16[80,1280]{1,0:T(8,128)(2,1)S(1)} collective-permute-done((bf16[80,1280]{1,0:T(8,128)(2,1)S(1)}, bf16[80,1280]{1,0:T(8,128)(2,1)S(1)}, u32[]{:S(2)}, u32[]{:S(2)}) %collective-permute-start.4) | collective-permute-done | bytes 204832 | tf_op jit(solution)/shard_map/ppermute | solution.py:184
  100.6 0.1 fusion.11
  100.7 0.8 pad_maximum_fusion
Async XLA Ops:
  6.5 10.1 %copy-start = (bf16[1,1024,1024]{2,1,0:T(8,128)(2,1)S(1)}, bf16[1,1024,1024]{2,1,0:T(8,128)(2,1)}, u32[]{:S(2)}) copy-start(bf16[1,1024,1024]{2,1,0:T(8,128)(2,1)} %param.9) | copy-start | bytes 6291460
  6.5 69.2 %all-gather.2.cloned.1.call-start = ((), (), s32[]{:S(2)}) async-start(), calls=%async_computation.2 | async-start | bytes 5570560 | tf_op jit(solution)/shard_map/all_gather | solution.py:159
  6.5 15.1 %collective-permute-start = (bf16[80,1024]{1,0:T(8,128)(2,1)}, bf16[80,1024]{1,0:T(8,128)(2,1)S(1)}, u32[]{:S(2)}, u32[]{:S(2)}) collective-permute-start(bf16[80,1024]{1,0:T(8,128)(2,1)} %bitcast.25), channel_id=1, source_target_pairs={{0,2},{2,0},{1,3},{3,1},{4,6},{6,4},{5,7},{7,5},{8,10},{10,8},{9,1... | collective-permute-start | bytes 491528 | tf_op jit(solution)/shard_map/ppermute | solution.py:152
  14.9 0.9 copy-start.1
  22.4 16.4 %all-to-all-start = ((bf16[4,80,1024]{2,1,0:T(8,128)(2,1)}), bf16[4,80,1024]{2,1,0:T(8,128)(2,1)S(1)}, u32[]{:S(2)}, u32[]{:S(2)}) async-start(bf16[4,80,1024]{2,1,0:T(8,128)(2,1)} %bitcast.11), calls=%async_computation | async-start | bytes 1310720 | tf_op jit(solution)/shard_map/all_to_all | solution.py:160
  39.9 18.7 %all-to-all-start.1 = ((bf16[4,80,1024]{2,1,0:T(8,128)(2,1)}), bf16[4,80,1024]{2,1,0:T(8,128)(2,1)S(1)}, u32[]{:S(2)}, u32[]{:S(2)}) async-start(bf16[4,80,1024]{2,1,0:T(8,128)(2,1)} %broadcast_in_dim.10), calls=%async_computation.1 | async-start | bytes 1310720 | tf_op jit(solution)/shard_map/all_to_all | solution.py:32
  80.0 9.6 %collective-permute-start.1 = (bf16[80,1280]{1,0:T(8,128)(2,1)S(1)}, bf16[80,1280]{1,0:T(8,128)(2,1)S(1)}, u32[]{:S(2)}, u32[]{:S(2)}) collective-permute-start(bf16[80,1280]{1,0:T(8,128)(2,1)S(1)} %get-tuple-element.19), channel_id=1, source_target_pairs={{0,128},{1,385},{128,256},{129,1},{256,384},{257,129},{384,0},{385... | collective-permute-start | bytes 614408 | tf_op jit(solution)/shard_map/ppermute | solution.py:176
  84.3 8.8 %collective-permute-start.3 = (bf16[80,1280]{1,0:T(8,128)(2,1)S(1)}, bf16[80,1280]{1,0:T(8,128)(2,1)S(1)}, u32[]{:S(2)}, u32[]{:S(2)}) collective-permute-start(bf16[80,1280]{1,0:T(8,128)(2,1)S(1)} %get-tuple-element.23), channel_id=1, source_target_pairs={{0,128},{1,385},{128,256},{129,1},{256,384},{257,129},{384,0},{385... | collective-permute-start | bytes 614408 | tf_op jit(solution)/shard_map/ppermute | solution.py:176
  86.6 12.6 %collective-permute-start.2 = (bf16[80,2560]{1,0:T(8,128)(2,1)S(1)}, bf16[80,2560]{1,0:T(8,128)(2,1)S(1)}, u32[]{:S(2)}, u32[]{:S(2)}) collective-permute-start(bf16[80,2560]{1,0:T(8,128)(2,1)S(1)} %get-tuple-element.21), channel_id=1, source_target_pairs={{0,384},{1,129},{128,0},{129,257},{256,128},{257,385},{384,256},{3... | collective-permute-start | bytes 1228808 | tf_op jit(solution)/shard_map/ppermute | solution.py:177
  89.7 9.7 %collective-permute-start.5 = (bf16[80,1280]{1,0:T(8,128)(2,1)S(1)}, bf16[80,1280]{1,0:T(8,128)(2,1)S(1)}, u32[]{:S(2)}, u32[]{:S(2)}) collective-permute-start(bf16[80,1280]{1,0:T(8,128)(2,1)S(1)} %add_convert_fusion.1), channel_id=1, source_target_pairs={{0,128},{1,385},{128,256},{129,1},{256,384},{257,129},{384,0},{385... | collective-permute-start | bytes 614408 | tf_op jit(solution)/shard_map/ppermute | solution.py:184
  93.2 6.0 %copy-start.2 = (bf16[80,2560]{1,0:T(8,128)(2,1)S(1)}, bf16[80,2560]{1,0:T(8,128)(2,1)}, u32[]{:S(2)}) copy-start(bf16[80,2560]{1,0:T(8,128)(2,1)} %param.11) | copy-start | bytes 1228804
  93.2 7.4 %collective-permute-start.4 = (bf16[80,1280]{1,0:T(8,128)(2,1)S(1)}, bf16[80,1280]{1,0:T(8,128)(2,1)S(1)}, u32[]{:S(2)}, u32[]{:S(2)}) collective-permute-start(bf16[80,1280]{1,0:T(8,128)(2,1)S(1)} %add_convert_fusion), channel_id=1, source_target_pairs={{0,128},{1,385},{128,256},{129,1},{256,384},{257,129},{384,0},{385... | collective-permute-start | bytes 614408 | tf_op jit(solution)/shard_map/ppermute | solution.py:184
Sparse Core Ops, SparseCore 0:
  22.5 53.1 all-gather.1

commit v10 on v9

--- a/solution.py
+++ b/solution.py
@@ -85,7 +85,7 @@
         to = (4 * z + core) * strip + jnp.where(half == k, 0, 2 * strip)
         block = uppers[n // share][n % share * strip : (n % share + 1) * strip, :]
         panel[pl.ds(pl.multiple_of(to, 16), strip), :] = block
-    value = (dot(rows[...], panel[...], ((1,), (1,))) * mask[...]).astype(jnp.bfloat16)
+    value = dot(rows[...], panel[...], ((1,), (1,))).astype(jnp.bfloat16) * mask[...]
     if first:
         outs[0][...] = value
         return
@@ -167,7 +167,7 @@
     mask = lax.dynamic_slice_in_dim(
         row_pattern[0], row_index * (groups * 8 * slab_rows), groups * 8 * slab_rows, 0
     )
-    mask = mask.reshape(1, -1).astype(jnp.float32)
+    mask = mask.reshape(1, -1).astype(jnp.bfloat16)
 
     onward = jnp.where(core_index == 0, 1, 3)
     targets = (layer_index + jnp.stack([2 * onward, 3 * onward, onward, 0 * onward])) % groups

time: 109 us -> 109 us (level)
  no operation moved by 1% of the time
where the time goes in v10:
time: 109 us; the launch traced here: 108 us
  waiting for transfers between devices  45.4 us (42%)
  starting transfers between devices  32 us (29%)
  between operations  13.6 us (12%)
  Pallas kernels  9.68 us (9%)
  matrix products  2.93 us (3%)
  other arithmetic  2.92 us (3%)
  local copies, waits for them, and re-layouts  1.87 us (2%)
    all_gather x1, waiting for transfers between devices, shards(): upper = lax.all_gather(both, ('deep', 'core'), axis=0, tiled=True)  17 us
    all_to_all x1, waiting for transfers between devices, spread(): return lax.all_to_all(copies, axis, 0, 0, tiled=True)  12.8 us
    all_to_all x1, waiting for transfers between devices, shards(): lax.all_to_all(partial_value.reshape(groups, slab_rows, width), 'row', 0,...  12.1 us
    ppermute x4, starting transfers between devices, shards(): lax.ppermute(part, ('layer', 'core'), layer_pairs(1))  12.1 us
    ppermute x1, starting transfers between devices, shards(): other = lax.ppermute(coupling_t, 'half', SWAP)  8.4 us
    pallas_call x2, Pallas kernels, multiply(): pl.pallas_call(functools.partial(multiply_kernel, 3 if kept else 0), grid...  8.26 us
    all_to_all x1, starting transfers between devices, spread(): return lax.all_to_all(copies, axis, 0, 0, tiled=True)  5.03 us
    all_to_all x1, starting transfers between devices, shards(): lax.all_to_all(partial_value.reshape(groups, slab_rows, width), 'row', 0,...  3.49 us
  transfers between devices with their start and end apart: 9, of which 5 were waited for; matrix products, arithmetic and copies ran while one was open for 5% of the time, Pallas kernels for 4%

profile of v10, /device:TPU:1, one launch (start us, length us, event | category | flops | bytes accessed | tf_op | source)
XLA Modules:
  0.0 108.3 jit_solution(8137886610352621559)
XLA Ops:
  6.5 0.0 copy-start
  6.5 0.0 all-gather.2.cloned.1.call-start
  6.5 8.4 %collective-permute-start = (bf16[80,1024]{1,0:T(8,128)(2,1)}, bf16[80,1024]{1,0:T(8,128)(2,1)S(1)}, u32[]{:S(2)}, u32[]{:S(2)}) collective-permute-start(bf16[80,1024]{1,0:T(8,128)(2,1)} %bitcast.25), channel_id=1, source_target_pairs={{0,2},{2,0},{1,3},{3,1},{4,6},{6,4},{5,7},{7,5},{8,10},{10,8},{9,1... | collective-permute-start | bytes 491528 | tf_op jit(solution)/shard_map/ppermute | solution.py:152
  14.9 0.0 copy-start.1
  15.0 0.9 copy-done.1
  15.9 0.7 shard_map.64.held
  16.6 0.0 copy-done
  16.6 2.9 %fusion.5 = bf16[320,1024]{1,0:T(8,128)(2,1)} fusion(bf16[320,256]{1,0:T(8,128)(2,1)} %bitcast.27, bf16[1,1024,1024]{2,1,0:T(8,128)(2,1)S(1)} %copy-done, bf16[1,256,1024]{2,1,0:T(8,128)(2,1)} %param.7), kind=kOutput, calls=%fused_computation.5 | convolution fusion | flops 705232896 | bytes 3440640 | tf_op jit(solution)/shard_map/dot_general | solution.py:27
  19.6 2.1 %collective-permute-done.part = bf16[80,1024]{1,0:T(8,128)(2,1)S(1)} collective-permute-done((bf16[80,1024]{1,0:T(8,128)(2,1)}, bf16[80,1024]{1,0:T(8,128)(2,1)S(1)}, u32[]{:S(2)}, u32[]{:S(2)}) %collective-permute-start) | collective-permute-done | bytes 163872 | tf_op jit(solution)/shard_map/ppermute | solution.py:152
  21.7 0.7 shard_map.65
  22.4 0.0 all-gather.2.cloned.1.call-update
  22.4 3.5 %all-to-all-start = ((bf16[4,80,1024]{2,1,0:T(8,128)(2,1)}), bf16[4,80,1024]{2,1,0:T(8,128)(2,1)S(1)}, u32[]{:S(2)}, u32[]{:S(2)}) async-start(bf16[4,80,1024]{2,1,0:T(8,128)(2,1)} %bitcast.11), calls=%async_computation | async-start | bytes 1310720 | tf_op jit(solution)/shard_map/all_to_all | solution.py:160
  25.9 0.8 convert_bitcast_fusion
  26.7 12.1 %all-to-all-done = bf16[4,80,1024]{2,1,0:T(8,128)(2,1)S(1)} async-done(((bf16[4,80,1024]{2,1,0:T(8,128)(2,1)}), bf16[4,80,1024]{2,1,0:T(8,128)(2,1)S(1)}, u32[]{:S(2)}, u32[]{:S(2)}) %all-to-all-start) | async-done | bytes 655392 | tf_op jit(solution)/shard_map/all_to_all | solution.py:160
  38.8 0.1 convert_reduce_fusion
  38.9 0.1 multiply_convert_fusion
  39.0 0.9 broadcast_in_dim.10
  39.9 5.0 %all-to-all-start.1 = ((bf16[4,80,1024]{2,1,0:T(8,128)(2,1)}), bf16[4,80,1024]{2,1,0:T(8,128)(2,1)S(1)}, u32[]{:S(2)}, u32[]{:S(2)}) async-start(bf16[4,80,1024]{2,1,0:T(8,128)(2,1)} %broadcast_in_dim.10), calls=%async_computation.1 | async-start | bytes 1310720 | tf_op jit(solution)/shard_map/all_to_all | solution.py:32
  45.0 0.1 and_select_fusion
  45.0 0.1 pad_add_fusion.place
  45.1 0.7 dynamic-slice_convert_fusion.mask
  45.8 12.8 %all-to-all-done.1.lower = bf16[4,80,1024]{2,1,0:T(8,128)(2,1)S(1)} async-done(((bf16[4,80,1024]{2,1,0:T(8,128)(2,1)}), bf16[4,80,1024]{2,1,0:T(8,128)(2,1)S(1)}, u32[]{:S(2)}, u32[]{:S(2)}) %all-to-all-start.1) | async-done | bytes 655392 | tf_op jit(solution)/shard_map/all_to_all | solution.py:32
  58.7 17.0 %all-gather.2.cloned.1.call-done.refs_0_.refs_1_ = bf16[2560,1024]{1,0:T(8,128)(2,1)} async-done(((bf16[160,1024]{1,0:T(8,128)(2,1)}), bf16[2560,1024]{1,0:T(8,128)(2,1)}) %all-gather.2.cloned.1.call-update) | async-done | bytes 5242896 | tf_op jit(solution)/shard_map/all_gather | solution.py:159
  75.7 4.3 %shard_map.66 = (bf16[80,1280]{1,0:T(8,128)(2,1)S(1)}, bf16[80,1280]{1,0:T(8,128)(2,1)S(1)}, bf16[80,1280]{1,0:T(8,128)(2,1)S(1)}, bf16[80,1280]{1,0:T(8,128)(2,1)S(1)}, bf16[80,2560]{1,0:T(8,128)(2,1)S(1)}) custom-call(s32[5]{0:T(128)S(1)} %pad_add_fusion.place, bf16[1,2560]{1,0:T(2,128)(2,1)S(1)} %dynamic-slice_convert_fusion.mask, ...), custom_call_target="tpu_custom_call" | custom-call | tf_op jit(solution)/shard_map/pallas_call | solution.py:121
  80.0 4.3 %collective-permute-start.1 = (bf16[80,1280]{1,0:T(8,128)(2,1)S(1)}, bf16[80,1280]{1,0:T(8,128)(2,1)S(1)}, u32[]{:S(2)}, u32[]{:S(2)}) collective-permute-start(bf16[80,1280]{1,0:T(8,128)(2,1)S(1)} %get-tuple-element.19), channel_id=1, source_target_pairs={{0,128},{1,385},{128,256},{129,1},{256,384},{257,129},{384,0},{385... | collective-permute-start | bytes 614408 | tf_op jit(solution)/shard_map/ppermute | solution.py:176
  84.3 2.3 %collective-permute-start.3 = (bf16[80,1280]{1,0:T(8,128)(2,1)S(1)}, bf16[80,1280]{1,0:T(8,128)(2,1)S(1)}, u32[]{:S(2)}, u32[]{:S(2)}) collective-permute-start(bf16[80,1280]{1,0:T(8,128)(2,1)S(1)} %get-tuple-element.23), channel_id=1, source_target_pairs={{0,128},{1,385},{128,256},{129,1},{256,384},{257,129},{384,0},{385... | collective-permute-start | bytes 614408 | tf_op jit(solution)/shard_map/ppermute | solution.py:176
  86.6 3.0 %collective-permute-start.2 = (bf16[80,2560]{1,0:T(8,128)(2,1)S(1)}, bf16[80,2560]{1,0:T(8,128)(2,1)S(1)}, u32[]{:S(2)}, u32[]{:S(2)}) collective-permute-start(bf16[80,2560]{1,0:T(8,128)(2,1)S(1)} %get-tuple-element.21), channel_id=1, source_target_pairs={{0,384},{1,129},{128,0},{129,257},{256,128},{257,385},{384,256},{3... | collective-permute-start | bytes 1228808 | tf_op jit(solution)/shard_map/ppermute | solution.py:177
  89.6 0.0 collective-permute-done.1
  89.6 0.1 add_convert_fusion.1
  89.7 3.5 %collective-permute-start.5 = (bf16[80,1280]{1,0:T(8,128)(2,1)S(1)}, bf16[80,1280]{1,0:T(8,128)(2,1)S(1)}, u32[]{:S(2)}, u32[]{:S(2)}) collective-permute-start(bf16[80,1280]{1,0:T(8,128)(2,1)S(1)} %add_convert_fusion.1), channel_id=1, source_target_pairs={{0,128},{1,385},{128,256},{129,1},{256,384},{257,129},{384,0},{385... | collective-permute-start | bytes 614408 | tf_op jit(solution)/shard_map/ppermute | solution.py:184
  93.2 0.0 collective-permute-done.3
  93.2 0.1 add_convert_fusion
  93.2 0.0 copy-start.2
  93.3 2.1 %collective-permute-start.4 = (bf16[80,1280]{1,0:T(8,128)(2,1)S(1)}, bf16[80,1280]{1,0:T(8,128)(2,1)S(1)}, u32[]{:S(2)}, u32[]{:S(2)}) collective-permute-start(bf16[80,1280]{1,0:T(8,128)(2,1)S(1)} %add_convert_fusion), channel_id=1, source_target_pairs={{0,128},{1,385},{128,256},{129,1},{256,384},{257,129},{384,0},{385... | collective-permute-start | bytes 614408 | tf_op jit(solution)/shard_map/ppermute | solution.py:184
  95.3 3.9 %shard_map.67 = bf16[80,2560]{1,0:T(8,128)(2,1)S(1)} custom-call(s32[5]{0:T(128)S(1)} %pad_add_fusion.place, bf16[1,2560]{1,0:T(2,128)(2,1)S(1)} %dynamic-slice_convert_fusion.mask, bf16[4,80,1024]{2,1,0:T(8,128)(2,1)S(1)} %all-to-all-done.1.lower, bf16[2560,1024]{1,0:T(8,128)(2,1)} %all-gather.2.cloned.1.call-done.refs_0_.refs_1_, ...), custom_call_target="tpu_custom_call" | custom-call | tf_op jit(solution)/shard_map/pallas_call | solution.py:121
  99.3 0.0 collective-permute-done.2
  99.3 0.0 copy-done.2
  99.3 0.1 add_subtract_fusion
  99.4 0.0 collective-permute-done.5
  99.4 1.2 %collective-permute-done.4 = bf16[80,1280]{1,0:T(8,128)(2,1)S(1)} collective-permute-done((bf16[80,1280]{1,0:T(8,128)(2,1)S(1)}, bf16[80,1280]{1,0:T(8,128)(2,1)S(1)}, u32[]{:S(2)}, u32[]{:S(2)}) %collective-permute-start.4) | collective-permute-done | bytes 204832 | tf_op jit(solution)/shard_map/ppermute | solution.py:184
  100.6 0.1 fusion.11
  100.7 0.8 pad_maximum_fusion
Async XLA Ops:
  6.5 10.1 %copy-start = (bf16[1,1024,1024]{2,1,0:T(8,128)(2,1)S(1)}, bf16[1,1024,1024]{2,1,0:T(8,128)(2,1)}, u32[]{:S(2)}) copy-start(bf16[1,1024,1024]{2,1,0:T(8,128)(2,1)} %param.9) | copy-start | bytes 6291460
  6.5 69.2 %all-gather.2.cloned.1.call-start = ((), (), s32[]{:S(2)}) async-start(), calls=%async_computation.2 | async-start | bytes 5570560 | tf_op jit(solution)/shard_map/all_gather | solution.py:159
  6.5 15.1 %collective-permute-start = (bf16[80,1024]{1,0:T(8,128)(2,1)}, bf16[80,1024]{1,0:T(8,128)(2,1)S(1)}, u32[]{:S(2)}, u32[]{:S(2)}) collective-permute-start(bf16[80,1024]{1,0:T(8,128)(2,1)} %bitcast.25), channel_id=1, source_target_pairs={{0,2},{2,0},{1,3},{3,1},{4,6},{6,4},{5,7},{7,5},{8,10},{10,8},{9,1... | collective-permute-start | bytes 491528 | tf_op jit(solution)/shard_map/ppermute | solution.py:152
  14.9 0.9 copy-start.1
  22.4 16.4 %all-to-all-start = ((bf16[4,80,1024]{2,1,0:T(8,128)(2,1)}), bf16[4,80,1024]{2,1,0:T(8,128)(2,1)S(1)}, u32[]{:S(2)}, u32[]{:S(2)}) async-start(bf16[4,80,1024]{2,1,0:T(8,128)(2,1)} %bitcast.11), calls=%async_computation | async-start | bytes 1310720 | tf_op jit(solution)/shard_map/all_to_all | solution.py:160
  39.9 18.7 %all-to-all-start.1 = ((bf16[4,80,1024]{2,1,0:T(8,128)(2,1)}), bf16[4,80,1024]{2,1,0:T(8,128)(2,1)S(1)}, u32[]{:S(2)}, u32[]{:S(2)}) async-start(bf16[4,80,1024]{2,1,0:T(8,128)(2,1)} %broadcast_in_dim.10), calls=%async_computation.1 | async-start | bytes 1310720 | tf_op jit(solution)/shard_map/all_to_all | solution.py:32
  80.0 9.6 %collective-permute-start.1 = (bf16[80,1280]{1,0:T(8,128)(2,1)S(1)}, bf16[80,1280]{1,0:T(8,128)(2,1)S(1)}, u32[]{:S(2)}, u32[]{:S(2)}) collective-permute-start(bf16[80,1280]{1,0:T(8,128)(2,1)S(1)} %get-tuple-element.19), channel_id=1, source_target_pairs={{0,128},{1,385},{128,256},{129,1},{256,384},{257,129},{384,0},{385... | collective-permute-start | bytes 614408 | tf_op jit(solution)/shard_map/ppermute | solution.py:176
  84.3 8.9 %collective-permute-start.3 = (bf16[80,1280]{1,0:T(8,128)(2,1)S(1)}, bf16[80,1280]{1,0:T(8,128)(2,1)S(1)}, u32[]{:S(2)}, u32[]{:S(2)}) collective-permute-start(bf16[80,1280]{1,0:T(8,128)(2,1)S(1)} %get-tuple-element.23), channel_id=1, source_target_pairs={{0,128},{1,385},{128,256},{129,1},{256,384},{257,129},{384,0},{385... | collective-permute-start | bytes 614408 | tf_op jit(solution)/shard_map/ppermute | solution.py:176
  86.6 12.7 %collective-permute-start.2 = (bf16[80,2560]{1,0:T(8,128)(2,1)S(1)}, bf16[80,2560]{1,0:T(8,128)(2,1)S(1)}, u32[]{:S(2)}, u32[]{:S(2)}) collective-permute-start(bf16[80,2560]{1,0:T(8,128)(2,1)S(1)} %get-tuple-element.21), channel_id=1, source_target_pairs={{0,384},{1,129},{128,0},{129,257},{256,128},{257,385},{384,256},{3... | collective-permute-start | bytes 1228808 | tf_op jit(solution)/shard_map/ppermute | solution.py:177
  89.7 9.7 %collective-permute-start.5 = (bf16[80,1280]{1,0:T(8,128)(2,1)S(1)}, bf16[80,1280]{1,0:T(8,128)(2,1)S(1)}, u32[]{:S(2)}, u32[]{:S(2)}) collective-permute-start(bf16[80,1280]{1,0:T(8,128)(2,1)S(1)} %add_convert_fusion.1), channel_id=1, source_target_pairs={{0,128},{1,385},{128,256},{129,1},{256,384},{257,129},{384,0},{385... | collective-permute-start | bytes 614408 | tf_op jit(solution)/shard_map/ppermute | solution.py:184
  93.2 6.0 %copy-start.2 = (bf16[80,2560]{1,0:T(8,128)(2,1)S(1)}, bf16[80,2560]{1,0:T(8,128)(2,1)}, u32[]{:S(2)}) copy-start(bf16[80,2560]{1,0:T(8,128)(2,1)} %param.11) | copy-start | bytes 1228804
  93.3 7.4 %collective-permute-start.4 = (bf16[80,1280]{1,0:T(8,128)(2,1)S(1)}, bf16[80,1280]{1,0:T(8,128)(2,1)S(1)}, u32[]{:S(2)}, u32[]{:S(2)}) collective-permute-start(bf16[80,1280]{1,0:T(8,128)(2,1)S(1)} %add_convert_fusion), channel_id=1, source_target_pairs={{0,128},{1,385},{128,256},{129,1},{256,384},{257,129},{384,0},{385... | collective-permute-start | bytes 614408 | tf_op jit(solution)/shard_map/ppermute | solution.py:184
Sparse Core Ops, SparseCore 0:
  22.5 53.1 all-gather.1
